TPU v7x, 32 devices: a whole 2x2x4 slice. The times are simulated.
32 devices in a mesh: fsdp: 16 (over z, y, x), vocab: 2 (over core).
Axes of the slice: x: 2, y: 2, z: 4, core: 2. Of those that a mesh axis runs over, the one named last changes fastest.
Arguments:
- token_ids: int32 [32, 512], P('fsdp'), may hold values from 0 to 30719
- lengths: int32 [32], replicated, may hold values from 32 to 512, as said below
- masked_pos: int32 [32, 80], replicated, may hold values from 0 to 511, as said below
- teacher: bfloat16 [2560, 30720], P('fsdp', 'vocab'), may hold values from -12 to 12
- stack_index: int32 [6144, 48], P(('fsdp', 'vocab')), may hold values from 17476 to 61166, as said below
- down_index: int32 [768, 192], P(('fsdp', 'vocab')), may hold values from 17476 to 61166, as said below
- stack_next: int32 [6144, 48], P(('fsdp', 'vocab')), may hold values from 17476 to 61166, as said below
- down_next: int32 [768, 192], P(('fsdp', 'vocab')), may hold values from 17476 to 61166, as said below
- word_table: float32 [30720, 768], P('vocab', 'fsdp')
- table_first: float32 [30720, 768], P('vocab', 'fsdp'), may hold values from -1.4305115e-06 to 1.4305115e-06
- table_second: float32 [30720, 768], P('vocab', 'fsdp'), may hold values from 8.0371547e-16 to 3.2148619e-15
- pos_table: float32 [512, 768], P(None, ('fsdp', 'vocab')), may hold values from -6 to 6
- pos_first: float32 [512, 768], P(None, ('fsdp', 'vocab')), may hold values from -1.4305115e-06 to 1.4305115e-06
- pos_second: float32 [512, 768], P(None, ('fsdp', 'vocab')), may hold values from 8.0371547e-16 to 3.2148619e-15
- proj_stack: float32 [6144, 768], P(('fsdp', 'vocab')), may hold values from -0.21875 to 0.21875
- stack_first: float32 [6144, 768], P(('fsdp', 'vocab')), may hold values from -1.4305115e-06 to 1.4305115e-06
- stack_second: float32 [6144, 768], P(('fsdp', 'vocab')), may hold values from 8.0371547e-16 to 3.2148619e-15
- ffn_down: float32 [768, 3072], P(('fsdp', 'vocab')), may hold values from -0.109375 to 0.109375
- down_first: float32 [768, 3072], P(('fsdp', 'vocab')), may hold values from -1.4305115e-06 to 1.4305115e-06
- down_second: float32 [768, 3072], P(('fsdp', 'vocab')), may hold values from 8.0371547e-16 to 3.2148619e-15
- vectors: float32 [10752], P(('fsdp', 'vocab'))
- vectors_first: float32 [10752], P(('fsdp', 'vocab')), may hold values from -7.6293945e-06 to 7.6293945e-06
- vectors_second: float32 [10752], P(('fsdp', 'vocab')), may hold values from 2.0092887e-14 to 8.037155e-14
- head_bias: float32 [30720], P('vocab'), may hold values from -6 to 6
- bias_first: float32 [30720], P('vocab'), may hold values from -7.6293945e-06 to 7.6293945e-06
- bias_second_moment: float32 [30720], P('vocab'), may hold values from 2.0092887e-14 to 8.037155e-14
Outputs:
- table_moment: float32 [30720, 768], P('vocab', 'fsdp')
- table_square: float32 [30720, 768], P('vocab', 'fsdp')
- table_new: float32 [30720, 768], P('vocab', 'fsdp')
- pos_moment: float32 [512, 768], P(None, ('fsdp', 'vocab'))
- pos_square: float32 [512, 768], P(None, ('fsdp', 'vocab'))
- pos_new: float32 [512, 768], P(None, ('fsdp', 'vocab'))
- stack_moment: float32 [6144, 768], P(('fsdp', 'vocab'))
- stack_square: float32 [6144, 768], P(('fsdp', 'vocab'))
- updated_stack: float32 [6144, 768], P(('fsdp', 'vocab'))
- down_moment: float32 [768, 3072], P(('fsdp', 'vocab'))
- down_square: float32 [768, 3072], P(('fsdp', 'vocab'))
- down_new: float32 [768, 3072], P(('fsdp', 'vocab'))
- vectors_moment: float32 [10752], P(('fsdp', 'vocab'))
- vectors_square: float32 [10752], P(('fsdp', 'vocab'))
- vectors_new: float32 [10752], P(('fsdp', 'vocab'))
- bias_moment: float32 [30720], P('vocab')
- bias_square: float32 [30720], P('vocab')
- bias_new: float32 [30720], P('vocab')
- loss_sum: float32 [], replicated
- masked_slot_count: float32 [], replicated
- grad_norm: float32 [], replicated
- mask_changes: int32 [], replicated
Inputs may be any that keep to these rules, and one draw needn't show every extreme that they name: Sequence s has its first lengths[s] slots live; one sequence has exactly 512 and one exactly 32. `masked_pos`: within a sequence the slots are distinct; the first is below 32. `stack_index`: each word packs 8 digits; the two digits of a group are distinct, the first the smaller. `down_index`: as stack_index. `stack_next`: as stack_index. `down_next`: as stack_index.
All inputs are finite; a program needn't handle non-finite values.
Results may differ from a plain program's by a relative error of at most 0.004.
The roundings to bfloat16 on the way count: a program that leaves them out, or rounds other values in their place, can miss the bound.
Values may be sent and summed in bfloat16 or wider, within the bound.
No kernel may reach another device: no remote copies, remote signals or barrier semaphores. Data moves between devices by JAX's collectives and lax.ppermute only.
A program may use at most 320 MiB of HBM per device.

v0:
```python
import jax
import jax.numpy as jnp
from jax import lax
from jax.sharding import PartitionSpec as P

HEAD_DIM = 64
STEP = 10


NORM_EPS = 1e-05
CLIP = 0.005
PRUNE_DECAY = 0.0002
BETA_ONE = 0.9
BETA_TWO = 0.999
ADAM_EPS = 1e-08
WEIGHT_DECAY = 0.01
RATE_MATRIX = 0.1
RATE_VECTOR = 1.0
SCORE_SCALE = 0.125


def combined_all(x, axis, combine):
    everything = jax.tree.map(lambda part: lax.all_gather(part, axis), x)
    first = jax.tree.map(lambda part: part[0], everything)

    def turn(k, so_far):
        return combine(so_far, jax.tree.map(lambda part: part[k], everything))

    return lax.fori_loop(1, lax.axis_size(axis), turn, first)


def unpack(words):
    powers = 4 ** jnp.arange(8, dtype=jnp.int32)
    digits = words[..., None] // powers % 4
    return digits.reshape(words.shape[0], words.shape[1] * 8)


def keep_mask(words):
    count_rows = words.shape[0]
    groups = words.shape[1] * 4
    places = unpack(words).reshape(count_rows, groups, 2)
    spots = jnp.arange(4, dtype=jnp.int32)
    chosen = (places[:, :, 0:1] == spots) | (places[:, :, 1:2] == spots)
    return chosen.reshape(count_rows, groups * 4).astype(jnp.float32)


def select_kept(weight_matrix, words):
    count_rows, width = weight_matrix.shape
    grouped = weight_matrix.reshape(count_rows, width // 4, 4)
    places = unpack(words).reshape(count_rows, width // 4, 2)
    kept = jnp.take_along_axis(grouped, places, axis=2)
    return kept.reshape(count_rows, width // 2).astype(jnp.bfloat16)


def expand(kept, words):
    count_rows = kept.shape[0]
    groups = kept.shape[1] // 2
    pairs = kept.reshape(count_rows, groups, 2)
    places = unpack(words).reshape(count_rows, groups, 2)
    spots = jnp.arange(4, dtype=jnp.int32)
    nothing = jnp.zeros((), jnp.bfloat16)
    dense = jnp.where(places[:, :, 0:1] == spots, pairs[:, :, 0:1], nothing) + jnp.where(
        places[:, :, 1:2] == spots, pairs[:, :, 1:2], nothing
    )
    return dense.reshape(count_rows, groups * 4)


def split_vectors(vectors_all, width):
    hidden_units = vectors_all.shape[0] - 10 * width
    pieces = []
    offset = 0
    for piece_len in [width] * 9 + [hidden_units, width]:
        pieces.append(vectors_all[offset : offset + piece_len])
        offset = offset + piece_len
    return pieces


def layer_norm(input_batch, gain, shift):
    center = input_batch - jnp.mean(input_batch, axis=-1, keepdims=True)
    spread = jnp.mean(center * center, axis=-1, keepdims=True)
    return center * lax.rsqrt(spread + NORM_EPS) * gain + shift


def norm_back(input_batch, gain, shift, gradient_tree):
    unused, pull = jax.vjp(layer_norm, input_batch, gain, shift)
    return pull(gradient_tree)


def activate(input_batch):
    return jax.nn.gelu(input_batch, approximate=False)


def project(input_batch, weight_matrix):
    return jnp.einsum("ymh,ph->ymp", input_batch, weight_matrix, preferred_element_type=jnp.float32)


def project_back(gradient_tree, weight_matrix):
    return jnp.einsum(
        "faz,zh->fah", gradient_tree, weight_matrix, preferred_element_type=jnp.float32
    )


def weight_grad(gradient_tree, input_batch):
    return jnp.einsum("ebu,ebw->uw", gradient_tree, input_batch, preferred_element_type=jnp.float32)


def column_sum(gradient_tree):
    return jnp.sum(gradient_tree.astype(jnp.float32), axis=(0, 1))


def collect(proj_stack, ffn_down, stack_index, down_index, pos_table, vectors):
    pos_low = pos_table.astype(jnp.bfloat16)
    vectors_low = vectors.astype(jnp.bfloat16)
    kept_stack, kept_down, words_stack, words_down, pos_all, vectors_all = (
        lax.all_gather(select_kept(proj_stack, stack_index), ("fsdp", "vocab"), axis=0, tiled=True),
        lax.all_gather(select_kept(ffn_down, down_index), ("fsdp", "vocab"), axis=0, tiled=True),
        lax.all_gather(stack_index, ("fsdp", "vocab"), axis=0, tiled=True),
        lax.all_gather(down_index, ("fsdp", "vocab"), axis=0, tiled=True),
        lax.all_gather(pos_low, ("fsdp", "vocab"), axis=1, tiled=True),
        lax.all_gather(vectors_low, ("fsdp", "vocab"), axis=0, tiled=True),
    )
    return (expand(kept_stack, words_stack), expand(kept_down, words_down), pos_all, vectors_all)


def attend(pieces):
    query, key_rows, value_rows, live_row = pieces
    raw = (
        jnp.einsum("qhe,khe->hqk", query, key_rows, preferred_element_type=jnp.float32)
        * SCORE_SCALE
    )
    scores = jnp.where(live_row[None, None, :], raw, -1e30)
    top = jnp.max(scores, axis=-1, keepdims=True)
    total = jnp.sum(jnp.exp(scores - top), axis=-1, keepdims=True)
    lse = top + jnp.log(total)
    prob = jnp.exp(scores - lse).astype(jnp.bfloat16)
    context = jnp.einsum("hqk,khe->qhe", prob, value_rows, preferred_element_type=jnp.float32)
    return (context, lse)


def attend_back(pieces):
    query, key_rows, value_rows, grad_out, lse, live_row = pieces
    raw = (
        jnp.einsum("qhe,khe->hqk", query, key_rows, preferred_element_type=jnp.float32)
        * SCORE_SCALE
    )
    scores = jnp.where(live_row[None, None, :], raw, -1e30)
    prob = jnp.exp(scores - lse)
    grad_prob = jnp.einsum("qhe,khe->hqk", grad_out, value_rows, preferred_element_type=jnp.float32)
    grad_value = jnp.einsum(
        "hqk,qhe->khe", prob.astype(jnp.bfloat16), grad_out, preferred_element_type=jnp.float32
    )
    grad_score = (prob * (grad_prob - jnp.sum(prob * grad_prob, axis=-1, keepdims=True))).astype(
        jnp.bfloat16
    )
    grad_query = (
        jnp.einsum("hqk,khe->qhe", grad_score, key_rows, preferred_element_type=jnp.float32)
        * SCORE_SCALE
    )
    grad_key = (
        jnp.einsum("hqk,qhe->khe", grad_score, query, preferred_element_type=jnp.float32)
        * SCORE_SCALE
    )
    seq_len = query.shape[0]
    return jnp.concatenate(
        [
            grad_query.reshape(seq_len, -1),
            grad_key.reshape(seq_len, -1),
            grad_value.reshape(seq_len, -1),
        ],
        -1,
    )


def layer_forward(embedded, live, dense_stack, dense_down, parts):
    (
        gain_embed,
        shift_embed,
        gain_attn,
        shift_attn,
        gain_ffn,
        shift_ffn,
        bias_query,
        bias_value,
        bias_out,
        bias_hidden,
        bias_down,
    ) = parts
    seqs, seq_len, width = embedded.shape
    heads = width // HEAD_DIM
    normed = layer_norm(embedded, gain_embed, shift_embed)
    normed_low = normed.astype(jnp.bfloat16)
    qkv_bias = jnp.concatenate([bias_query, jnp.zeros_like(bias_query), bias_value])
    qkv_low = (project(normed_low, dense_stack[: 3 * width]) + qkv_bias).astype(jnp.bfloat16)
    split = qkv_low.reshape(seqs, seq_len, 3, heads, HEAD_DIM)
    context, lse = lax.map(attend, (split[:, :, 0], split[:, :, 1], split[:, :, 2], live))
    context_low = context.reshape(seqs, seq_len, width).astype(jnp.bfloat16)
    first_sum = normed + project(context_low, dense_stack[3 * width : 4 * width]) + bias_out
    first_out = layer_norm(first_sum, gain_attn, shift_attn)
    first_low = first_out.astype(jnp.bfloat16)
    pre_act = project(first_low, dense_stack[4 * width :]) + bias_hidden
    act_low = activate(pre_act).astype(jnp.bfloat16)
    second_sum = first_out + project(act_low, dense_down) + bias_down
    final = layer_norm(second_sum, gain_ffn, shift_ffn)
    saved = (
        embedded,
        normed_low,
        qkv_low,
        lse,
        context_low,
        first_sum,
        first_low,
        pre_act,
        act_low,
        second_sum,
    )
    return (final, saved)


def layer_backward(grad_final, saved, live, dense_stack, dense_down, parts):
    (
        gain_embed,
        shift_embed,
        gain_attn,
        shift_attn,
        gain_ffn,
        shift_ffn,
        bias_query,
        bias_value,
        bias_out,
        bias_hidden,
        bias_down,
    ) = parts
    (
        embedded,
        normed_low,
        qkv_low,
        lse,
        context_low,
        first_sum,
        first_low,
        pre_act,
        act_low,
        second_sum,
    ) = saved
    seqs, seq_len, width = embedded.shape
    heads = width // HEAD_DIM
    grad_second, grad_gain_ffn, grad_shift_ffn = norm_back(
        second_sum, gain_ffn, shift_ffn, grad_final
    )
    grad_down_low = grad_second.astype(jnp.bfloat16)
    down_grad = weight_grad(grad_down_low, act_low)
    grad_act = project_back(grad_down_low, dense_down)
    unused, act_pull = jax.vjp(activate, pre_act)
    grad_pre_low = act_pull(grad_act)[0].astype(jnp.bfloat16)
    hidden_grad = weight_grad(grad_pre_low, first_low)
    grad_first = grad_second + project_back(grad_pre_low, dense_stack[4 * width :])
    grad_first_sum, grad_gain_attn, grad_shift_attn = norm_back(
        first_sum, gain_attn, shift_attn, grad_first
    )
    grad_out_low = grad_first_sum.astype(jnp.bfloat16)
    out_grad = weight_grad(grad_out_low, context_low)
    grad_context_low = project_back(grad_out_low, dense_stack[3 * width : 4 * width]).astype(
        jnp.bfloat16
    )
    split = qkv_low.reshape(seqs, seq_len, 3, heads, HEAD_DIM)
    grad_qkv = lax.map(
        attend_back,
        (
            split[:, :, 0],
            split[:, :, 1],
            split[:, :, 2],
            grad_context_low.reshape(seqs, seq_len, heads, HEAD_DIM),
            lse,
            live,
        ),
    )
    grad_qkv_low = grad_qkv.astype(jnp.bfloat16)
    qkv_grad = weight_grad(grad_qkv_low, normed_low)
    grad_normed = grad_first_sum + project_back(grad_qkv_low, dense_stack[: 3 * width])
    grad_embed, grad_gain_embed, grad_shift_embed = norm_back(
        embedded, gain_embed, shift_embed, grad_normed
    )
    stack_grad = jnp.concatenate([qkv_grad, out_grad, hidden_grad], 0)
    vectors_grad = jnp.concatenate(
        [
            grad_gain_embed,
            grad_shift_embed,
            grad_gain_attn,
            grad_shift_attn,
            grad_gain_ffn,
            grad_shift_ffn,
            column_sum(grad_qkv_low[:, :, :width]),
            column_sum(grad_qkv_low[:, :, 2 * width :]),
            column_sum(grad_out_low),
            column_sum(grad_pre_low),
            column_sum(grad_down_low),
        ]
    )
    return (grad_embed, stack_grad, down_grad, vectors_grad)


def combine_stats(first, second):
    s_top_one, s_total_one, t_top_one, t_total_one, cross_one = first
    s_top_two, s_total_two, t_top_two, t_total_two, cross_two = second
    s_top = jnp.maximum(s_top_one, s_top_two)
    t_top = jnp.maximum(t_top_one, t_top_two)
    s_total = s_total_one * jnp.exp(s_top_one - s_top) + s_total_two * jnp.exp(s_top_two - s_top)
    t_scale_one = jnp.exp(t_top_one - t_top)
    t_scale_two = jnp.exp(t_top_two - t_top)
    t_total = t_total_one * t_scale_one + t_total_two * t_scale_two
    cross = cross_one * t_scale_one + cross_two * t_scale_two
    return (s_top, s_total, t_top, t_total, cross)


def adam(weight_matrix, grad, first, second, rate):
    first = BETA_ONE * first + (1.0 - BETA_ONE) * grad
    second = BETA_TWO * second + (1.0 - BETA_TWO) * grad * grad
    first_hat = first / (1.0 - BETA_ONE**STEP)
    second_hat = second / (1.0 - BETA_TWO**STEP)
    new = weight_matrix - rate * (
        first_hat / (jnp.sqrt(second_hat) + ADAM_EPS) + WEIGHT_DECAY * weight_matrix
    )
    return (first, second, new)


def local(
    token_ids,
    lengths,
    masked_pos,
    teacher,
    stack_index,
    down_index,
    stack_next,
    down_next,
    word_table,
    table_first,
    table_second,
    pos_table,
    pos_first,
    pos_second,
    proj_stack,
    stack_first,
    stack_second,
    ffn_down,
    down_first,
    down_second,
    vectors,
    vectors_first,
    vectors_second,
    head_bias,
    bias_first,
    bias_second_moment,
):
    width = proj_stack.shape[1]
    pair_seqs, seq_len = token_ids.shape
    own_seqs = pair_seqs // lax.axis_size("vocab")
    core_index = lax.axis_index("vocab")
    column_index = lax.axis_index("fsdp")
    vocab_dev = word_table.shape[0]
    own_rows = own_seqs * seq_len
    mask_slots = masked_pos.shape[1]
    stack_mask = keep_mask(stack_index)
    down_mask = keep_mask(down_index)
    dense_stack, dense_down, pos_all, vectors_all = collect(
        proj_stack, ffn_down, stack_index, down_index, pos_table, vectors
    )
    parts = split_vectors(vectors_all.astype(jnp.float32), width)
    table_half = lax.all_gather(word_table.astype(jnp.bfloat16), "fsdp", axis=1, tiled=True)
    local_ids = token_ids.reshape(-1) - core_index * vocab_dev
    inside = (local_ids >= 0) & (local_ids < vocab_dev)
    clipped_ids = jnp.clip(local_ids, 0, vocab_dev - 1)
    looked = jnp.where(
        inside[:, None], jnp.take(table_half, clipped_ids, axis=0).astype(jnp.float32), 0.0
    )
    own_embed = lax.psum_scatter(
        looked.astype(jnp.bfloat16), "vocab", scatter_dimension=0, tiled=True
    ).astype(jnp.float32)
    embedded = own_embed.reshape(own_seqs, seq_len, width) + pos_all.astype(jnp.float32)[None]
    pair_start = column_index * pair_seqs
    seq_start = pair_start + core_index * own_seqs
    own_lengths = lax.dynamic_slice_in_dim(lengths, seq_start, own_seqs)
    live = jnp.arange(seq_len, dtype=jnp.int32)[None, :] < own_lengths[:, None]
    final, saved = layer_forward(embedded, live, dense_stack, dense_down, parts)
    own_pos = lax.dynamic_slice_in_dim(masked_pos, seq_start, own_seqs, 0)
    flat_rows = (jnp.arange(own_seqs, dtype=jnp.int32)[:, None] * seq_len + own_pos).reshape(-1)
    picked = jnp.take(final.reshape(own_rows, width), flat_rows, axis=0).astype(jnp.bfloat16)
    pair_rows = lax.all_gather(picked, "vocab", axis=0, tiled=True)
    output_logits = (
        jnp.einsum("pd,vd->pv", pair_rows, table_half, preferred_element_type=jnp.float32)
        + head_bias
    )
    teach = teacher.astype(jnp.float32)
    student_top = jnp.max(output_logits, axis=-1)
    student_total = jnp.sum(jnp.exp(output_logits - student_top[:, None]), axis=-1)
    teacher_top = jnp.max(teach, axis=-1)
    weighted = jnp.exp(teach - teacher_top[:, None])
    teacher_total = jnp.sum(weighted, axis=-1)
    cross = jnp.sum(weighted * (teach - output_logits), axis=-1)
    student_top, student_total, teacher_top, teacher_total, cross = combined_all(
        (student_top, student_total, teacher_top, teacher_total, cross), "vocab", combine_stats
    )
    student_lse = student_top + jnp.log(student_total)
    teacher_lse = teacher_top + jnp.log(teacher_total)
    divergence = cross / teacher_total - teacher_lse + student_lse
    pair_pos = lax.dynamic_slice_in_dim(masked_pos, pair_start, pair_seqs, 0)
    pair_lengths = lax.dynamic_slice_in_dim(lengths, pair_start, pair_seqs)
    pair_valid = (pair_pos < pair_lengths[:, None]).astype(jnp.float32).reshape(-1)
    count = jnp.sum((masked_pos < lengths[:, None]).astype(jnp.float32))
    own_slots = own_seqs * mask_slots
    own_loss = jnp.sum(
        lax.dynamic_slice_in_dim(divergence * pair_valid, core_index * own_slots, own_slots)
    )
    scale_rows = (pair_valid / count)[:, None]
    grad_logits = (
        (jnp.exp(output_logits - student_lse[:, None]) - jnp.exp(teach - teacher_lse[:, None]))
        * scale_rows
    ).astype(jnp.bfloat16)
    bias_local = jnp.sum(grad_logits.astype(jnp.float32), axis=0)
    table_grad = jnp.einsum("pv,pd->vd", grad_logits, pair_rows, preferred_element_type=jnp.float32)
    rows_grad = jnp.einsum("pv,vd->pd", grad_logits, table_half, preferred_element_type=jnp.float32)
    own_rows_grad = lax.psum_scatter(rows_grad, "vocab", scatter_dimension=0, tiled=True)
    grad_final = (
        jnp.zeros((own_rows, width), jnp.float32)
        .at[flat_rows]
        .add(own_rows_grad)
        .reshape(own_seqs, seq_len, width)
    )
    back_stack, back_down, pos_again, vectors_again = collect(
        proj_stack, ffn_down, stack_index, down_index, pos_table, vectors
    )
    grad_embed, stack_grad, down_grad, vectors_grad = layer_backward(
        grad_final, saved, live, back_stack, back_down, parts
    )
    pos_grad = jnp.sum(grad_embed, axis=0)
    pair_embed_grad = lax.all_gather(
        grad_embed.reshape(own_rows, width).astype(jnp.bfloat16), "vocab", axis=0, tiled=True
    ).astype(jnp.float32)
    table_grad = table_grad.at[clipped_ids].add(jnp.where(inside[:, None], pair_embed_grad, 0.0))
    stack_total, down_total, pos_total, vectors_total = (
        lax.psum_scatter(stack_grad, ("fsdp", "vocab"), scatter_dimension=0, tiled=True),
        lax.psum_scatter(down_grad, ("fsdp", "vocab"), scatter_dimension=0, tiled=True),
        lax.psum_scatter(pos_grad, ("fsdp", "vocab"), scatter_dimension=1, tiled=True),
        lax.psum_scatter(vectors_grad, ("fsdp", "vocab"), scatter_dimension=0, tiled=True),
    )
    table_total = lax.psum_scatter(table_grad, "fsdp", scatter_dimension=1, tiled=True)
    bias_total = lax.psum(bias_local, "fsdp")
    stack_total = stack_total + PRUNE_DECAY * (1.0 - stack_mask) * proj_stack
    down_total = down_total + PRUNE_DECAY * (1.0 - down_mask) * ffn_down
    changes = jnp.sum((stack_mask != keep_mask(stack_next)).astype(jnp.float32)) + jnp.sum(
        (down_mask != keep_mask(down_next)).astype(jnp.float32)
    )
    squares = (
        jnp.sum(stack_total * stack_total)
        + jnp.sum(down_total * down_total)
        + jnp.sum(pos_total * pos_total)
        + jnp.sum(vectors_total * vectors_total)
        + jnp.sum(table_total * table_total)
        + jnp.sum(bias_total * bias_total) / lax.axis_size("fsdp")
    )
    total_squares, loss_sum, change_total = lax.psum(
        (squares, own_loss, changes), ("fsdp", "vocab")
    )
    grad_norm = jnp.sqrt(total_squares)
    factor = jnp.minimum(1.0, CLIP / (grad_norm + 1e-06))
    table_out = adam(word_table, table_total * factor, table_first, table_second, RATE_MATRIX)
    pos_out = adam(pos_table, pos_total * factor, pos_first, pos_second, RATE_MATRIX)
    stack_out = adam(proj_stack, stack_total * factor, stack_first, stack_second, RATE_MATRIX)
    down_out = adam(ffn_down, down_total * factor, down_first, down_second, RATE_MATRIX)
    vectors_out = adam(vectors, vectors_total * factor, vectors_first, vectors_second, RATE_VECTOR)
    bias_out = adam(head_bias, bias_total * factor, bias_first, bias_second_moment, RATE_VECTOR)
    return (
        table_out[0],
        table_out[1],
        table_out[2],
        pos_out[0],
        pos_out[1],
        pos_out[2],
        stack_out[0],
        stack_out[1],
        stack_out[2],
        down_out[0],
        down_out[1],
        down_out[2],
        vectors_out[0],
        vectors_out[1],
        vectors_out[2],
        bias_out[0],
        bias_out[1],
        bias_out[2],
        loss_sum,
        count,
        grad_norm,
        change_total.astype(jnp.int32),
    )


def solution(mesh):
    in_specs = (
        P("fsdp", None),
        P(),
        P(),
        P("fsdp", "vocab"),
        P(("fsdp", "vocab"), None),
        P(("fsdp", "vocab"), None),
        P(("fsdp", "vocab"), None),
        P(("fsdp", "vocab"), None),
        P("vocab", "fsdp"),
        P("vocab", "fsdp"),
        P("vocab", "fsdp"),
        P(None, ("fsdp", "vocab")),
        P(None, ("fsdp", "vocab")),
        P(None, ("fsdp", "vocab")),
        P(("fsdp", "vocab"), None),
        P(("fsdp", "vocab"), None),
        P(("fsdp", "vocab"), None),
        P(("fsdp", "vocab"), None),
        P(("fsdp", "vocab"), None),
        P(("fsdp", "vocab"), None),
        P(("fsdp", "vocab")),
        P(("fsdp", "vocab")),
        P(("fsdp", "vocab")),
        P("vocab"),
        P("vocab"),
        P("vocab"),
    )
    out_specs = (
        P("vocab", "fsdp"),
        P("vocab", "fsdp"),
        P("vocab", "fsdp"),
        P(None, ("fsdp", "vocab")),
        P(None, ("fsdp", "vocab")),
        P(None, ("fsdp", "vocab")),
        P(("fsdp", "vocab"), None),
        P(("fsdp", "vocab"), None),
        P(("fsdp", "vocab"), None),
        P(("fsdp", "vocab"), None),
        P(("fsdp", "vocab"), None),
        P(("fsdp", "vocab"), None),
        P(("fsdp", "vocab")),
        P(("fsdp", "vocab")),
        P(("fsdp", "vocab")),
        P("vocab"),
        P("vocab"),
        P("vocab"),
        P(),
        P(),
        P(),
        P(),
    )
    return jax.shard_map(local, mesh=mesh, in_specs=in_specs, out_specs=out_specs, check_vma=False)
```

profile of v0, /device:TPU:0, one launch (start us, length us, event | category | flops | bytes accessed | tf_op | source)
XLA Modules:
  0.0 3110.4 jit_solution(14105110119474564720)
XLA Ops:
  12.7 16.7 add_select_fusion.6
  43.3 339.3 %gather_fusion.3 = bf16[36864]{0:T(1024)(128)(2,1)S(1)} fusion(bf16[24,768,4]{0,2,1:T(4,128)(2,1)S(1)} %bitcast.228, s32[36864]{0:T(1024)S(1)} %reshape.1007), kind=kCustom, calls=%fused_computation.1.clone | custom fusion | bytes 589824 | tf_op jit(solution)/shard_map/jit(take_along_axis)/gather | solution.py:51
  382.6 11.4 reshape.1010
  420.2 14.1 reshape.1002
  434.3 701.1 %gather_fusion.2 = bf16[73728]{0:T(1024)(128)(2,1)S(1)} fusion(bf16[192,192,4]{0,2,1:T(4,128)(2,1)S(1)} %reshape.878, s32[73728]{0:T(1024)S(1)} %reshape.1002), kind=kCustom, calls=%fused_computation.clone | custom fusion | bytes 1179648 | tf_op jit(solution)/shard_map/jit(take_along_axis)/gather | solution.py:51
  1135.5 21.4 reshape.1005
  1177.5 42.5 %all-reduce = bf16[10752]{0:T(1024)(128)(2,1)S(1)} all-reduce(bf16[10752]{0:T(1024)(128)(2,1)S(1)} %dynamic-update-slice), channel_id=1, replica_groups=mesh['fsdp'=16,'vocab'=2] {'fsdp','vocab'}, use_global_device_ids=true, to_apply=%add | all-reduce | flops 10752 | bytes 43008
  1220.9 44.6 %all_gather.60 = bf16[512,768]{0,1:T(8,128)(2,1)S(1)} all-gather(bf16[512,24]{0,1:T(8,128)(2,1)S(1)} %convert_element_type.180), channel_id=1, replica_groups=mesh['fsdp'=16,'vocab'=2] {'fsdp','vocab'}, dimensions={1}, use_global_device_ids=true | all-gather | bytes 811008 | tf_op jit(solution)/shard_map/all_gather | solution.py:119
  1266.7 42.3 %all_gather.64 = s32[768,192]{1,0:T(8,128)S(1)} all-gather(s32[24,192]{1,0:T(8,128)S(1)} %copy-done.47), channel_id=1, replica_groups=mesh['fsdp'=16,'vocab'=2] {'fsdp','vocab'}, dimensions={0}, use_global_device_ids=true | all-gather | bytes 608256 | tf_op jit(solution)/shard_map/all_gather | solution.py:118
  1309.6 48.9 %add_select_fusion.3 = s32[768,192,8]{0,2,1:T(8,128)} fusion(s32[8]{0:T(128)S(1)} %copy-done.78, s32[768,192]{0,1:T(8,128)S(1)} %copy.235, s32[768,192]{0,1:T(8,128)S(1)} %copy.234, s32[8]{0:T(128)S(1)} %copy-done.81), kind=kLoop, calls=%fused_computation.44 | loop fusion | flops 21233664 | bytes 5898304 | tf_op jit(solution)/shard_map/jit(remainder)/select_n | solution.py:34
  1383.9 12.0 eq.310
  1401.1 12.0 eq.317
  1424.9 96.8 %add_select_fusion.1 = s32[6144,48,8]{0,2,1:T(8,128)} fusion(s32[8]{0:T(128)S(1)} %copy-done.78, s32[6144,48]{0,1:T(8,128)S(1)} %rem.236, s32[6144,48]{0,1:T(8,128)S(1)} %sign_bitcast_fusion, s32[8]{0:T(128)S(1)} %copy-done.81), kind=kLoop, calls=%fused_computation.16 | loop fusion | flops 42467328 | bytes 11796544 | tf_op jit(solution)/shard_map/jit(remainder)/select_n | solution.py:34
  1521.7 11.4 reshape_reshape.24
  1533.1 11.7 fusion.96
  1589.4 12.9 fusion.22
  1617.0 30.7 copy.220
  1647.6 15.2 gather_fusion
  1678.5 12.3 fusion.12
  1745.8 18.6 multiply_convert_fusion.1
  1773.8 15.4 fusion.107
  1802.7 10.7 convert_reduce_fusion
  1813.4 13.9 fusion.109
  1868.1 10.5 multiply_reduce_fusion
  1922.5 20.1 fusion.108
  1942.6 39.0 %scatter_custom_fusion.1 = f32[15360,768]{1,0:T(8,128)} fusion(f32[15360,768]{1,0:T(8,128)} %fusion.108, s32[1024]{0:T(1024)} %bitcast.285, bf16[1024,768]{1,0:T(8,128)(2,1)} %all-gather.18.cloned.1.call-done, pred[1024]{0:T(1024)(128)(4,1)S(1)} %copy-done.75), kind=kCustom, calls=%fused_computation.302 | custom fusion | flops 2359296 | bytes 48759808 | tf_op jit(solution)/shard_map/scatter-add | solution.py:438
  1981.6 46.0 %copy.275 = f32[15360,768]{0,1:T(8,128)} copy(f32[15360,768]{1,0:T(8,128)} %scatter_custom_fusion.1) | data formatting | bytes 94371840
  2046.4 79.1 %psum.28 = f32[15360]{0:T(1024)S(1)} all-reduce(f32[15360]{0:T(1024)S(1)} %copy-done.46), channel_id=1, replica_groups=mesh['fsdp'=16,'vocab'=2] {'fsdp'}, use_global_device_ids=true, to_apply=%region_46.53 | all-reduce | flops 15360 | bytes 122880 | tf_op jit(solution)/shard_map/psum | solution.py:446
  2141.3 37.4 %all-reduce.6 = f32[10752]{0:T(1024)S(1)} all-reduce(f32[10752]{0:T(1024)} %constant_dynamic-update-slice_fusion), channel_id=13, replica_groups=mesh['fsdp'=16,'vocab'=2] {'fsdp','vocab'}, use_global_device_ids=true, to_apply=%region_42.49.clone | all-reduce | flops 10752 | bytes 86016
  2183.7 183.8 %reduce-scatter.15.cloned.1.call-done = f32[192,768]{1,0:T(8,128)} async-done(((f32[6144,768]{1,0:T(8,128)}), f32[192,768]{1,0:T(8,128)}) %reduce-scatter.15.cloned.1.call-update) | async-done | bytes 589840 | tf_op jit(solution)/shard_map/reduce_scatter | solution.py:440
  2372.7 660.3 %reduce-scatter.19.cloned.1.call-done = f32[48,15360]{1,0:T(8,128)} async-done(((f32[768,15360]{1,0:T(8,128)}), f32[48,15360]{1,0:T(8,128)}) %reduce-scatter.19.cloned.1.call-update) | async-done | bytes 2949136
  3045.1 39.9 %all-reduce.7 = (f32[]{:T(128)}, f32[]{:T(128)}, f32[]{:T(128)}) all-reduce(f32[]{:T(128)S(6)} %add.507, f32[]{:T(128)} %dynamic-slice_reduce_fusion, f32[]{:T(128)S(6)} %add.544), channel_id=1, replica_groups=mesh['fsdp'=16,'vocab'=2] {'fsdp','vocab'}, use_global_device_ids=true, to_apply=%region_48.55 | all-reduce | flops 3 | bytes 24 | tf_op jit(solution)/shard_map/psum | solution.py:460
  (472 shorter events, 412.5 us)
Async XLA Ops:
  7.2 1411.7 %all-gather.20.cloned.1.call-start = ((), (), s32[]{:S(2)}) async-start(), calls=%async_computation.14 | async-start | bytes 1622016 | tf_op jit(solution)/shard_map/all_gather | solution.py:117
  7.9 1544.7 %all-gather.16.cloned.1.call-start = ((), (), s32[]{:S(2)}) async-start(), calls=%async_computation.9 | async-start | bytes 2433024 | tf_op jit(solution)/shard_map/all_gather | solution.py:116
  400.1 1202.2 %all-gather.14.cloned.1.call-start = ((), (), s32[]{:S(2)}) async-start(), calls=%async_computation.8 | async-start | bytes 4866048 | tf_op jit(solution)/shard_map/all_gather | solution.py:115
  1168.0 52.6 %copy-start.50 = (f32[512,24]{0,1:T(8,128)S(1)}, f32[512,24]{0,1:T(8,128)}, u32[]{:S(2)}) copy-start(f32[512,24]{0,1:T(8,128)} %param.49) | copy-start | bytes 147460
  1168.0 449.0 %all-gather.12.cloned.1.call-start = ((), (), s32[]{:S(2)}) async-start(), calls=%async_computation.6 | async-start | bytes 25067520 | tf_op jit(solution)/shard_map/all_gather | solution.py:368
  1169.3 97.3 %copy-start.47 = (s32[24,192]{1,0:T(8,128)S(1)}, s32[24,192]{1,0:T(8,128)}, u32[]{:S(2)}) copy-start(s32[24,192]{1,0:T(8,128)} %param.43) | copy-start | bytes 55300
  1169.3 540.6 %reduce-scatter.11.cloned.1.call-start = ((), (), s32[]{:S(2)}) async-start(), calls=%async_computation.7 | async-start | bytes 2359296 | tf_op jit(solution)/shard_map/reduce_scatter | solution.py:375
  1176.5 133.0 %copy-start.78 = (s32[8]{0:T(128)S(1)}, s32[8]{0:T(128)}, u32[]{:S(2)}) copy-start(s32[8]{0:T(128)} %copy-done.76) | copy-start | bytes 100
  1176.5 133.0 %copy-start.81 = (s32[8]{0:T(128)S(1)}, s32[8]{0:T(128)}, u32[]{:S(2)}) copy-start(s32[8]{0:T(128)} %copy-done.79) | copy-start | bytes 100
  1177.2 485.7 %copy-start.74 = (pred[1024]{0:T(1024)(128)(4,1)}, pred[1024]{0:T(1024)(128)(4,1)S(1)}, u32[]{:S(2)}) copy-start(pred[1024]{0:T(1024)(128)(4,1)S(1)} %and.226) | copy-start | bytes 3076
  1220.8 368.5 %copy-start.52 = (s32[3072]{0:T(1024)}, s32[3072]{0:T(1024)S(1)}, u32[]{:S(2)}) copy-start(s32[3072]{0:T(1024)S(1)} %eq.312) | copy-start | bytes 36868
  1416.3 313.8 %copy-start.71 = (pred[512]{0:T(512)(128)(4,1)}, pred[512]{0:T(512)(128)(4,1)S(1)}, u32[]{:S(2)}) copy-start(pred[512]{0:T(512)(128)(4,1)S(1)} %iota_compare_fusion.10) | copy-start | bytes 1540
  1417.6 346.8 %copy-start.86 = (f32[768]{0:T(1024)}, f32[768]{0:T(1024)S(1)}, u32[]{:S(2)}) copy-start(f32[768]{0:T(1024)S(1)} %get-tuple-element.279) | copy-start | bytes 9220
  1417.6 438.3 %copy-start.69 = (f32[768]{0:T(1024)}, f32[768]{0:T(1024)S(1)}, u32[]{:S(2)}) copy-start(f32[768]{0:T(1024)S(1)} %get-tuple-element.278) | copy-start | bytes 9220
  1664.6 168.5 %reduce-scatter.13.cloned.1.call-start = ((), (), s32[]{:S(2)}) async-start(), calls=%async_computation.10 | async-start | bytes 737280 | tf_op jit(solution)/shard_map/reduce_scatter | solution.py:421
  1827.3 115.3 %all-gather.18.cloned.1.call-start = ((), (), s32[]{:S(2)}) async-start(), calls=%async_computation.11 | async-start | bytes 2359296 | tf_op jit(solution)/shard_map/all_gather | solution.py:435
  1897.1 282.3 %reduce-scatter.21.cloned.1.call-start = ((), (), s32[]{:S(2)}) async-start(), calls=%async_computation.16 | async-start | bytes 1622016
  1898.8 282.2 %reduce-scatter.17.cloned.1.call-start = ((), (), s32[]{:S(2)}) async-start(), calls=%async_computation.13 | async-start | bytes 9732096 | tf_op jit(solution)/shard_map/reduce_scatter | solution.py:441
  1905.9 461.5 %reduce-scatter.15.cloned.1.call-start = ((), (), s32[]{:S(2)}) async-start(), calls=%async_computation.12 | async-start | bytes 19464192 | tf_op jit(solution)/shard_map/reduce_scatter | solution.py:440
  1922.5 1110.5 %reduce-scatter.19.cloned.1.call-start = ((), (), s32[]{:S(2)}) async-start(), calls=%async_computation.15 | async-start | bytes 50135040
  2034.8 92.1 %copy-start.58 = (f32[12,64]{1,0:T(8,128)S(1)}, f32[12,64]{1,0:T(8,128)}, u32[]{:S(2)}) copy-start(f32[12,64]{1,0:T(8,128)} %get-tuple-element.305) | copy-start | bytes 9220
  2034.8 92.2 %copy-start.66 = (f32[768]{0:T(1024)S(1)}, f32[768]{0:T(1024)}, u32[]{:S(2)}) copy-start(f32[768]{0:T(1024)} %get-tuple-element.200) | copy-start | bytes 9220
  2034.8 97.4 %copy-start.65 = (f32[768]{0:T(1024)S(1)}, f32[768]{0:T(1024)}, u32[]{:S(2)}) copy-start(f32[768]{0:T(1024)} %get-tuple-element.202) | copy-start | bytes 9220
  2034.8 98.7 %copy-start.63 = (f32[768]{0:T(1024)S(1)}, f32[768]{0:T(1024)}, u32[]{:S(2)}) copy-start(f32[768]{0:T(1024)} %get-tuple-element.206) | copy-start | bytes 9220
  2034.9 105.2 %copy-start.64 = (f32[768]{0:T(1024)S(1)}, f32[768]{0:T(1024)}, u32[]{:S(2)}) copy-start(f32[768]{0:T(1024)} %get-tuple-element.243) | copy-start | bytes 9220
  2036.0 145.0 %copy-start.31 = (f32[24,3072]{1,0:T(8,128)S(1)}, f32[24,3072]{1,0:T(8,128)}, u32[]{:S(2)}) copy-start(f32[24,3072]{1,0:T(8,128)} %param.55) | copy-start | bytes 884740
  2036.0 145.0 %copy-start.53 = (s32[3072]{0:T(1024)S(1)}, s32[3072]{0:T(1024)}, u32[]{:S(2)}) copy-start(s32[3072]{0:T(1024)} %copy-done.52) | copy-start | bytes 36868
  2036.0 331.4 %copy-start.20 = (f32[192,768]{1,0:T(8,128)S(1)}, f32[192,768]{1,0:T(8,128)}, u32[]{:S(2)}) copy-start(f32[192,768]{1,0:T(8,128)} %param.52) | copy-start | bytes 1769476
  2037.5 330.0 %copy-start.32 = (s32[192,768]{1,0:T(8,128)S(1)}, s32[192,768]{1,0:T(8,128)}, u32[]{:S(2)}) copy-start(s32[192,768]{1,0:T(8,128)} %copy.259) | copy-start | bytes 1769476
  2037.5 330.0 %copy-start.33 = (s32[192,768]{1,0:T(8,128)S(1)}, s32[192,768]{1,0:T(8,128)}, u32[]{:S(2)}) copy-start(s32[192,768]{1,0:T(8,128)} %copy.260) | copy-start | bytes 1769476
  2125.6 53.8 %copy-start.43 = (f32[15360]{0:T(1024)}, f32[15360]{0:T(1024)S(1)}, u32[]{:S(2)}) copy-start(f32[15360]{0:T(1024)S(1)} %psum.28) | copy-start | bytes 184324
  3044.3 51.2 %copy-start.7 = (f32[15360,48]{0,1:T(8,128)S(1)}, f32[15360,48]{0,1:T(8,128)}, u32[]{:S(2)}) copy-start(f32[15360,48]{0,1:T(8,128)} %param.46) | copy-start | bytes 8847364
  (91 other events, 789.3 us)
Sparse Core Ops, SparseCore 0:
  10.9 57.6 all-gather.19
  400.2 59.9 all-gather.15
  1168.1 67.5 all-gather.13
  1238.9 260.7 all-gather.11
  1664.7 6.7 reduce-scatter.10
  1827.4 5.6 reduce-scatter.12
  1897.2 10.9 all-gather.17
  1914.9 98.2 reduce-scatter.20
  2020.1 135.1 reduce-scatter.16
  2161.6 205.8 reduce-scatter.14
  2373.6 659.3 reduce-scatter.18
where the time goes:
time: 3130 us; the launch traced here: 3110 us
  local copies, waits for them, and re-layouts  1460 us (47%)
  waiting for transfers between devices  851 us (27%)
  other arithmetic  347 us (11%)
  blocking collectives  291 us (9%)
  matrix products  138 us (4%)
    gather x10, local copies, waits for them, and re-layouts, select_kept(): kept = jnp.take_along_axis(grouped, places, axis=2)  1120 us
    unnamed x13, waiting for transfers between devices  661 us
    reduce_scatter x1, waiting for transfers between devices, local(): lax.psum_scatter(stack_grad, ('fsdp', 'vocab'), scatter_dimension=0, tile...  184 us
    select_n x4, other arithmetic, unpack(): digits = words[..., None] // powers % 4  171 us
    unnamed x258, local copies, waits for them, and re-layouts  95.6 us
    unnamed x3, blocking collectives  83.3 us
    psum x1, blocking collectives, local(): bias_total = lax.psum(bias_local, 'fsdp')  79.1 us
  transfers between devices with their start and end apart: 11, of which 3 were waited for; matrix products, arithmetic and copies ran while one was open for 54% of the time, Pallas kernels for 0%

commit v1 on v0

--- a/solution.py
+++ b/solution.py
@@ -1,6 +1,11 @@
+import functools
+import math
+
 import jax
 import jax.numpy as jnp
 from jax import lax
+from jax.experimental import pallas as pl
+from jax.experimental.pallas import tpu as pltpu
 from jax.sharding import PartitionSpec as P
 
 HEAD_DIM = 64
@@ -19,50 +24,223 @@
 SCORE_SCALE = 0.125
 
 
-def combined_all(x, axis, combine):
-    everything = jax.tree.map(lambda part: lax.all_gather(part, axis), x)
-    first = jax.tree.map(lambda part: part[0], everything)
-
-    def turn(k, so_far):
-        return combine(so_far, jax.tree.map(lambda part: part[k], everything))
-
-    return lax.fori_loop(1, lax.axis_size(axis), turn, first)
-
-
-def unpack(words):
-    powers = 4 ** jnp.arange(8, dtype=jnp.int32)
-    digits = words[..., None] // powers % 4
-    return digits.reshape(words.shape[0], words.shape[1] * 8)
-
-
-def keep_mask(words):
-    count_rows = words.shape[0]
-    groups = words.shape[1] * 4
-    places = unpack(words).reshape(count_rows, groups, 2)
-    spots = jnp.arange(4, dtype=jnp.int32)
-    chosen = (places[:, :, 0:1] == spots) | (places[:, :, 1:2] == spots)
-    return chosen.reshape(count_rows, groups * 4).astype(jnp.float32)
-
-
-def select_kept(weight_matrix, words):
-    count_rows, width = weight_matrix.shape
-    grouped = weight_matrix.reshape(count_rows, width // 4, 4)
-    places = unpack(words).reshape(count_rows, width // 4, 2)
-    kept = jnp.take_along_axis(grouped, places, axis=2)
-    return kept.reshape(count_rows, width // 2).astype(jnp.bfloat16)
-
-
-def expand(kept, words):
-    count_rows = kept.shape[0]
-    groups = kept.shape[1] // 2
-    pairs = kept.reshape(count_rows, groups, 2)
-    places = unpack(words).reshape(count_rows, groups, 2)
-    spots = jnp.arange(4, dtype=jnp.int32)
-    nothing = jnp.zeros((), jnp.bfloat16)
-    dense = jnp.where(places[:, :, 0:1] == spots, pairs[:, :, 0:1], nothing) + jnp.where(
-        places[:, :, 1:2] == spots, pairs[:, :, 1:2], nothing
-    )
-    return dense.reshape(count_rows, groups * 4)
+HIGH_COUNT = 512
+BOTH = ("fsdp", "vocab")
+
+
+def kept(words):
+    columns = words.shape[1] * 16
+    place = lax.broadcasted_iota(jnp.int32, (2 * words.shape[1], columns), 0)
+    column = lax.broadcasted_iota(jnp.int32, (2 * words.shape[1], columns), 1)
+    spread = (place % words.shape[1] * 2 + place // words.shape[1] == column // 8).astype(
+        jnp.bfloat16
+    )
+    bytes_low = jnp.concatenate([words & 255, words >> 8], 1).astype(jnp.bfloat16)
+    byte = jnp.dot(bytes_low, spread, preferred_element_type=jnp.float32).astype(jnp.int32)
+    spot = lax.broadcasted_iota(jnp.int32, byte.shape, 1)
+    nibble = jnp.where(spot % 8 < 4, byte & 15, byte >> 4)
+    spot = spot % 4
+    return ((nibble & 3) == spot) | ((nibble >> 2) == spot)
+
+
+def swap(x, axis, bit):
+    size = lax.axis_size(axis)
+    return lax.ppermute(x, axis, [(i, i ^ bit) for i in range(size)])
+
+
+def my_bit(axis, bit):
+    return lax.axis_index(axis) // bit % 2
+
+
+def bits_of(size):
+    return [1 << k for k in range(size.bit_length() - 1)]
+
+
+def sum_all(x, axis, bits):
+    for bit in bits:
+        x = jax.tree.map(lambda part: part + swap(part, axis, bit), x)
+    return x
+
+
+def join(x, axis, bit):
+    other = swap(x, axis, bit)
+    upper = my_bit(axis, bit) == 1
+    return jnp.stack([jnp.where(upper, other, x), jnp.where(upper, x, other)])
+
+
+def halve(x, axis, bit):
+    mine = my_bit(axis, bit)
+    return lax.dynamic_index_in_dim(x, mine, 0, False) + swap(
+        lax.dynamic_index_in_dim(x, 1 - mine, 0, False), axis, bit
+    )
+
+
+def near_exchange(take, near):
+    size = lax.axis_size("fsdp")
+    p = lax.axis_index("fsdp") % near
+    return [take(p)] + [
+        lax.ppermute(take(p ^ k), "fsdp", [(i, i ^ k) for i in range(size)]) for k in range(1, near)
+    ]
+
+
+def far_groups(near):
+    size = lax.axis_size("fsdp")
+    return [list(range(q, size, near)) for q in range(near)]
+
+
+def far_gather(x, near):
+    size = lax.axis_size("fsdp")
+    far = size // near
+    if far != 4:
+        return lax.all_gather(x, "fsdp", axis=0, tiled=True, axis_index_groups=far_groups(near))
+    z = lax.axis_index("fsdp") // near
+    up, down = [], []
+    send_up = send_down = x
+    for k in range(1, far):
+        send_up = lax.ppermute(
+            send_up, "fsdp", [(i, i + near) for i in range((k - 1) * near, size - near)]
+        )
+        send_down = lax.ppermute(
+            send_down, "fsdp", [(i, i - near) for i in range(near, size - (k - 1) * near)]
+        )
+        up.append(send_up)
+        down.append(send_down)
+    line = jnp.concatenate(up[::-1] + [x] + down, 0)
+    rows = x.shape[0]
+    return lax.dynamic_slice_in_dim(line, (far - 1 - z) * rows, far * rows, 0)
+
+
+def far_scatter(x, near):
+    size = lax.axis_size("fsdp")
+    far = size // near
+    if far != 4:
+        flat = lax.psum_scatter(
+            x, "fsdp", scatter_dimension=0, tiled=True, axis_index_groups=far_groups(near)
+        )
+        return flat[0]
+    z = lax.axis_index("fsdp") // near
+
+    def entry(j):
+        return lax.dynamic_index_in_dim(x, jnp.clip(j, 0, far - 1), 0, False)
+
+    up = down = None
+    for k in range(1, far):
+        send_up, send_down = entry(far - k + z), entry(z - far + k)
+        if up is not None:
+            send_up, send_down = send_up + up, send_down + down
+        up = lax.ppermute(send_up, "fsdp", [(i, i + near) for i in range(k * near)])
+        down = lax.ppermute(
+            send_down, "fsdp", [(i, i - near) for i in range(size - k * near, size)]
+        )
+    return entry(z) + up + down
+
+
+def lookup_kernel(low_count, ids_ref, table_ref, out_ref, spread):
+    width = table_ref.shape[0]
+
+    @pl.when(pl.program_id(0) == 0)
+    def _():
+        for low in range(low_count):
+            spread[low * width : (low + 1) * width, :] = table_ref[
+                :, low * HIGH_COUNT : (low + 1) * HIGH_COUNT
+            ].astype(jnp.bfloat16)
+
+    ids = ids_ref[0]
+    low_ids = ids >> 9
+    row = lax.broadcasted_iota(jnp.int32, (HIGH_COUNT, ids.shape[1]), 0)
+    match = (row == (ids & (HIGH_COUNT - 1))).astype(jnp.bfloat16)
+    found = jnp.dot(spread[...], match, preferred_element_type=jnp.float32)
+    total = jnp.zeros((width, ids.shape[1]), jnp.float32)
+    for low in range(low_count):
+        total = jnp.where(low_ids == low, found[low * width : (low + 1) * width, :], total)
+    out_ref[0] = total.astype(out_ref.dtype)
+
+
+def lookup(table_t, ids):
+    rows = table_t.shape[0]
+    table_t = jnp.pad(table_t, ((0, -rows % 16), (0, 0)))
+    width, vocab = table_t.shape
+    blocks, _, length = ids.shape
+    low_count = vocab // HIGH_COUNT
+    found = pl.pallas_call(
+        functools.partial(lookup_kernel, low_count),
+        grid=(blocks,),
+        in_specs=[
+            pl.BlockSpec((1, 1, length), lambda i: (i, 0, 0)),
+            pl.BlockSpec((width, vocab), lambda i: (0, 0)),
+        ],
+        out_specs=pl.BlockSpec((1, width, length), lambda i: (i, 0, 0)),
+        out_shape=jax.ShapeDtypeStruct((blocks, width, length), jnp.bfloat16),
+        scratch_shapes=[pltpu.VMEM((low_count * width, HIGH_COUNT), jnp.bfloat16)],
+        compiler_params=pltpu.CompilerParams(vmem_limit_bytes=40 * 1024 * 1024),
+        cost_estimate=pl.CostEstimate(
+            flops=2 * blocks * length * width * vocab,
+            bytes_accessed=4 * width * vocab + 2 * blocks * width * length,
+            transcendentals=0,
+        ),
+        name="lookup",
+    )(ids, table_t)
+    return found[:, :rows]
+
+
+def spread_kernel(low_count, ids_ref, grad_ref, base_ref, out_ref, lhs, total):
+    width = grad_ref.shape[1]
+    step = pl.program_id(0)
+
+    @pl.when(step == 0)
+    def _():
+        total[...] = jnp.zeros_like(total)
+
+    ids = ids_ref[0]
+    low_ids = ids >> 9
+    grad = grad_ref[0].astype(jnp.float32)
+    for low in range(low_count):
+        lhs[low * width : (low + 1) * width, :] = jnp.where(low_ids == low, grad, 0.0).astype(
+            jnp.bfloat16
+        )
+    row = lax.broadcasted_iota(jnp.int32, (HIGH_COUNT, ids.shape[1]), 0)
+    match = (row == (ids & (HIGH_COUNT - 1))).astype(jnp.bfloat16)
+    total[...] += lax.dot_general(
+        lhs[...], match, (((1,), (1,)), ((), ())), preferred_element_type=jnp.float32
+    )
+
+    @pl.when(step == pl.num_programs(0) - 1)
+    def _():
+        for low in range(low_count):
+            span = slice(low * HIGH_COUNT, (low + 1) * HIGH_COUNT)
+            out_ref[:, span] = base_ref[:, span] + total[low * width : (low + 1) * width, :]
+
+
+def spread_add(base_t, grads, ids):
+    rows = base_t.shape[0]
+    base_t = jnp.pad(base_t, ((0, -rows % 16), (0, 0)))
+    grads = jnp.pad(grads, ((0, 0), (0, -rows % 16), (0, 0)))
+    width, vocab = base_t.shape
+    blocks, _, length = ids.shape
+    low_count = vocab // HIGH_COUNT
+    summed = pl.pallas_call(
+        functools.partial(spread_kernel, low_count),
+        grid=(blocks,),
+        in_specs=[
+            pl.BlockSpec((1, 1, length), lambda i: (i, 0, 0)),
+            pl.BlockSpec((1, width, length), lambda i: (i, 0, 0)),
+            pl.BlockSpec((width, vocab), lambda i: (0, 0)),
+        ],
+        out_specs=pl.BlockSpec((width, vocab), lambda i: (0, 0)),
+        out_shape=jax.ShapeDtypeStruct((width, vocab), jnp.float32),
+        scratch_shapes=[
+            pltpu.VMEM((low_count * width, length), jnp.bfloat16),
+            pltpu.VMEM((low_count * width, HIGH_COUNT), jnp.float32),
+        ],
+        compiler_params=pltpu.CompilerParams(vmem_limit_bytes=40 * 1024 * 1024),
+        cost_estimate=pl.CostEstimate(
+            flops=2 * blocks * length * width * vocab,
+            bytes_accessed=8 * width * vocab + 2 * blocks * width * length,
+            transcendentals=0,
+        ),
+        name="spread_add",
+    )(ids, grads, base_t)
+    return summed[:rows]
 
 
 def split_vectors(vectors_all, width):
@@ -106,20 +284,6 @@
 
 def column_sum(gradient_tree):
     return jnp.sum(gradient_tree.astype(jnp.float32), axis=(0, 1))
-
-
-def collect(proj_stack, ffn_down, stack_index, down_index, pos_table, vectors):
-    pos_low = pos_table.astype(jnp.bfloat16)
-    vectors_low = vectors.astype(jnp.bfloat16)
-    kept_stack, kept_down, words_stack, words_down, pos_all, vectors_all = (
-        lax.all_gather(select_kept(proj_stack, stack_index), ("fsdp", "vocab"), axis=0, tiled=True),
-        lax.all_gather(select_kept(ffn_down, down_index), ("fsdp", "vocab"), axis=0, tiled=True),
-        lax.all_gather(stack_index, ("fsdp", "vocab"), axis=0, tiled=True),
-        lax.all_gather(down_index, ("fsdp", "vocab"), axis=0, tiled=True),
-        lax.all_gather(pos_low, ("fsdp", "vocab"), axis=1, tiled=True),
-        lax.all_gather(vectors_low, ("fsdp", "vocab"), axis=0, tiled=True),
-    )
-    return (expand(kept_stack, words_stack), expand(kept_down, words_down), pos_all, vectors_all)
 
 
 def attend(pieces):
@@ -351,103 +515,199 @@
     bias_first,
     bias_second_moment,
 ):
+    size = lax.axis_size("fsdp")
+    devices = size * lax.axis_size("vocab")
+    near = math.gcd(4, size)
+    far = size // near
     width = proj_stack.shape[1]
+    units = ffn_down.shape[1]
     pair_seqs, seq_len = token_ids.shape
-    own_seqs = pair_seqs // lax.axis_size("vocab")
-    core_index = lax.axis_index("vocab")
-    column_index = lax.axis_index("fsdp")
-    vocab_dev = word_table.shape[0]
+    own_seqs = pair_seqs // 2
     own_rows = own_seqs * seq_len
+    core = lax.axis_index("vocab")
+    place = lax.axis_index("fsdp")
+    p = place % near
+    vocab_dev, columns = word_table.shape
+    part = vocab_dev // near
     mask_slots = masked_pos.shape[1]
-    stack_mask = keep_mask(stack_index)
-    down_mask = keep_mask(down_index)
-    dense_stack, dense_down, pos_all, vectors_all = collect(
-        proj_stack, ffn_down, stack_index, down_index, pos_table, vectors
-    )
+    near_bits = bits_of(near)
+    far_bits = [near * bit for bit in bits_of(far)]
+
+    stack_mask = kept(stack_index)
+    down_mask = kept(down_index)
+    stack_rows = proj_stack.shape[0]
+    down_rows = ffn_down.shape[0]
+    chunks = units // width
+    own_stack = jnp.where(stack_mask, proj_stack, 0.0).astype(jnp.bfloat16)
+    own_down = jnp.where(down_mask, ffn_down, 0.0).astype(jnp.bfloat16)
+    own_small = jnp.concatenate(
+        [pos_table.T.reshape(-1), vectors], 0
+    ).astype(jnp.bfloat16)
+    small_rows = -(-own_small.shape[0] // (16 * width)) * 16
+    own_small = jnp.pad(own_small, (0, small_rows * width - own_small.shape[0]))
+    everything = lax.all_gather(
+        jnp.concatenate(
+            [own_stack]
+            + [own_down[:, j * width : (j + 1) * width] for j in range(chunks)]
+            + [own_small.reshape(small_rows, width)],
+            0,
+        ),
+        BOTH,
+        axis=0,
+    )
+    dense_stack = everything[:, :stack_rows].reshape(-1, width)
+    dense_down = jnp.concatenate(
+        [
+            everything[:, stack_rows + j * down_rows : stack_rows + (j + 1) * down_rows].reshape(
+                -1, width
+            )
+            for j in range(chunks)
+        ],
+        1,
+    )
+    small = everything[:, stack_rows + chunks * down_rows :].reshape(devices, -1)
+    pos_count = pos_table.size
+    pos_all_t = small[:, :pos_count].reshape(width, seq_len)
+    vectors_all = small[:, pos_count : pos_count + vectors.shape[0]].reshape(-1)
     parts = split_vectors(vectors_all.astype(jnp.float32), width)
-    table_half = lax.all_gather(word_table.astype(jnp.bfloat16), "fsdp", axis=1, tiled=True)
-    local_ids = token_ids.reshape(-1) - core_index * vocab_dev
-    inside = (local_ids >= 0) & (local_ids < vocab_dev)
-    clipped_ids = jnp.clip(local_ids, 0, vocab_dev - 1)
-    looked = jnp.where(
-        inside[:, None], jnp.take(table_half, clipped_ids, axis=0).astype(jnp.float32), 0.0
-    )
-    own_embed = lax.psum_scatter(
-        looked.astype(jnp.bfloat16), "vocab", scatter_dimension=0, tiled=True
-    ).astype(jnp.float32)
-    embedded = own_embed.reshape(own_seqs, seq_len, width) + pos_all.astype(jnp.float32)[None]
-    pair_start = column_index * pair_seqs
-    seq_start = pair_start + core_index * own_seqs
+
+    table_t = word_table.T
+    all_ids = lax.all_to_all(
+        jnp.broadcast_to(token_ids[None], (size, pair_seqs, seq_len)), "fsdp", 0, 0, tiled=True
+    ).reshape(size, 2, own_seqs, seq_len)
+    local_ids = (
+        jnp.concatenate(
+            [
+                lax.dynamic_index_in_dim(all_ids, core, 1, False),
+                lax.dynamic_index_in_dim(all_ids, 1 - core, 1, False),
+            ],
+            0,
+        ).reshape(2 * size * own_seqs, 1, seq_len)
+        - core * vocab_dev
+    )
+    half = size * own_seqs
+    found = lookup(table_t, local_ids)
+    own_found = found[:half] + swap(found[half:], "vocab", 1)
+    own_found = own_found.reshape(size, own_seqs, columns, seq_len)
+    tokens_t = lax.all_to_all(own_found, "fsdp", 0, 0, tiled=True)
+    tokens_t = tokens_t.transpose(1, 0, 2, 3).reshape(own_seqs, width, seq_len)
+    embedded = (tokens_t.astype(jnp.float32) + pos_all_t.astype(jnp.float32)[None]).transpose(
+        0, 2, 1
+    )
+
+    table_low = table_t.astype(jnp.bfloat16)
+    blocks = near_exchange(
+        lambda q: lax.dynamic_slice_in_dim(table_low, q * part, part, 1), near
+    )
+    near_table = jnp.zeros((near * columns, part), jnp.bfloat16)
+    for k, block in enumerate(blocks):
+        near_table = lax.dynamic_update_slice_in_dim(near_table, block, (p ^ k) * columns, 0)
+    table_part = far_gather(near_table, near)
+    teach = jnp.concatenate(
+        near_exchange(lambda q: lax.dynamic_slice_in_dim(teacher, q * part, part, 1), near), 0
+    )
+
+    seq_start = place * pair_seqs + core * own_seqs
     own_lengths = lax.dynamic_slice_in_dim(lengths, seq_start, own_seqs)
     live = jnp.arange(seq_len, dtype=jnp.int32)[None, :] < own_lengths[:, None]
     final, saved = layer_forward(embedded, live, dense_stack, dense_down, parts)
     own_pos = lax.dynamic_slice_in_dim(masked_pos, seq_start, own_seqs, 0)
     flat_rows = (jnp.arange(own_seqs, dtype=jnp.int32)[:, None] * seq_len + own_pos).reshape(-1)
     picked = jnp.take(final.reshape(own_rows, width), flat_rows, axis=0).astype(jnp.bfloat16)
-    pair_rows = lax.all_gather(picked, "vocab", axis=0, tiled=True)
-    output_logits = (
-        jnp.einsum("pd,vd->pv", pair_rows, table_half, preferred_element_type=jnp.float32)
-        + head_bias
-    )
-    teach = teacher.astype(jnp.float32)
+    rows = join(picked, "vocab", 1).reshape(-1, width)
+    for bit in near_bits:
+        rows = jnp.concatenate([rows, swap(rows, "fsdp", bit)], 0)
+    rows = rows.reshape(-1, width)
+
+    bias_part = lax.dynamic_slice_in_dim(head_bias, p * part, part)
+    output_logits = jnp.dot(rows, table_part, preferred_element_type=jnp.float32) + bias_part
+    teach = teach.astype(jnp.float32)
     student_top = jnp.max(output_logits, axis=-1)
     student_total = jnp.sum(jnp.exp(output_logits - student_top[:, None]), axis=-1)
     teacher_top = jnp.max(teach, axis=-1)
     weighted = jnp.exp(teach - teacher_top[:, None])
     teacher_total = jnp.sum(weighted, axis=-1)
     cross = jnp.sum(weighted * (teach - output_logits), axis=-1)
-    student_top, student_total, teacher_top, teacher_total, cross = combined_all(
-        (student_top, student_total, teacher_top, teacher_total, cross), "vocab", combine_stats
-    )
+    stats = jnp.stack([student_top, student_total, teacher_top, teacher_total, cross])
+    stats = jnp.stack(combine_stats(stats, swap(stats, "vocab", 1)))
+    for bit in near_bits:
+        other = swap(stats, "fsdp", bit).reshape(5, near, -1)
+        other = jnp.concatenate([other[:, k ^ bit] for k in range(near)], 1)
+        stats = jnp.stack(combine_stats(stats, other))
+    student_top, student_total, teacher_top, teacher_total, cross = stats
     student_lse = student_top + jnp.log(student_total)
     teacher_lse = teacher_top + jnp.log(teacher_total)
     divergence = cross / teacher_total - teacher_lse + student_lse
-    pair_pos = lax.dynamic_slice_in_dim(masked_pos, pair_start, pair_seqs, 0)
-    pair_lengths = lax.dynamic_slice_in_dim(lengths, pair_start, pair_seqs)
-    pair_valid = (pair_pos < pair_lengths[:, None]).astype(jnp.float32).reshape(-1)
+    group_pos = []
+    group_lengths = []
+    for k in range(near):
+        start = (place ^ k) * pair_seqs
+        group_pos.append(lax.dynamic_slice_in_dim(masked_pos, start, pair_seqs, 0))
+        group_lengths.append(lax.dynamic_slice_in_dim(lengths, start, pair_seqs))
+    group_valid = (
+        (jnp.concatenate(group_pos, 0) < jnp.concatenate(group_lengths, 0)[:, None])
+        .astype(jnp.float32)
+        .reshape(-1)
+    )
     count = jnp.sum((masked_pos < lengths[:, None]).astype(jnp.float32))
-    own_slots = own_seqs * mask_slots
-    own_loss = jnp.sum(
-        lax.dynamic_slice_in_dim(divergence * pair_valid, core_index * own_slots, own_slots)
-    )
-    scale_rows = (pair_valid / count)[:, None]
+    group_loss = jnp.sum(divergence * group_valid) / (2 * near)
+    scale_rows = (group_valid / count)[:, None]
     grad_logits = (
         (jnp.exp(output_logits - student_lse[:, None]) - jnp.exp(teach - teacher_lse[:, None]))
         * scale_rows
     ).astype(jnp.bfloat16)
-    bias_local = jnp.sum(grad_logits.astype(jnp.float32), axis=0)
-    table_grad = jnp.einsum("pv,pd->vd", grad_logits, pair_rows, preferred_element_type=jnp.float32)
-    rows_grad = jnp.einsum("pv,vd->pd", grad_logits, table_half, preferred_element_type=jnp.float32)
-    own_rows_grad = lax.psum_scatter(rows_grad, "vocab", scatter_dimension=0, tiled=True)
+    rows_grad = lax.dot_general(
+        grad_logits, table_part, (((1,), (1,)), ((), ())), preferred_element_type=jnp.float32
+    )
+    rows_grad = rows_grad.reshape(near, 2, -1, width).transpose(1, 0, 2, 3)
+    rows_grad = halve(rows_grad, "vocab", 1)
+    for bit in near_bits[::-1]:
+        rows_grad = rows_grad[:bit] + swap(rows_grad[bit:], "fsdp", bit)
+    own_rows_grad = rows_grad[0]
     grad_final = (
         jnp.zeros((own_rows, width), jnp.float32)
         .at[flat_rows]
         .add(own_rows_grad)
         .reshape(own_seqs, seq_len, width)
     )
-    back_stack, back_down, pos_again, vectors_again = collect(
-        proj_stack, ffn_down, stack_index, down_index, pos_table, vectors
-    )
+
+    bias_grad = sum_all(jnp.sum(grad_logits.astype(jnp.float32), axis=0), "fsdp", far_bits)
+    for bit in near_bits:
+        bias_grad = join(bias_grad, "fsdp", bit).reshape(-1)
+    head_grad = lax.dot_general(
+        rows, grad_logits, (((0,), (0,)), ((), ())), preferred_element_type=jnp.float32
+    )
+    head_grad = far_scatter(head_grad.reshape(far, near, columns, part), near)
+    blocks = near_exchange(lambda q: lax.dynamic_index_in_dim(head_grad, q, 0, False), near)
+    head_grad_t = jnp.zeros((columns, vocab_dev), jnp.float32)
+    for k, block in enumerate(blocks):
+        head_grad_t = lax.dynamic_update_slice_in_dim(head_grad_t, block, (p ^ k) * part, 1)
+
     grad_embed, stack_grad, down_grad, vectors_grad = layer_backward(
-        grad_final, saved, live, back_stack, back_down, parts
-    )
-    pos_grad = jnp.sum(grad_embed, axis=0)
-    pair_embed_grad = lax.all_gather(
-        grad_embed.reshape(own_rows, width).astype(jnp.bfloat16), "vocab", axis=0, tiled=True
-    ).astype(jnp.float32)
-    table_grad = table_grad.at[clipped_ids].add(jnp.where(inside[:, None], pair_embed_grad, 0.0))
-    stack_total, down_total, pos_total, vectors_total = (
-        lax.psum_scatter(stack_grad, ("fsdp", "vocab"), scatter_dimension=0, tiled=True),
-        lax.psum_scatter(down_grad, ("fsdp", "vocab"), scatter_dimension=0, tiled=True),
-        lax.psum_scatter(pos_grad, ("fsdp", "vocab"), scatter_dimension=1, tiled=True),
-        lax.psum_scatter(vectors_grad, ("fsdp", "vocab"), scatter_dimension=0, tiled=True),
-    )
-    table_total = lax.psum_scatter(table_grad, "fsdp", scatter_dimension=1, tiled=True)
-    bias_total = lax.psum(bias_local, "fsdp")
-    stack_total = stack_total + PRUNE_DECAY * (1.0 - stack_mask) * proj_stack
-    down_total = down_total + PRUNE_DECAY * (1.0 - down_mask) * ffn_down
-    changes = jnp.sum((stack_mask != keep_mask(stack_next)).astype(jnp.float32)) + jnp.sum(
-        (down_mask != keep_mask(down_next)).astype(jnp.float32)
+        grad_final, saved, live, dense_stack, dense_down, parts
+    )
+    stack_total = lax.psum_scatter(stack_grad, BOTH, scatter_dimension=0, tiled=True)
+    down_total = lax.psum_scatter(down_grad, BOTH, scatter_dimension=0, tiled=True)
+
+    embed_t = grad_embed.transpose(0, 2, 1).astype(jnp.bfloat16)
+    embed_t = embed_t.reshape(own_seqs, size, columns, seq_len).transpose(1, 0, 2, 3)
+    embed_t = lax.all_to_all(embed_t, "fsdp", 0, 0, tiled=True).reshape(half, columns, seq_len)
+    embed_t = jnp.concatenate([embed_t, swap(embed_t, "vocab", 1)], 0)
+    table_total = spread_add(head_grad_t, embed_t, local_ids)
+    pos_total = jnp.sum(embed_t.astype(jnp.float32), axis=0)
+    pos_total = lax.dynamic_slice_in_dim(pos_total, core * (columns // 2), columns // 2, 0)
+
+    vectors_grad = sum_all(vectors_grad, "vocab", [1])
+    vectors_grad = sum_all(vectors_grad, "fsdp", near_bits + far_bits)
+    small_count = vectors.shape[0]
+    vectors_total = lax.dynamic_slice_in_dim(
+        vectors_grad, (2 * place + core) * small_count, small_count
+    )
+
+    stack_total = stack_total + jnp.where(stack_mask, 0.0, PRUNE_DECAY) * proj_stack
+    down_total = down_total + jnp.where(down_mask, 0.0, PRUNE_DECAY) * ffn_down
+    changes = jnp.sum((stack_mask != kept(stack_next)).astype(jnp.float32)) + jnp.sum(
+        (down_mask != kept(down_next)).astype(jnp.float32)
     )
     squares = (
         jnp.sum(stack_total * stack_total)
@@ -455,26 +715,27 @@
         + jnp.sum(pos_total * pos_total)
         + jnp.sum(vectors_total * vectors_total)
         + jnp.sum(table_total * table_total)
-        + jnp.sum(bias_total * bias_total) / lax.axis_size("fsdp")
-    )
-    total_squares, loss_sum, change_total = lax.psum(
-        (squares, own_loss, changes), ("fsdp", "vocab")
-    )
+        + jnp.sum(bias_grad * bias_grad) / size
+    )
+    scalars = jnp.stack([squares, group_loss, changes])
+    scalars = sum_all(scalars, "vocab", [1])
+    scalars = sum_all(scalars, "fsdp", near_bits + far_bits)
+    total_squares, loss_sum, change_total = scalars[0], scalars[1], scalars[2]
     grad_norm = jnp.sqrt(total_squares)
     factor = jnp.minimum(1.0, CLIP / (grad_norm + 1e-06))
-    table_out = adam(word_table, table_total * factor, table_first, table_second, RATE_MATRIX)
-    pos_out = adam(pos_table, pos_total * factor, pos_first, pos_second, RATE_MATRIX)
+    table_out = adam(table_t, table_total * factor, table_first.T, table_second.T, RATE_MATRIX)
+    pos_out = adam(pos_table.T, pos_total * factor, pos_first.T, pos_second.T, RATE_MATRIX)
     stack_out = adam(proj_stack, stack_total * factor, stack_first, stack_second, RATE_MATRIX)
     down_out = adam(ffn_down, down_total * factor, down_first, down_second, RATE_MATRIX)
     vectors_out = adam(vectors, vectors_total * factor, vectors_first, vectors_second, RATE_VECTOR)
-    bias_out = adam(head_bias, bias_total * factor, bias_first, bias_second_moment, RATE_VECTOR)
+    bias_out = adam(head_bias, bias_grad * factor, bias_first, bias_second_moment, RATE_VECTOR)
     return (
-        table_out[0],
-        table_out[1],
-        table_out[2],
-        pos_out[0],
-        pos_out[1],
-        pos_out[2],
+        table_out[0].T,
+        table_out[1].T,
+        table_out[2].T,
+        pos_out[0].T,
+        pos_out[1].T,
+        pos_out[2].T,
         stack_out[0],
         stack_out[1],
         stack_out[2],

time: 3130 us -> 1060 us (0.34)
  local copies, waits for them, and re-layouts: 1460 us -> 105 us
  waiting for transfers between devices: 851 us -> 422 us
  blocking collectives: 291 us -> 0 us
  other arithmetic: 347 us -> 129 us
  starting transfers between devices: 0.86 us -> 185 us
  Pallas kernels: 0 us -> 62.7 us
    gather x11 -> x0, local copies, waits for them, and re-layouts: 1140 us -> none  [the longest x10 1120 us: select_kept(): kept = jnp.take_along_axis(grouped, places, axis=2)]
    unnamed x13 -> x3, waiting for transfers between devices: 661 us -> 0.05 us
    ppermute x0 -> x46, waiting for transfers between devices: none -> 374 us  [the longest x3 172 us: far_scatter(): up = lax.ppermute(send_up, 'fsdp', [(i, i + near) for i in range(k * near)])]
    reduce_scatter x4 -> x2, waiting for transfers between devices: 190 us -> 0.01 us  [the longest x1 0.01 us: local(): lax.psum_scatter(down_grad, BOTH, scatter_dimension=0, tiled=True)]
    select_n x7 -> x3, other arithmetic: 171 us -> 0.02 us  [the longest x2 0.01 us: join(): return jnp.stack([jnp.where(upper, other, x), jnp.where(upper, x, other)])]
    ppermute x0 -> x46, starting transfers between devices: none -> 163 us  [the longest x25 112 us: swap(): return lax.ppermute(x, axis, [(i, i ^ bit) for i in range(size)])]
    psum x2 -> x0, blocking collectives: 119 us -> none  [the longest x1 79.1 us: local(): bias_total = lax.psum(bias_local, 'fsdp')]
    all_gather x3 -> x0, blocking collectives: 88.9 us -> none  [the longest x1 44.6 us: collect(): lax.all_gather(pos_low, ('fsdp', 'vocab'), axis=1, tiled=True)]
  transfers between devices with their start and end apart: 11 -> 52, of which waited for: 3 -> 30; matrix products, arithmetic and copies ran while one was open for 54% -> 24% of each run, Pallas kernels for 0% -> 6%
where the time goes in v1:
time: 1060 us; the launch traced here: 1050 us
  waiting for transfers between devices  422 us (40%)
  starting transfers between devices  185 us (17%)
  other arithmetic  129 us (12%)
  matrix products  122 us (12%)
  local copies, waits for them, and re-layouts  105 us (10%)
  Pallas kernels  62.7 us (6%)
  between operations  27.3 us (3%)
    ppermute x3, waiting for transfers between devices, far_scatter(): up = lax.ppermute(send_up, 'fsdp', [(i, i + near) for i in range(k * near)])  172 us
    ppermute x25, starting transfers between devices, swap(): return lax.ppermute(x, axis, [(i, i ^ bit) for i in range(size)])  112 us
    ppermute x25, waiting for transfers between devices, swap(): return lax.ppermute(x, axis, [(i, i ^ bit) for i in range(size)])  97.7 us
    ppermute x9, waiting for transfers between devices, near_exchange(): lax.ppermute(take(p ^ k), 'fsdp', [(i, i ^ k) for i in range(size)])  63 us
    all_to_all x1, waiting for transfers between devices, local(): lax.all_to_all(jnp.broadcast_to(token_ids[None], (size, pair_seqs, seq_le...  47.3 us
    ppermute x3, waiting for transfers between devices, far_gather(): lax.ppermute(send_down, 'fsdp', [(i, i - near) for i in range(near, size...  41.6 us
    unnamed x352, local copies, waits for them, and re-layouts  41 us
    pallas_call x1, Pallas kernels, spread_add(): pl.pallas_call(functools.partial(spread_kernel, low_count), grid=(blocks,...  31.9 us
  transfers between devices with their start and end apart: 52, of which 30 were waited for; matrix products, arithmetic and copies ran while one was open for 24% of the time, Pallas kernels for 6%

profile of v1, /device:TPU:0, one launch (start us, length us, event | category | flops | bytes accessed | tf_op | source)
XLA Modules:
  0.0 1052.8 jit_solution(6821185610490891270)
XLA Ops:
  23.5 10.3 collective-permute-done.4
  35.6 7.2 collective-permute-done.5
  55.3 47.3 %all-to-all-done = s32[16,2,512]{2,1,0:T(2,128)S(1)} async-done(((s32[16,2,512]{2,1,0:T(2,128)}), s32[16,2,512]{2,1,0:T(2,128)S(1)}, u32[]{:S(2)}, u32[]{:S(2)}) %all-to-all-start) | async-done | bytes 65568 | tf_op jit(solution)/shard_map/all_to_all | solution.py:575
  105.9 30.7 %lookup.1 = bf16[32,48,512]{2,1,0:T(8,128)(2,1)S(1)} custom-call(s32[32,1,512]{2,1,0:T(1,128)S(1)} %add_subtract_fusion.1.ids_ref, f32[48,15360]{1,0:T(8,128)S(1)} %bitcast.292), custom_call_target="tpu_custom_call" | custom-call | flops 24159191040 | bytes 4521984 | tf_op jit(solution)/shard_map/lookup/pallas_call | solution.py:165
  143.6 10.8 %all-to-all-start.1 = ((bf16[16,1,48,512]{3,2,1,0:T(8,128)(2,1)}), bf16[16,1,48,512]{3,2,1,0:T(8,128)(2,1)}, u32[]{:S(2)}, u32[]{:S(2)}) async-start(bf16[16,1,48,512]{3,2,1,0:T(8,128)(2,1)} %fusion.36), calls=%async_computation.1 | async-start | bytes 1572864 | tf_op jit(solution)/shard_map/all_to_all | solution.py:592
  154.5 29.7 %collective-permute-done.10 = bf16[192,3840]{1,0:T(8,128)(2,1)} collective-permute-done((bf16[192,3840]{1,0:T(8,128)(2,1)}, bf16[192,3840]{1,0:T(8,128)(2,1)}, u32[]{:S(2)}, u32[]{:S(2)}) %collective-permute-start.10) | collective-permute-done | bytes 1474592 | tf_op jit(solution)/shard_map/ppermute | solution.py:103
  195.5 8.9 collective-permute-done.15
  213.9 11.9 %collective-permute-done.11 = bf16[192,3840]{1,0:T(8,128)(2,1)} collective-permute-done((bf16[192,3840]{1,0:T(8,128)(2,1)}, bf16[192,3840]{1,0:T(8,128)(2,1)}, u32[]{:S(2)}, u32[]{:S(2)}) %collective-permute-start.11) | collective-permute-done | bytes 1474592 | tf_op jit(solution)/shard_map/ppermute | solution.py:103
  287.5 10.0 fusion.9
  303.4 19.7 %multiply_convert_fusion.1 = (bf16[512,3072]{1,0:T(8,128)(2,1)S(1)}, f32[512,3072]{1,0:T(8,128)}, f32[512,3072]{1,0:T(8,128)}) fusion(f32[3072]{0:T(1024)S(1)} %slice.228, bf16[3072,768]{1,0:T(8,128)(2,1)S(1)} %bitcast.322, f32[1,512,768]{2,1,0:T(8,128)S(1)} %get-tuple-element.226, f32[768]{0:T(1024)S(1)} %get-tuple-element.178, ...), kind=kOutput, calls=%fused_computation.28 | convolution fusion | flops 2521694208 | bytes 22042624 | tf_op jit(solution)/shard_map/ymh,ph->ymp/dot_general | solution.py:272
  348.0 6.7 collective-permute-done.3
  361.5 7.5 fusion.3
  380.2 7.8 convert_reduce_fusion
  388.0 8.4 fusion.16
  404.3 12.4 %collective-permute-done.20 = f32[2,80,768]{2,1,0:T(8,128)S(1)} collective-permute-done((f32[2,80,768]{2,1,0:T(8,128)S(1)}, f32[2,80,768]{2,1,0:T(8,128)S(1)}, u32[]{:S(2)}, u32[]{:S(2)}) %collective-permute-start.20) | collective-permute-done | bytes 491552 | tf_op jit(solution)/shard_map/ppermute | solution.py:48
  437.8 11.3 %convert_reduce_fusion.1 = (f32[3072]{0:T(1024)}, bf16[512,3072]{1,0:T(8,128)(2,1)S(1)}) fusion(f32[512,3072]{1,0:T(8,128)} %get-tuple-element.137, bf16[768,768]{1,0:T(8,128)(2,1)} %bitcast.339, bf16[768,768]{1,0:T(8,128)(2,1)} %bitcast.341, bf16[768,768]{1,0:T(8,128)(2,1)} %bitcast.343, bf16[768,768]{1,0:T(8,128)(2,1)} %bitcast.337, ...), kind=kOutput, calls=%fused_computation.26 | convolution fusion | flops 2461529088 | bytes 21258240 | tf_op jit(solution)/shard_map/faz,zh->fah/dot_general | solution.py:276
  463.6 12.0 %multiply_reduce_fusion = (f32[12,512]{1,0:T(8,128)S(1)}, f32[12,512,512]{1,2,0:T(8,128)}) fusion(f32[12,512,512]{1,2,0:T(8,128)} %copy-done.4, f32[12,512]{1,0:T(8,128)S(1)} %log_add_fusion, pred[512]{0:T(512)(128)(4,1)S(1)} %copy-done.87, bf16[512,12,64]{0,2,1:T(8,128)(2,1)S(1)} %bitcast.312, bf16[1,512,3,12,64]{1,4,3,2,0:T(8,128)(2,1)S(1)} %bitcast.304), kind=kOutput, calls=%fused_computation.7 | convolution fusion | flops 418375680 | bytes 26796544 | tf_op jit(solution)/shard_map/while/body/eval_jaxpr/qhe,khe->hqk/dot_general | solution.py:312
  477.3 10.8 %multiply_convert_fusion = bf16[12,512,512]{1,2,0:T(8,128)(2,1)} fusion(f32[12,512,512]{1,2,0:T(8,128)} %get-tuple-element.234, f32[12,512,512]{1,2,0:T(8,128)S(1)} %bitcast.294, f32[12,512]{1,0:T(8,128)S(1)} %get-tuple-element.233, f32[12,512]{1,0:T(8,128)S(1)} %log_add_fusion, pred[512]{0:T(512)(128)(4,1)S(1)} %copy-done.87), kind=kLoop, calls=%fused_computation.6 | loop fusion | flops 18874368 | bytes 31506944 | tf_op jit(solution)/shard_map/while/body/eval_jaxpr/convert_element_type | solution.py:316
  503.0 7.4 pad_maximum_fusion
  511.5 7.5 fusion.53
  525.1 11.0 %collective-permute-start.23 = (f32[4,48,3840]{2,1,0:T(8,128)}, f32[4,48,3840]{2,1,0:T(8,128)}, u32[]{:S(2)}, u32[]{:S(2)}) collective-permute-start(f32[4,48,3840]{2,1,0:T(8,128)} %get-tuple-element.146), channel_id=1, source_target_pairs={{0,8},{2,10},{4,12},{6,14},{1,9},{3,11},{5,13},{7,15}} | collective-permute-start | bytes 8847368 | tf_op jit(solution)/shard_map/ppermute | solution.py:131
  538.3 77.6 %collective-permute-done.23 = f32[4,48,3840]{2,1,0:T(8,128)} collective-permute-done((f32[4,48,3840]{2,1,0:T(8,128)}, f32[4,48,3840]{2,1,0:T(8,128)}, u32[]{:S(2)}, u32[]{:S(2)}) %collective-permute-start.23) | collective-permute-done | bytes 2949152 | tf_op jit(solution)/shard_map/ppermute | solution.py:131
  627.2 94.0 %collective-permute-done.24 = f32[4,48,3840]{2,1,0:T(8,128)} collective-permute-done((f32[4,48,3840]{2,1,0:T(8,128)}, f32[4,48,3840]{2,1,0:T(8,128)}, u32[]{:S(2)}, u32[]{:S(2)}) %collective-permute-start.24) | collective-permute-done | bytes 2949152 | tf_op jit(solution)/shard_map/ppermute | solution.py:131
  721.2 7.8 bitcast_add_fusion.3
  731.4 7.9 collective-permute-start.37
  741.0 82.5 %collective-permute-start.38 = (f32[3840]{0:T(1024)S(1)}, f32[3840]{0:T(1024)S(1)}, u32[]{:S(2)}, u32[]{:S(2)}) collective-permute-start(f32[3840]{0:T(1024)S(1)} %add.843), channel_id=1, source_target_pairs={{0,16},{2,18},{4,20},{6,22},{8,24},{10,26},{12,28},{14,30},{16,0},... | collective-permute-start | bytes 46088 | tf_op jit(solution)/shard_map/ppermute | solution.py:48
  850.1 7.3 all-to-all-start.2
  873.8 46.6 %collective-permute-done.35 = f32[10752]{0:T(1024)S(1)} collective-permute-done((f32[10752]{0:T(1024)S(1)}, f32[10752]{0:T(1024)S(1)}, u32[]{:S(2)}, u32[]{:S(2)}) %collective-permute-start.35) | collective-permute-done | bytes 43040 | tf_op jit(solution)/shard_map/ppermute | solution.py:48
  933.9 10.9 %collective-permute-done.29 = f32[48,3840]{1,0:T(8,128)S(1)} collective-permute-done((f32[48,3840]{1,0:T(8,128)S(1)}, f32[48,3840]{1,0:T(8,128)S(1)}, u32[]{:S(2)}, u32[]{:S(2)}) %collective-permute-start.29) | collective-permute-done | bytes 737312 | tf_op jit(solution)/shard_map/ppermute | solution.py:82
  944.8 20.3 %collective-permute-done.30 = f32[48,3840]{1,0:T(8,128)S(1)} collective-permute-done((f32[48,3840]{1,0:T(8,128)S(1)}, f32[48,3840]{1,0:T(8,128)S(1)}, u32[]{:S(2)}, u32[]{:S(2)}) %collective-permute-start.30) | collective-permute-done | bytes 737312 | tf_op jit(solution)/shard_map/ppermute | solution.py:82
  965.2 31.9 %spread_add.1 = f32[48,15360]{1,0:T(8,128)S(1)} custom-call(s32[32,1,512]{2,1,0:T(1,128)S(1)} %copy-done.3, bf16[32,48,512]{2,1,0:T(8,128)(2,1)S(1)} %pad_maximum_fusion.4.grad_ref, f32[48,15360]{1,0:T(8,128)S(1)} %constant_dynamic-update-slice_fusion.9.base_ref), custom_call_target="tpu_custom_call" | custom-call | flops 24159191040 | bytes 7471104 | tf_op jit(solution)/shard_map/spread_add/pallas_call | solution.py:221
  1030.9 8.8 subtract_bitcast_fusion
  (671 shorter events, 340.5 us)
Async XLA Ops:
  7.2 228.0 %all-gather.3.cloned.1.call-start = ((), (), s32[]{:S(2)}) async-start(), calls=%async_computation.7 | async-start | bytes 16220160 | tf_op jit(solution)/shard_map/all_gather | solution.py:548
  19.0 14.8 %collective-permute-start.4 = (bf16[48,3840]{1,0:T(8,128)(2,1)}, bf16[48,3840]{1,0:T(8,128)(2,1)}, u32[]{:S(2)}, u32[]{:S(2)}) collective-permute-start(bf16[48,3840]{1,0:T(8,128)(2,1)} %get-tuple-element.160), channel_id=1, source_target_pairs={{0,2},{2,0},{4,6},{6,4},{8,10},{10,8},{12,14},{14,12},{16,18},{18,... | collective-permute-start | bytes 1105928 | tf_op jit(solution)/shard_map/ppermute | solution.py:82
  22.0 20.8 %collective-permute-start.5 = (bf16[48,3840]{1,0:T(8,128)(2,1)}, bf16[48,3840]{1,0:T(8,128)(2,1)}, u32[]{:S(2)}, u32[]{:S(2)}) collective-permute-start(bf16[48,3840]{1,0:T(8,128)(2,1)} %get-tuple-element.159), channel_id=1, source_target_pairs={{0,4},{2,6},{4,0},{6,2},{8,12},{10,14},{12,8},{14,10},{16,20},{18,... | collective-permute-start | bytes 1105928 | tf_op jit(solution)/shard_map/ppermute | solution.py:82
  23.5 21.0 %collective-permute-start.6 = (bf16[48,3840]{1,0:T(8,128)(2,1)}, bf16[48,3840]{1,0:T(8,128)(2,1)S(1)}, u32[]{:S(2)}, u32[]{:S(2)}) collective-permute-start(bf16[48,3840]{1,0:T(8,128)(2,1)} %get-tuple-element.158), channel_id=1, source_target_pairs={{0,6},{2,4},{4,2},{6,0},{8,14},{10,12},{12,10},{14,8},{16,22},{18,... | collective-permute-start | bytes 1105928 | tf_op jit(solution)/shard_map/ppermute | solution.py:82
  45.3 58.8 %collective-permute-start.7 = (bf16[192,3840]{1,0:T(8,128)(2,1)}, bf16[192,3840]{1,0:T(8,128)(2,1)}, u32[]{:S(2)}, u32[]{:S(2)}) collective-permute-start(bf16[192,3840]{1,0:T(8,128)(2,1)} %constant_dynamic-update-slice_fusion.12), channel_id=1, source_target_pairs={{0,8},{2,10},{4,12},{6,14},{8,16},{10,18},{12,20},{14,22},{16,24},... | collective-permute-start | bytes 4423688 | tf_op jit(solution)/shard_map/ppermute | solution.py:100
  50.6 52.1 %all-to-all-start = ((s32[16,2,512]{2,1,0:T(2,128)}), s32[16,2,512]{2,1,0:T(2,128)S(1)}, u32[]{:S(2)}, u32[]{:S(2)}) async-start(s32[16,2,512]{2,1,0:T(2,128)} %broadcast_in_dim.91), calls=%async_computation | async-start | bytes 131072 | tf_op jit(solution)/shard_map/all_to_all | solution.py:575
  102.8 81.4 %collective-permute-start.10 = (bf16[192,3840]{1,0:T(8,128)(2,1)}, bf16[192,3840]{1,0:T(8,128)(2,1)}, u32[]{:S(2)}, u32[]{:S(2)}) collective-permute-start(bf16[192,3840]{1,0:T(8,128)(2,1)} %constant_dynamic-update-slice_fusion.12), channel_id=1, source_target_pairs={{8,0},{10,2},{12,4},{14,6},{16,8},{18,10},{20,12},{22,14},{24,16},... | collective-permute-start | bytes 4423688 | tf_op jit(solution)/shard_map/ppermute | solution.py:103
  104.1 81.4 %collective-permute-start.8 = (bf16[192,3840]{1,0:T(8,128)(2,1)}, bf16[192,3840]{1,0:T(8,128)(2,1)}, u32[]{:S(2)}, u32[]{:S(2)}) collective-permute-start(bf16[192,3840]{1,0:T(8,128)(2,1)} %collective-permute-done.7), channel_id=1, source_target_pairs={{8,16},{10,18},{12,20},{14,22},{16,24},{18,26},{20,28},{22,30},{9,... | collective-permute-start | bytes 4423688 | tf_op jit(solution)/shard_map/ppermute | solution.py:100
  139.2 50.9 %collective-permute-start.13 = (bf16[160,3840]{1,0:T(8,128)(2,1)}, bf16[160,3840]{1,0:T(8,128)(2,1)}, u32[]{:S(2)}, u32[]{:S(2)}) collective-permute-start(bf16[160,3840]{1,0:T(8,128)(2,1)} %get-tuple-element.152), channel_id=1, source_target_pairs={{0,2},{2,0},{4,6},{6,4},{8,10},{10,8},{12,14},{14,12},{16,18},{18,... | collective-permute-start | bytes 3686408 | tf_op jit(solution)/shard_map/ppermute | solution.py:82
  139.2 56.4 %collective-permute-start.14 = (bf16[160,3840]{1,0:T(8,128)(2,1)}, bf16[160,3840]{1,0:T(8,128)(2,1)}, u32[]{:S(2)}, u32[]{:S(2)}) collective-permute-start(bf16[160,3840]{1,0:T(8,128)(2,1)} %get-tuple-element.154), channel_id=1, source_target_pairs={{0,4},{2,6},{4,0},{6,2},{8,12},{10,14},{12,8},{14,10},{16,20},{18,... | collective-permute-start | bytes 3686408 | tf_op jit(solution)/shard_map/ppermute | solution.py:82
  141.2 63.2 %collective-permute-start.15 = (bf16[160,3840]{1,0:T(8,128)(2,1)}, bf16[160,3840]{1,0:T(8,128)(2,1)}, u32[]{:S(2)}, u32[]{:S(2)}) collective-permute-start(bf16[160,3840]{1,0:T(8,128)(2,1)} %get-tuple-element.153), channel_id=1, source_target_pairs={{0,6},{2,4},{4,2},{6,0},{8,14},{10,12},{12,10},{14,8},{16,22},{18,... | collective-permute-start | bytes 3686408 | tf_op jit(solution)/shard_map/ppermute | solution.py:82
  143.6 64.7 %all-to-all-start.1 = ((bf16[16,1,48,512]{3,2,1,0:T(8,128)(2,1)}), bf16[16,1,48,512]{3,2,1,0:T(8,128)(2,1)}, u32[]{:S(2)}, u32[]{:S(2)}) async-start(bf16[16,1,48,512]{3,2,1,0:T(8,128)(2,1)} %fusion.36), calls=%async_computation.1 | async-start | bytes 1572864 | tf_op jit(solution)/shard_map/all_to_all | solution.py:592
  154.4 845.7 %reduce-scatter.5.cloned.1.call-start = ((), (), s32[]{:S(2)}) async-start(), calls=%async_computation.6 | async-start | bytes 9732096 | tf_op jit(solution)/shard_map/reduce_scatter | solution.py:690
  184.2 41.6 %collective-permute-start.11 = (bf16[192,3840]{1,0:T(8,128)(2,1)}, bf16[192,3840]{1,0:T(8,128)(2,1)}, u32[]{:S(2)}, u32[]{:S(2)}) collective-permute-start(bf16[192,3840]{1,0:T(8,128)(2,1)} %collective-permute-done.10), channel_id=1, source_target_pairs={{8,0},{10,2},{12,4},{14,6},{16,8},{18,10},{20,12},{22,14},{9,1},{1... | collective-permute-start | bytes 4423688 | tf_op jit(solution)/shard_map/ppermute | solution.py:103
  185.5 41.9 %collective-permute-start.9 = (bf16[192,3840]{1,0:T(8,128)(2,1)}, bf16[192,3840]{1,0:T(8,128)(2,1)}, u32[]{:S(2)}, u32[]{:S(2)}) collective-permute-start(bf16[192,3840]{1,0:T(8,128)(2,1)} %collective-permute-done.8), channel_id=1, source_target_pairs={{16,24},{18,26},{20,28},{22,30},{17,25},{19,27},{21,29},{23,31}} | collective-permute-start | bytes 4423688 | tf_op jit(solution)/shard_map/ppermute | solution.py:100
  225.8 119.6 %collective-permute-start.12 = (bf16[192,3840]{1,0:T(8,128)(2,1)}, bf16[192,3840]{1,0:T(8,128)(2,1)}, u32[]{:S(2)}, u32[]{:S(2)}) collective-permute-start(bf16[192,3840]{1,0:T(8,128)(2,1)} %collective-permute-done.11), channel_id=1, source_target_pairs={{8,0},{10,2},{12,4},{14,6},{9,1},{11,3},{13,5},{15,7}} | collective-permute-start | bytes 4423688 | tf_op jit(solution)/shard_map/ppermute | solution.py:103
  341.8 12.9 %collective-permute-start.3 = (bf16[320,768]{1,0:T(8,128)(2,1)S(1)}, bf16[320,768]{1,0:T(8,128)(2,1)S(1)}, u32[]{:S(2)}, u32[]{:S(2)}) collective-permute-start(bf16[320,768]{1,0:T(8,128)(2,1)S(1)} %pad_maximum_fusion.12), channel_id=1, source_target_pairs={{0,4},{2,6},{4,0},{6,2},{8,12},{10,14},{12,8},{14,10},{16,20},{18,... | collective-permute-start | bytes 1474568 | tf_op jit(solution)/shard_map/ppermute | solution.py:48
  403.4 13.3 %collective-permute-start.20 = (f32[2,80,768]{2,1,0:T(8,128)S(1)}, f32[2,80,768]{2,1,0:T(8,128)S(1)}, u32[]{:S(2)}, u32[]{:S(2)}) collective-permute-start(f32[2,80,768]{2,1,0:T(8,128)S(1)} %slice.245), channel_id=1, source_target_pairs={{0,4},{2,6},{4,0},{6,2},{8,12},{10,14},{12,8},{14,10},{16,20},{18,... | collective-permute-start | bytes 1474568 | tf_op jit(solution)/shard_map/ppermute | solution.py:48
  437.7 564.1 %reduce-scatter.3.cloned.1.call-start = ((), (), s32[]{:S(2)}) async-start(), calls=%async_computation.5 | async-start | bytes 19464192 | tf_op jit(solution)/shard_map/reduce_scatter | solution.py:689
  525.1 90.8 %collective-permute-start.23 = (f32[4,48,3840]{2,1,0:T(8,128)}, f32[4,48,3840]{2,1,0:T(8,128)}, u32[]{:S(2)}, u32[]{:S(2)}) collective-permute-start(f32[4,48,3840]{2,1,0:T(8,128)} %get-tuple-element.146), channel_id=1, source_target_pairs={{0,8},{2,10},{4,12},{6,14},{1,9},{3,11},{5,13},{7,15}} | collective-permute-start | bytes 8847368 | tf_op jit(solution)/shard_map/ppermute | solution.py:131
  536.1 91.1 %collective-permute-start.26 = (f32[4,48,3840]{2,1,0:T(8,128)}, f32[4,48,3840]{2,1,0:T(8,128)}, u32[]{:S(2)}, u32[]{:S(2)}) collective-permute-start(f32[4,48,3840]{2,1,0:T(8,128)} %get-tuple-element.147), channel_id=1, source_target_pairs={{24,16},{26,18},{28,20},{30,22},{25,17},{27,19},{29,21},{31,23}} | collective-permute-start | bytes 8847368 | tf_op jit(solution)/shard_map/ppermute | solution.py:132
  621.0 100.2 %collective-permute-start.24 = (f32[4,48,3840]{2,1,0:T(8,128)}, f32[4,48,3840]{2,1,0:T(8,128)}, u32[]{:S(2)}, u32[]{:S(2)}) collective-permute-start(f32[4,48,3840]{2,1,0:T(8,128)} %bitcast_add_fusion.2), channel_id=1, source_target_pairs={{0,8},{2,10},{4,12},{6,14},{8,16},{10,18},{12,20},{14,22},{1,9},{3... | collective-permute-start | bytes 8847368 | tf_op jit(solution)/shard_map/ppermute | solution.py:131
  729.0 107.2 %collective-permute-start.27 = (f32[4,48,3840]{2,1,0:T(8,128)}, f32[4,48,3840]{2,1,0:T(8,128)}, u32[]{:S(2)}, u32[]{:S(2)}) collective-permute-start(f32[4,48,3840]{2,1,0:T(8,128)} %get-tuple-element.145), channel_id=1, source_target_pairs={{16,8},{18,10},{20,12},{22,14},{24,16},{26,18},{28,20},{30,22},{17... | collective-permute-start | bytes 8847368 | tf_op jit(solution)/shard_map/ppermute | solution.py:132
  741.0 84.3 %collective-permute-start.38 = (f32[3840]{0:T(1024)S(1)}, f32[3840]{0:T(1024)S(1)}, u32[]{:S(2)}, u32[]{:S(2)}) collective-permute-start(f32[3840]{0:T(1024)S(1)} %add.843), channel_id=1, source_target_pairs={{0,16},{2,18},{4,20},{6,22},{8,24},{10,26},{12,28},{14,30},{16,0},... | collective-permute-start | bytes 46088 | tf_op jit(solution)/shard_map/ppermute | solution.py:48
  825.3 32.4 %collective-permute-start.39 = (f32[3840]{0:T(1024)S(1)}, f32[3840]{0:T(1024)S(1)}, u32[]{:S(2)}, u32[]{:S(2)}) collective-permute-start(f32[3840]{0:T(1024)S(1)} %add.844), channel_id=1, source_target_pairs={{0,2},{2,0},{4,6},{6,4},{8,10},{10,8},{12,14},{14,12},{16,18},{18,... | collective-permute-start | bytes 46088 | tf_op jit(solution)/shard_map/ppermute | solution.py:48
  832.7 88.5 %collective-permute-start.25 = (f32[4,48,3840]{2,1,0:T(8,128)}, f32[4,48,3840]{2,1,0:T(8,128)}, u32[]{:S(2)}, u32[]{:S(2)}) collective-permute-start(f32[4,48,3840]{2,1,0:T(8,128)} %get-tuple-element.144), channel_id=1, source_target_pairs={{0,8},{2,10},{4,12},{6,14},{8,16},{10,18},{12,20},{14,22},{16,24},... | collective-permute-start | bytes 8847368 | tf_op jit(solution)/shard_map/ppermute | solution.py:131
  840.8 80.4 %collective-permute-start.28 = (f32[4,48,3840]{2,1,0:T(8,128)}, f32[4,48,3840]{2,1,0:T(8,128)}, u32[]{:S(2)}, u32[]{:S(2)}) collective-permute-start(f32[4,48,3840]{2,1,0:T(8,128)} %bitcast_add_fusion.1), channel_id=1, source_target_pairs={{8,0},{10,2},{12,4},{14,6},{16,8},{18,10},{20,12},{22,14},{24,16},... | collective-permute-start | bytes 8847368 | tf_op jit(solution)/shard_map/ppermute | solution.py:132
  850.1 71.1 %all-to-all-start.2 = ((bf16[16,1,48,512]{3,2,1,0:T(8,128)(2,1)}), bf16[16,1,48,512]{3,2,1,0:T(8,128)(2,1)}, u32[]{:S(2)}, u32[]{:S(2)}) async-start(bf16[16,1,48,512]{3,2,1,0:T(8,128)(2,1)} %bitcast.330), calls=%async_computation.2 | async-start | bytes 1572864 | tf_op jit(solution)/shard_map/all_to_all | solution.py:694
  869.7 50.7 %collective-permute-start.35 = (f32[10752]{0:T(1024)S(1)}, f32[10752]{0:T(1024)S(1)}, u32[]{:S(2)}, u32[]{:S(2)}) collective-permute-start(f32[10752]{0:T(1024)S(1)} %add.835), channel_id=1, source_target_pairs={{0,8},{2,10},{4,12},{6,14},{8,0},{10,2},{12,4},{14,6},{16,24},{18,... | collective-permute-start | bytes 129032 | tf_op jit(solution)/shard_map/ppermute | solution.py:48
  925.4 19.4 %collective-permute-start.29 = (f32[48,3840]{1,0:T(8,128)S(1)}, f32[48,3840]{1,0:T(8,128)S(1)}, u32[]{:S(2)}, u32[]{:S(2)}) collective-permute-start(f32[48,3840]{1,0:T(8,128)S(1)} %get-tuple-element.157), channel_id=1, source_target_pairs={{0,2},{2,0},{4,6},{6,4},{8,10},{10,8},{12,14},{14,12},{16,18},{18,... | collective-permute-start | bytes 2211848 | tf_op jit(solution)/shard_map/ppermute | solution.py:82
  930.6 34.5 %collective-permute-start.30 = (f32[48,3840]{1,0:T(8,128)S(1)}, f32[48,3840]{1,0:T(8,128)S(1)}, u32[]{:S(2)}, u32[]{:S(2)}) collective-permute-start(f32[48,3840]{1,0:T(8,128)S(1)} %get-tuple-element.156), channel_id=1, source_target_pairs={{0,4},{2,6},{4,0},{6,2},{8,12},{10,14},{12,8},{14,10},{16,20},{18,... | collective-permute-start | bytes 2211848 | tf_op jit(solution)/shard_map/ppermute | solution.py:82
  931.9 33.2 %collective-permute-start.31 = (f32[48,3840]{1,0:T(8,128)S(1)}, f32[48,3840]{1,0:T(8,128)S(1)}, u32[]{:S(2)}, u32[]{:S(2)}) collective-permute-start(f32[48,3840]{1,0:T(8,128)S(1)} %get-tuple-element.155), channel_id=1, source_target_pairs={{0,6},{2,4},{4,2},{6,0},{8,14},{10,12},{12,10},{14,8},{16,22},{18,... | collective-permute-start | bytes 2211848 | tf_op jit(solution)/shard_map/ppermute | solution.py:82
  (181 other events, 5319.2 us)
Sparse Core Ops, SparseCore 0:
  16.6 157.1 all-gather.2
  437.8 150.3 reduce-scatter.4
  595.8 262.2 reduce-scatter.2

commit v2 on v1

v2 whole, which is shorter than its diff:
```python
import functools
import math

import jax
import jax.numpy as jnp
from jax import lax
from jax.experimental import pallas as pl
from jax.experimental.pallas import tpu as pltpu
from jax.sharding import PartitionSpec as P

HEAD_DIM = 64
STEP = 10


NORM_EPS = 1e-05
CLIP = 0.005
PRUNE_DECAY = 0.0002
BETA_ONE = 0.9
BETA_TWO = 0.999
ADAM_EPS = 1e-08
WEIGHT_DECAY = 0.01
RATE_MATRIX = 0.1
RATE_VECTOR = 1.0
SCORE_SCALE = 0.125


HIGH_COUNT = 512
BOTH = ("fsdp", "vocab")


def kept(words):
    columns = words.shape[1] * 16
    place = lax.broadcasted_iota(jnp.int32, (2 * words.shape[1], columns), 0)
    column = lax.broadcasted_iota(jnp.int32, (2 * words.shape[1], columns), 1)
    spread = (place % words.shape[1] * 2 + place // words.shape[1] == column // 8).astype(
        jnp.bfloat16
    )
    bytes_low = jnp.concatenate([words & 255, words >> 8], 1).astype(jnp.bfloat16)
    byte = jnp.dot(bytes_low, spread, preferred_element_type=jnp.float32).astype(jnp.int32)
    spot = lax.broadcasted_iota(jnp.int32, byte.shape, 1)
    nibble = jnp.where(spot % 8 < 4, byte & 15, byte >> 4)
    spot = spot % 4
    return ((nibble & 3) == spot) | ((nibble >> 2) == spot)


def swap(x, axis, bit):
    size = lax.axis_size(axis)
    return lax.ppermute(x, axis, [(i, i ^ bit) for i in range(size)])


def my_bit(axis, bit):
    return lax.axis_index(axis) // bit % 2


def bits_of(size):
    return [1 << k for k in range(size.bit_length() - 1)]


def after(x, *needed):
    if not needed:
        return x
    return lax.optimization_barrier((x, needed))[0]


def tree_sum(parts):
    while len(parts) > 1:
        parts = [one + two for one, two in zip(parts[::2], parts[1::2])]
    return parts[0]


def sum_all(x, near):
    x = x + swap(x, "vocab", 1)
    x = tree_sum(near_exchange(lambda q: x, near))
    return sum_far(x, near)


def sum_far(x, near):
    far = lax.axis_size("fsdp") // near
    if far == 4:
        return tree_sum([x] + [swap(x, "fsdp", k * near) for k in range(1, far)])
    for bit in bits_of(far):
        x = x + swap(x, "fsdp", bit * near)
    return x


def join(x, axis, bit):
    other = swap(x, axis, bit)
    upper = my_bit(axis, bit) == 1
    return jnp.stack([jnp.where(upper, other, x), jnp.where(upper, x, other)])


def halve(x, axis, bit):
    mine = my_bit(axis, bit)
    return lax.dynamic_index_in_dim(x, mine, 0, False) + swap(
        lax.dynamic_index_in_dim(x, 1 - mine, 0, False), axis, bit
    )


def near_exchange(take, near):
    size = lax.axis_size("fsdp")
    p = lax.axis_index("fsdp") % near
    return [take(p)] + [
        lax.ppermute(take(p ^ k), "fsdp", [(i, i ^ k) for i in range(size)]) for k in range(1, near)
    ]


def far_groups(near):
    size = lax.axis_size("fsdp")
    return [list(range(q, size, near)) for q in range(near)]


def near_groups(near):
    size = lax.axis_size("fsdp")
    return [list(range(start, start + near)) for start in range(0, size, near)]


def exchange(x, groups):
    return lax.all_to_all(x, "fsdp", 0, 0, tiled=True, axis_index_groups=groups)


def in_rows(parts, near):
    p = lax.axis_index("fsdp") % near
    rows = parts[0].shape[0]
    stacked = jnp.zeros((near * rows,) + parts[0].shape[1:], parts[0].dtype)
    for k, part in enumerate(parts):
        stacked = lax.dynamic_update_slice_in_dim(stacked, part, (p ^ k) * rows, 0)
    return stacked


def far_gather(x, near):
    return lax.all_gather(x, "fsdp", axis=0, tiled=True, axis_index_groups=far_groups(near))


class FarLine:
    def __init__(self, x, near):
        self.x, self.near = x, near
        self.far = 4
        self.z = lax.axis_index("fsdp") // near
        self.k = 0
        self.up = self.down = None

    def entry(self, j):
        return lax.dynamic_index_in_dim(self.x, jnp.clip(j, 0, self.far - 1), 0, False)

    def step(self, *needed):
        self.k += 1
        k, near, size = self.k, self.near, self.far * self.near
        send_up = self.entry(self.far - k + self.z)
        send_down = self.entry(self.z - self.far + k)
        if k > 1:
            up, down = after([self.up, self.down], *needed)
            send_up, send_down = send_up + up, send_down + down
        sends = [send_up.astype(jnp.bfloat16), send_down.astype(jnp.bfloat16)]
        self.up = lax.ppermute(sends[0], "fsdp", [(i, i + near) for i in range(k * near)])
        self.down = lax.ppermute(
            sends[1], "fsdp", [(i, i - near) for i in range(size - k * near, size)]
        )
        return sends

    def total(self, *needed):
        up, down = after([self.up, self.down], *needed)
        return self.entry(self.z) + up + down


def far_sends(x, near):
    far = lax.axis_size("fsdp") // near
    z = lax.axis_index("fsdp") // near
    sends = [
        lax.dynamic_index_in_dim(x, z ^ k, 0, False).astype(jnp.bfloat16) for k in range(1, far)
    ]
    return lax.dynamic_index_in_dim(x, z, 0, False), sends


def far_arrive(sends, near):
    return [swap(send, "fsdp", k * near) for k, send in enumerate(sends, 1)]


def added(own, parts):
    for part in parts:
        own = own + part.astype(jnp.float32)
    return own


def far_reduce(x, near):
    return lax.psum_scatter(
        x, "fsdp", scatter_dimension=0, tiled=True, axis_index_groups=far_groups(near)
    )[0]


def begin_pair_sum(grad, rows, near):
    core = lax.axis_index("vocab")
    grad = grad.reshape(-1, near, 2, rows, grad.shape[-1])
    send = lax.dynamic_index_in_dim(grad, 1 - core, 2, False).astype(jnp.bfloat16)
    return (lax.dynamic_index_in_dim(grad, core, 2, False), [send])


def in_order(parts, near):
    p = lax.axis_index("fsdp") % near
    stacked = []
    for q in range(near):
        entry = parts[0]
        for k in range(1, near):
            entry = jnp.where(p ^ k == q, parts[k], entry)
        stacked.append(entry)
    return jnp.stack(stacked)


def place_kernel(spans, blocks, order_ref, *refs):
    count = len(refs) - len(spans) - 1
    pieces, outs, sems = refs[:count], refs[count:-1], refs[-1]
    for i, piece in enumerate(pieces):
        for kz in range(blocks):
            n = i * blocks + kz
            block = order_ref[n]
            for m, (first, last, start, rows) in enumerate(spans):

                def copy(m=m, kz=kz, n=n, first=first, start=start, rows=rows, piece=piece):
                    pltpu.make_async_copy(
                        piece.at[kz, pl.ds(start, rows)], outs[m].at[block - first], sems.at[n, m]
                    ).start()

                pl.when((block >= first) & (block < last))(copy)
    for i, piece in enumerate(pieces):
        for kz in range(blocks):
            n = i * blocks + kz
            block = order_ref[n]
            for m, (first, last, start, rows) in enumerate(spans):

                def wait(m=m, kz=kz, n=n, first=first, start=start, rows=rows, piece=piece):
                    pltpu.make_async_copy(
                        piece.at[kz, pl.ds(start, rows)], outs[m].at[block - first], sems.at[n, m]
                    ).wait()

                pl.when((block >= first) & (block < last))(wait)


def gather_pieces(line):
    half = line.shape[0] // 2
    one, two = line[:half], line[half:]
    one_x, two_y = swap(one, "fsdp", 1), swap(two, "fsdp", 2)
    one_y, two_x = swap(one, "fsdp", 2), swap(two, "fsdp", 1)
    one_xy, two_xy = swap(one_x, "fsdp", 2), swap(two_y, "fsdp", 1)
    return [[one, one_x, one_y, one_xy], [two, two_x, two_y, two_xy]]


def place_blocks(pieces, order, spans):
    total, width = len(order), pieces[0].shape[-1]
    return pl.pallas_call(
        functools.partial(place_kernel, spans, pieces[0].shape[0]),
        grid_spec=pltpu.PrefetchScalarGridSpec(
            num_scalar_prefetch=1,
            grid=(1,),
            in_specs=[pl.BlockSpec(memory_space=pltpu.VMEM)] * len(pieces),
            out_specs=[pl.BlockSpec(memory_space=pl.ANY)] * len(spans),
            scratch_shapes=[pltpu.SemaphoreType.DMA((total, len(spans)))],
        ),
        out_shape=[
            jax.ShapeDtypeStruct((last - first, rows, width), pieces[0].dtype)
            for first, last, _, rows in spans
        ],
        compiler_params=pltpu.CompilerParams(vmem_limit_bytes=40 * 1024 * 1024),
        name="place",
    )(jnp.stack(order).astype(jnp.int32), *pieces)


def lookup_kernel(low_count, ids_ref, table_ref, out_ref, spread):
    width = table_ref.shape[0]

    @pl.when(pl.program_id(0) == 0)
    def _():
        for low in range(low_count):
            spread[low * width : (low + 1) * width, :] = table_ref[
                :, low * HIGH_COUNT : (low + 1) * HIGH_COUNT
            ].astype(jnp.bfloat16)

    ids = ids_ref[0]
    low_ids = ids >> 9
    row = lax.broadcasted_iota(jnp.int32, (HIGH_COUNT, ids.shape[1]), 0)
    match = (row == (ids & (HIGH_COUNT - 1))).astype(jnp.bfloat16)
    found = jnp.dot(spread[...], match, preferred_element_type=jnp.float32)
    total = jnp.zeros((width, ids.shape[1]), jnp.float32)
    for low in range(low_count):
        total = jnp.where(low_ids == low, found[low * width : (low + 1) * width, :], total)
    out_ref[0] = total.astype(out_ref.dtype)


def lookup(table_t, ids):
    rows = table_t.shape[0]
    table_t = jnp.pad(table_t, ((0, -rows % 16), (0, 0)))
    width, vocab = table_t.shape
    blocks, _, length = ids.shape
    low_count = vocab // HIGH_COUNT
    found = pl.pallas_call(
        functools.partial(lookup_kernel, low_count),
        grid=(blocks,),
        in_specs=[
            pl.BlockSpec((1, 1, length), lambda i: (i, 0, 0)),
            pl.BlockSpec((width, vocab), lambda i: (0, 0)),
        ],
        out_specs=pl.BlockSpec((1, width, length), lambda i: (i, 0, 0)),
        out_shape=jax.ShapeDtypeStruct((blocks, width, length), jnp.bfloat16),
        scratch_shapes=[pltpu.VMEM((low_count * width, HIGH_COUNT), jnp.bfloat16)],
        compiler_params=pltpu.CompilerParams(vmem_limit_bytes=40 * 1024 * 1024),
        cost_estimate=pl.CostEstimate(
            flops=2 * blocks * length * width * vocab,
            bytes_accessed=4 * width * vocab + 2 * blocks * width * length,
            transcendentals=0,
        ),
        name="lookup",
    )(ids, table_t)
    return found[:, :rows]


def spread_kernel(low_count, ids_ref, grad_ref, out_ref, lhs, total):
    width = grad_ref.shape[1]
    step = pl.program_id(0)

    @pl.when(step == 0)
    def _():
        total[...] = jnp.zeros_like(total)

    ids = ids_ref[0]
    low_ids = ids >> 9
    grad = grad_ref[0].astype(jnp.float32)
    for low in range(low_count):
        lhs[low * width : (low + 1) * width, :] = jnp.where(low_ids == low, grad, 0.0).astype(
            jnp.bfloat16
        )
    row = lax.broadcasted_iota(jnp.int32, (HIGH_COUNT, ids.shape[1]), 0)
    match = (row == (ids & (HIGH_COUNT - 1))).astype(jnp.bfloat16)
    total[...] += lax.dot_general(
        lhs[...], match, (((1,), (1,)), ((), ())), preferred_element_type=jnp.float32
    )

    @pl.when(step == pl.num_programs(0) - 1)
    def _():
        for low in range(low_count):
            span = slice(low * HIGH_COUNT, (low + 1) * HIGH_COUNT)
            out_ref[:, span] = total[low * width : (low + 1) * width, :]


def spread_add(grads, ids, vocab):
    rows = grads.shape[1]
    grads = jnp.pad(grads, ((0, 0), (0, -rows % 16), (0, 0)))
    width = grads.shape[1]
    blocks, _, length = ids.shape
    low_count = vocab // HIGH_COUNT
    summed = pl.pallas_call(
        functools.partial(spread_kernel, low_count),
        grid=(blocks,),
        in_specs=[
            pl.BlockSpec((1, 1, length), lambda i: (i, 0, 0)),
            pl.BlockSpec((1, width, length), lambda i: (i, 0, 0)),
        ],
        out_specs=pl.BlockSpec((width, vocab), lambda i: (0, 0)),
        out_shape=jax.ShapeDtypeStruct((width, vocab), jnp.float32),
        scratch_shapes=[
            pltpu.VMEM((low_count * width, length), jnp.bfloat16),
            pltpu.VMEM((low_count * width, HIGH_COUNT), jnp.float32),
        ],
        compiler_params=pltpu.CompilerParams(vmem_limit_bytes=40 * 1024 * 1024),
        cost_estimate=pl.CostEstimate(
            flops=2 * blocks * length * width * vocab,
            bytes_accessed=4 * width * vocab + 2 * blocks * width * length,
            transcendentals=0,
        ),
        name="spread_add",
    )(ids, grads)
    return summed[:rows]


def split_vectors(vectors_all, width):
    hidden_units = vectors_all.shape[0] - 10 * width
    pieces = []
    offset = 0
    for piece_len in [width] * 9 + [hidden_units, width]:
        pieces.append(vectors_all[offset : offset + piece_len])
        offset = offset + piece_len
    return pieces


def layer_norm(input_batch, gain, shift):
    center = input_batch - jnp.mean(input_batch, axis=-1, keepdims=True)
    spread = jnp.mean(center * center, axis=-1, keepdims=True)
    return center * lax.rsqrt(spread + NORM_EPS) * gain + shift


def norm_back(input_batch, gain, shift, gradient_tree):
    unused, pull = jax.vjp(layer_norm, input_batch, gain, shift)
    return pull(gradient_tree)


def project(input_batch, weight_matrix):
    return jnp.einsum("mh,ph->mp", input_batch, weight_matrix, preferred_element_type=jnp.float32)


def project_back(gradient, weight_matrix):
    return jnp.einsum("az,zh->ah", gradient, weight_matrix, preferred_element_type=jnp.float32)


def weight_grad(gradient, input_batch):
    return jnp.einsum("bu,bw->uw", gradient, input_batch, preferred_element_type=jnp.float32)


def column_sum(gradient):
    return jnp.sum(gradient.astype(jnp.float32), axis=0)


def scores_of(query, key_rows, live):
    raw = lax.dot_general(
        query * SCORE_SCALE, key_rows, (((1,), (1,)), ((), ())), preferred_element_type=jnp.float32
    )
    scores = jnp.where(live, raw, -1e30)
    powers = jnp.exp(scores - jnp.max(scores, axis=-1, keepdims=True))
    return powers * (1.0 / jnp.sum(powers, axis=-1, keepdims=True))


def attend_kernel(lengths_ref, query_ref, key_ref, value_ref, out_ref):
    length = lengths_ref[pl.program_id(0)]
    live = lax.broadcasted_iota(jnp.int32, (1, key_ref.shape[0]), 1) < length
    for start in range(0, query_ref.shape[1], HEAD_DIM):
        span = slice(start, start + HEAD_DIM)
        prob = scores_of(query_ref[:, span], key_ref[:, span], live).astype(jnp.bfloat16)
        context = jnp.dot(prob, value_ref[:, span], preferred_element_type=jnp.float32)
        out_ref[:, span] = context.astype(out_ref.dtype)


def attend(qkv, lengths, seqs):
    rows, total = qkv.shape
    seq_len, width = rows // seqs, total // 3
    lanes = 2 * HEAD_DIM
    blocks = width // lanes

    def part(which):
        return pl.BlockSpec((seq_len, lanes), lambda s, j, _: (s, which * blocks + j))

    return pl.pallas_call(
        attend_kernel,
        grid_spec=pltpu.PrefetchScalarGridSpec(
            num_scalar_prefetch=1,
            grid=(seqs, blocks),
            in_specs=[part(0), part(1), part(2)],
            out_specs=pl.BlockSpec((seq_len, lanes), lambda s, j, _: (s, j)),
        ),
        out_shape=jax.ShapeDtypeStruct((rows, width), jnp.bfloat16),
        compiler_params=pltpu.CompilerParams(vmem_limit_bytes=40 * 1024 * 1024),
        cost_estimate=pl.CostEstimate(
            flops=4 * rows * seq_len * width,
            bytes_accessed=2 * rows * (total + width),
            transcendentals=rows * seq_len * width // HEAD_DIM,
        ),
        name="attend",
    )(lengths, qkv, qkv, qkv)


def attend_back_kernel(lengths_ref, query_ref, key_ref, value_ref, grad_ref, out_ref):
    length = lengths_ref[pl.program_id(0)]
    step = pl.program_id(1)
    width = out_ref.shape[1] // 3
    live = lax.broadcasted_iota(jnp.int32, (1, key_ref.shape[0]), 1) < length
    parts = [[], [], []]
    for start in range(0, query_ref.shape[1], HEAD_DIM):
        span = slice(start, start + HEAD_DIM)
        query, key_rows, value_rows = query_ref[:, span], key_ref[:, span], value_ref[:, span]
        grad_out = grad_ref[:, span]
        prob = scores_of(query, key_rows, live)
        grad_prob = lax.dot_general(
            grad_out, value_rows, (((1,), (1,)), ((), ())), preferred_element_type=jnp.float32
        )
        grad_value = lax.dot_general(
            prob.astype(jnp.bfloat16),
            grad_out,
            (((0,), (0,)), ((), ())),
            preferred_element_type=jnp.float32,
        )
        mean = jnp.sum(prob * grad_prob, axis=-1, keepdims=True)
        grad_score = (prob * (grad_prob - mean)).astype(jnp.bfloat16)
        grad_query = jnp.dot(grad_score, key_rows, preferred_element_type=jnp.float32)
        grad_key = lax.dot_general(
            grad_score, query, (((0,), (0,)), ((), ())), preferred_element_type=jnp.float32
        )
        parts[0].append(grad_query * SCORE_SCALE)
        parts[1].append(grad_key * SCORE_SCALE)
        parts[2].append(grad_value)
    lanes = query_ref.shape[1]
    for which, pieces in enumerate(parts):
        start = pl.multiple_of(which * width + step * lanes, lanes)
        out_ref[:, pl.ds(start, lanes)] = jnp.concatenate(pieces, 1).astype(out_ref.dtype)


def attend_back(qkv, grad_context, lengths, seqs):
    rows, total = qkv.shape
    seq_len, width = rows // seqs, total // 3
    lanes = 2 * HEAD_DIM
    blocks = width // lanes

    def part(which):
        return pl.BlockSpec((seq_len, lanes), lambda s, j, _: (s, which * blocks + j))

    return pl.pallas_call(
        attend_back_kernel,
        grid_spec=pltpu.PrefetchScalarGridSpec(
            num_scalar_prefetch=1,
            grid=(seqs, blocks),
            in_specs=[part(0), part(1), part(2), part(0)],
            out_specs=pl.BlockSpec((seq_len, total), lambda s, j, _: (s, 0)),
        ),
        out_shape=jax.ShapeDtypeStruct((rows, total), jnp.bfloat16),
        compiler_params=pltpu.CompilerParams(vmem_limit_bytes=40 * 1024 * 1024),
        cost_estimate=pl.CostEstimate(
            flops=10 * rows * seq_len * width,
            bytes_accessed=2 * rows * (2 * total + width),
            transcendentals=rows * seq_len * width // HEAD_DIM,
        ),
        name="attend_back",
    )(lengths, qkv, qkv, qkv, grad_context)


def head_kernel(rows_ref, table_ref, bias_ref, teach_ref, logits_ref, stats_ref):
    logits = (
        jnp.dot(rows_ref[...], table_ref[...], preferred_element_type=jnp.float32) + bias_ref[...]
    )
    logits_ref[...] = logits
    teach = teach_ref[...].astype(jnp.float32)
    student_top = jnp.max(logits, axis=-1, keepdims=True)
    student_total = jnp.sum(jnp.exp(logits - student_top), axis=-1, keepdims=True)
    teacher_top = jnp.max(teach, axis=-1, keepdims=True)
    weighted = jnp.exp(teach - teacher_top)
    teacher_total = jnp.sum(weighted, axis=-1, keepdims=True)
    cross = jnp.sum(weighted * (teach - logits), axis=-1, keepdims=True)
    lane = lax.broadcasted_iota(jnp.int32, (logits.shape[0], 128), 1)
    packed = jnp.zeros((logits.shape[0], 128), jnp.float32)
    for i, stat in enumerate((student_top, student_total, teacher_top, teacher_total, cross)):
        packed = jnp.where(lane == i, stat, packed)
    stats_ref[0] = packed.T[:8]


def head(rows, table_part, bias_part, teach, near):
    count, width = rows.shape
    vocab = table_part.shape[1]
    block = count // near
    return pl.pallas_call(
        head_kernel,
        grid=(near,),
        in_specs=[
            pl.BlockSpec((block, width), lambda i: (i, 0)),
            pl.BlockSpec((width, vocab), lambda i: (0, 0)),
            pl.BlockSpec((1, vocab), lambda i: (0, 0)),
            pl.BlockSpec((block, vocab), lambda i: (i, 0)),
        ],
        out_specs=[
            pl.BlockSpec((block, vocab), lambda i: (i, 0)),
            pl.BlockSpec((1, 8, block), lambda i: (i, 0, 0)),
        ],
        out_shape=[
            jax.ShapeDtypeStruct((count, vocab), jnp.float32),
            jax.ShapeDtypeStruct((near, 8, block), jnp.float32),
        ],
        compiler_params=pltpu.CompilerParams(vmem_limit_bytes=48 * 1024 * 1024),
        cost_estimate=pl.CostEstimate(
            flops=2 * count * width * vocab,
            bytes_accessed=count * vocab * 6 + 2 * width * vocab,
            transcendentals=2 * count * vocab,
        ),
        name="head",
    )(rows, table_part, bias_part, teach)


def head_back_kernel(
    logits_ref, teach_ref, stats_ref, scale_ref, table_ref, grad_ref, rows_ref, bias_ref, loss_ref
):
    step = pl.program_id(0)
    stats = stats_ref[:, 0]
    tops, totals, teacher_tops, teacher_totals, crosses = (stats[:, i] for i in range(5))
    top = jnp.max(tops, axis=0, keepdims=True)
    total = jnp.sum(totals * jnp.exp(tops - top), axis=0, keepdims=True)
    teacher_top = jnp.max(teacher_tops, axis=0, keepdims=True)
    teacher_scale = jnp.exp(teacher_tops - teacher_top)
    teacher_total = jnp.sum(teacher_totals * teacher_scale, axis=0, keepdims=True)
    cross = jnp.sum(crosses * teacher_scale, axis=0, keepdims=True)
    student_lse = top + jnp.log(total)
    teacher_lse = teacher_top + jnp.log(teacher_total)
    loss_ref[0] = cross / teacher_total - teacher_lse + student_lse
    packed = jnp.concatenate(
        [student_lse, teacher_lse, scale_ref[0], jnp.zeros((5, top.shape[1]), jnp.float32)], 0
    ).T
    grad = (
        (
            jnp.exp(logits_ref[...] - packed[:, 0:1])
            - jnp.exp(teach_ref[...].astype(jnp.float32) - packed[:, 1:2])
        )
        * packed[:, 2:3]
    ).astype(jnp.bfloat16)
    grad_ref[...] = grad
    rows_ref[...] = lax.dot_general(
        grad, table_ref[...], (((1,), (1,)), ((), ())), preferred_element_type=jnp.float32
    )

    @pl.when(step == 0)
    def _():
        bias_ref[...] = jnp.zeros_like(bias_ref)

    bias_ref[...] += jnp.sum(grad.astype(jnp.float32), axis=0, keepdims=True)


def head_back(logits, teach, stats, scale, table_part, near):
    count, vocab = logits.shape
    width = table_part.shape[0]
    block = count // near
    members = stats.shape[0]
    return pl.pallas_call(
        head_back_kernel,
        grid=(near,),
        in_specs=[
            pl.BlockSpec((block, vocab), lambda i: (i, 0)),
            pl.BlockSpec((block, vocab), lambda i: (i, 0)),
            pl.BlockSpec((members, 1, 8, block), lambda i: (0, i, 0, 0)),
            pl.BlockSpec((1, 1, block), lambda i: (i, 0, 0)),
            pl.BlockSpec((width, vocab), lambda i: (0, 0)),
        ],
        out_specs=[
            pl.BlockSpec((block, vocab), lambda i: (i, 0)),
            pl.BlockSpec((block, width), lambda i: (i, 0)),
            pl.BlockSpec((1, vocab), lambda i: (0, 0)),
            pl.BlockSpec((1, 1, block), lambda i: (i, 0, 0)),
        ],
        out_shape=[
            jax.ShapeDtypeStruct((count, vocab), jnp.bfloat16),
            jax.ShapeDtypeStruct((count, width), jnp.float32),
            jax.ShapeDtypeStruct((1, vocab), jnp.float32),
            jax.ShapeDtypeStruct((near, 1, block), jnp.float32),
        ],
        compiler_params=pltpu.CompilerParams(vmem_limit_bytes=48 * 1024 * 1024),
        cost_estimate=pl.CostEstimate(
            flops=2 * count * width * vocab,
            bytes_accessed=count * vocab * 8 + 2 * width * vocab,
            transcendentals=2 * count * vocab,
        ),
        name="head_back",
    )(logits, teach, stats, scale, table_part)


def layer_forward(
    embedded, lengths, seqs, weight_qkv, weight_out, weight_up, weight_down_after, parts
):
    (
        gain_embed,
        shift_embed,
        gain_attn,
        shift_attn,
        gain_ffn,
        shift_ffn,
        bias_query,
        bias_value,
        bias_out,
        bias_hidden,
        bias_down,
    ) = parts
    normed = layer_norm(embedded, gain_embed, shift_embed)
    normed_low = normed.astype(jnp.bfloat16)
    qkv_bias = jnp.concatenate([bias_query, jnp.zeros_like(bias_query), bias_value])
    qkv_low = (project(normed_low, weight_qkv) + qkv_bias).astype(jnp.bfloat16)
    context_low = attend(qkv_low, lengths, seqs)
    first_sum = normed + project(context_low, weight_out) + bias_out
    first_out = layer_norm(first_sum, gain_attn, shift_attn)
    first_low = first_out.astype(jnp.bfloat16)
    pre_act = project(first_low, weight_up) + bias_hidden
    share = 0.5 + 0.5 * lax.erf(pre_act * math.sqrt(0.5))
    act_low = (pre_act * share).astype(jnp.bfloat16)
    weight_down = weight_down_after(first_low)
    slope = share + pre_act * jnp.exp(-0.5 * pre_act * pre_act) * (1.0 / math.sqrt(2.0 * math.pi))
    second_sum = first_out + project(act_low, weight_down) + bias_down
    final = layer_norm(second_sum, gain_ffn, shift_ffn)
    saved = (
        embedded,
        normed_low,
        qkv_low,
        context_low,
        first_sum,
        first_low,
        slope,
        act_low,
        second_sum,
    )
    return (final, saved, weight_down)


def layer_backward(
    grad_final,
    saved,
    lengths,
    seqs,
    weight_qkv,
    weight_out,
    weight_up,
    weight_down,
    parts,
    sums,
    line,
    embed_columns,
    stack_rows,
    down_rows,
):
    (
        gain_embed,
        shift_embed,
        gain_attn,
        shift_attn,
        gain_ffn,
        shift_ffn,
        bias_query,
        bias_value,
        bias_out,
        bias_hidden,
        bias_down,
    ) = parts
    (
        embedded,
        normed_low,
        qkv_low,
        context_low,
        first_sum,
        first_low,
        slope,
        act_low,
        second_sum,
    ) = saved
    width = embedded.shape[1]
    grad_second, grad_gain_ffn, grad_shift_ffn = norm_back(
        second_sum, gain_ffn, shift_ffn, grad_final
    )
    grad_down_low = grad_second.astype(jnp.bfloat16)
    sums.begin("down", weight_grad(grad_down_low, act_low), down_rows)
    grad_pre_low = (
        project_back(after(grad_down_low, *sums.sent("down")), weight_down) * slope
    ).astype(jnp.bfloat16)
    grad_pre_low = lax.optimization_barrier(grad_pre_low)
    sums.begin("up", weight_grad(grad_pre_low, first_low), stack_rows)
    grad_first = grad_second + project_back(after(grad_pre_low, *sums.sent("up")), weight_up)
    grad_first_sum, grad_gain_attn, grad_shift_attn = norm_back(
        first_sum, gain_attn, shift_attn, grad_first
    )
    grad_out_low = grad_first_sum.astype(jnp.bfloat16)
    grad_context_low = project_back(grad_out_low, weight_out).astype(jnp.bfloat16)
    out_grad = weight_grad(grad_out_low, context_low)
    sums.in_plane(("down", "up"), grad_context_low)
    line_sends = line.step(grad_context_low) if line else []
    grad_qkv_low = attend_back(
        qkv_low, after(grad_context_low, *sums.sent("up"), *line_sends), lengths, seqs
    )
    grad_normed = grad_first_sum + project_back(grad_qkv_low, weight_qkv)
    grad_embed, grad_gain_embed, grad_shift_embed = norm_back(
        embedded, gain_embed, shift_embed, grad_normed
    )
    embed_t = embed_columns(grad_embed)
    line_sends = line.step(embed_t) if line else []
    qkv_grad = weight_grad(after(grad_qkv_low, embed_t, *line_sends), normed_low)
    sums.begin("attention", jnp.concatenate([qkv_grad, out_grad], 0), stack_rows)
    vectors_grad = jnp.concatenate(
        [
            grad_gain_embed,
            grad_shift_embed,
            grad_gain_attn,
            grad_shift_attn,
            grad_gain_ffn,
            grad_shift_ffn,
            column_sum(grad_qkv_low[:, :width]),
            column_sum(grad_qkv_low[:, 2 * width :]),
            column_sum(grad_out_low),
            column_sum(grad_pre_low),
            column_sum(grad_down_low),
        ]
    )
    return (embed_t, vectors_grad)


class WeightSums:
    def __init__(self, near, far, width):
        self.near, self.staged, self.width = near, far == 4, width
        self.state = {}

    def begin(self, name, grad, rows):
        self.state[name] = begin_pair_sum(grad, rows, self.near) if self.staged else (grad, [])

    def sent(self, name):
        return self.state[name][1] if self.staged else []

    def narrow(self, x):
        parts = [
            x[..., j : j + self.width] for j in range(0, x.shape[-1], self.width)
        ]
        return parts[0] if len(parts) == 1 else jnp.concatenate(parts, -2)

    def in_plane(self, names, *needed):
        if not self.staged:
            return
        p = lax.axis_index("fsdp") % self.near
        owns, sends = [], [[] for _ in range(1, self.near)]
        for name in names:
            keep, pair_sends = self.state[name]
            arrived = after(swap(pair_sends[0], "vocab", 1), *needed)
            keep = keep + arrived.astype(jnp.float32)
            owns.append(self.narrow(lax.dynamic_index_in_dim(keep, p, 1, False)))
            for k in range(1, self.near):
                send = lax.dynamic_index_in_dim(keep, p ^ k, 1, False).astype(jnp.bfloat16)
                sends[k - 1].append(self.narrow(send).reshape(-1, self.width))
        sends = [parts[0] if len(parts) == 1 else jnp.concatenate(parts, 0) for parts in sends]
        for name, own in zip(names, owns):
            self.state[name] = (own, sends)

    def plane_totals(self, names, *needed):
        sends = self.state[names[0]][1]
        arrived = after([swap(send, "fsdp", k) for k, send in enumerate(sends, 1)], *needed)
        totals, start = [], 0
        for name in names:
            own = self.state[name][0]
            count = own.shape[0] * own.shape[1]
            totals.append(
                added(own, [part[start : start + count].reshape(own.shape) for part in arrived])
            )
            start += count
        return totals


def adam(weight_matrix, grad, first, second, rate):
    first = BETA_ONE * first + (1.0 - BETA_ONE) * grad
    second = BETA_TWO * second + (1.0 - BETA_TWO) * grad * grad
    first_hat = first / (1.0 - BETA_ONE**STEP)
    second_hat = second / (1.0 - BETA_TWO**STEP)
    new = weight_matrix - rate * (
        first_hat / (jnp.sqrt(second_hat) + ADAM_EPS) + WEIGHT_DECAY * weight_matrix
    )
    return (first, second, new)


def local(
    token_ids,
    lengths,
    masked_pos,
    teacher,
    stack_index,
    down_index,
    stack_next,
    down_next,
    word_table,
    table_first,
    table_second,
    pos_table,
    pos_first,
    pos_second,
    proj_stack,
    stack_first,
    stack_second,
    ffn_down,
    down_first,
    down_second,
    vectors,
    vectors_first,
    vectors_second,
    head_bias,
    bias_first,
    bias_second_moment,
):
    size = lax.axis_size("fsdp")
    near = math.gcd(4, size)
    far = size // near
    width = proj_stack.shape[1]
    units = ffn_down.shape[1]
    pair_seqs, seq_len = token_ids.shape
    own_seqs = pair_seqs // 2
    own_rows = own_seqs * seq_len
    core = lax.axis_index("vocab")
    place = lax.axis_index("fsdp")
    p = place % near
    vocab_dev, columns = word_table.shape
    part = vocab_dev // near
    mask_slots = masked_pos.shape[1]

    table_t = word_table.T
    all_ids = lax.all_to_all(
        jnp.broadcast_to(token_ids[None], (size, pair_seqs, seq_len)), "fsdp", 0, 0, tiled=True
    ).reshape(size, 2, own_seqs, seq_len)
    local_ids = (
        jnp.concatenate(
            [
                lax.dynamic_index_in_dim(all_ids, core, 1, False),
                lax.dynamic_index_in_dim(all_ids, 1 - core, 1, False),
            ],
            0,
        ).reshape(2 * size * own_seqs, 1, seq_len)
        - core * vocab_dev
    )

    stack_mask = kept(stack_index)
    down_mask = kept(down_index)
    stack_rows = proj_stack.shape[0]
    down_rows = ffn_down.shape[0]
    small_count = vectors.shape[0]
    own_stack = jnp.where(stack_mask, proj_stack, 0.0).astype(jnp.bfloat16)
    own_down = jnp.where(down_mask, ffn_down, 0.0).astype(jnp.bfloat16)
    pos_rows = -(-(columns // 2) // 16) * 16
    own_stack = jnp.concatenate(
        [
            own_stack,
            jnp.pad(
                pos_table.T.astype(jnp.bfloat16),
                ((0, pos_rows - columns // 2), (0, width - seq_len)),
            ),
            jnp.pad(
                vectors.astype(jnp.bfloat16)[None], ((0, 15), (0, width - small_count))
            ),
        ],
        0,
    )
    table_low = table_t.astype(jnp.bfloat16)
    half = size * own_seqs
    table_blocks = table_low.reshape(columns, near, part).transpose(1, 0, 2)
    def teacher_parts(*needed):
        given = after(teacher, *needed)
        return near_exchange(lambda q: lax.dynamic_slice_in_dim(given, q * part, part, 1), near)

    if far == 4:
        own_stack = after(own_stack, all_ids)
        stack_line = [swap(own_stack, "fsdp", k * near) for k in range(1, far)]
        near_table = exchange(after(table_blocks, all_ids), near_groups(near))
        found = lookup(table_t, after(local_ids, own_stack))
        near_table = after(near_table, found).reshape(near * columns, part)
        own_found = found[:half] + swap(found[half:], "vocab", 1)
        stack_line = jnp.stack([own_stack] + after(stack_line, found))
        stack_pieces = gather_pieces(stack_line)
        own_found = after(own_found, stack_line, near_table)
        tokens_t = exchange(own_found.reshape(size, own_seqs, columns, seq_len), None)
        own_down = after(own_down, own_found)
        down_line = exchange(
            after(jnp.broadcast_to(own_down[None], (far,) + own_down.shape), tokens_t),
            far_groups(near),
        )
        stack_others = [[swap(piece, "vocab", 1) for piece in half] for half in stack_pieces]
        own_blocks = exchange(
            after(
                jnp.broadcast_to(down_line[None], (near,) + down_line.shape),
                stack_pieces[0][3],
                stack_pieces[1][3],
            ),
            near_groups(near),
        )
        other_blocks = swap(own_blocks, "vocab", 1)
        teach_parts = teacher_parts(stack_pieces[0][3], stack_pieces[1][3])
        qkv_blocks = 3 * width // stack_rows
        attention_blocks = 4 * width // stack_rows
        weight_qkv, weight_out, weight_up, small = place_blocks(
            [piece for group in (stack_pieces, stack_others) for half in group for piece in half],
            [
                (place ^ ((first + kz) * near + kp)) * 2 + (core ^ kc)
                for kc in range(2)
                for first in (0, far // 2)
                for kp in range(near)
                for kz in range(far // 2)
            ],
            (
                (0, qkv_blocks, 0, stack_rows),
                (qkv_blocks, attention_blocks, 0, stack_rows),
                (attention_blocks, 2 * size, 0, stack_rows),
                (0, 2 * size, stack_rows, pos_rows + 16),
            ),
        )
        weight_qkv = weight_qkv.reshape(-1, width)
        weight_out = weight_out.reshape(-1, width)
        weight_up = weight_up.reshape(-1, width)

        def weight_down_after(*needed):
            arrived = after([own_blocks, other_blocks], *needed)
            (weight_down,) = place_blocks(
                [blocks.reshape((size,) + own_down.shape) for blocks in arrived],
                [
                    (kz * near + kp) * 2 + (core ^ kc)
                    for kc in range(2)
                    for kp in range(near)
                    for kz in range(far)
                ],
                ((0, 2 * size, 0, down_rows),),
            )
            return weight_down.reshape(-1, units)

    else:
        teach_parts = teacher_parts()
        stack_all = lax.all_gather(own_stack, BOTH, axis=0)
        dense_stack = stack_all[:, :stack_rows].reshape(-1, width)
        small = stack_all[:, stack_rows:]
        weight_qkv = dense_stack[: 3 * width]
        weight_out = dense_stack[3 * width : 4 * width]
        weight_up = dense_stack[4 * width :]
        weight_down = lax.all_gather(own_down, BOTH, axis=0, tiled=True)

        def weight_down_after(*needed):
            return weight_down

        near_table = exchange(table_blocks, near_groups(near)).reshape(near * columns, part)
        found = lookup(table_t, local_ids)
        own_found = found[:half] + swap(found[half:], "vocab", 1)
        tokens_t = exchange(own_found.reshape(size, own_seqs, columns, seq_len), None)
    pos_all_t = small[:, : columns // 2, :seq_len].reshape(width, seq_len)
    vectors_all = small[:, pos_rows, :small_count].reshape(-1)
    parts = split_vectors(vectors_all.astype(jnp.float32), width)

    table_part = far_gather(near_table, near)
    tokens_t = tokens_t.transpose(1, 0, 2, 3).reshape(own_seqs, width, seq_len)
    embedded = (
        tokens_t.transpose(0, 2, 1).astype(jnp.float32)
        + pos_all_t.T.astype(jnp.float32)[None]
    ).reshape(own_rows, width)

    seq_start = place * pair_seqs + core * own_seqs
    own_lengths = lax.dynamic_slice_in_dim(lengths, seq_start, own_seqs)
    final, saved, weight_down = layer_forward(
        embedded, own_lengths, own_seqs, weight_qkv, weight_out, weight_up, weight_down_after, parts
    )
    teach = in_rows(teach_parts, near)
    own_pos = lax.dynamic_slice_in_dim(masked_pos, seq_start, own_seqs, 0)
    flat_rows = (jnp.arange(own_seqs, dtype=jnp.int32)[:, None] * seq_len + own_pos).reshape(-1)
    picked = jnp.take(final.reshape(own_rows, width), flat_rows, axis=0).astype(jnp.bfloat16)
    rows = join(picked, "vocab", 1).reshape(-1, width)
    rows = in_order(near_exchange(lambda q: rows, near), near).reshape(-1, width)

    bias_part = lax.dynamic_slice_in_dim(head_bias, p * part, part)
    output_logits, stats = head(rows, table_part, bias_part[None], teach, near)
    stats = jnp.stack(
        [stats]
        + [
            lax.ppermute(stats, BOTH, [(i, i ^ k) for i in range(2 * size)])
            for k in range(1, 2 * near)
        ]
    )
    group_start = (place - p) * pair_seqs
    group_pos = lax.dynamic_slice_in_dim(masked_pos, group_start, near * pair_seqs, 0)
    group_lengths = lax.dynamic_slice_in_dim(lengths, group_start, near * pair_seqs)
    group_valid = (group_pos < group_lengths[:, None]).astype(jnp.float32).reshape(near, 1, -1)
    count = jnp.sum((masked_pos < lengths[:, None]).astype(jnp.float32))
    grad_logits, rows_grad, bias_part_grad, divergence = head_back(
        output_logits, teach, stats, group_valid / count, table_part, near
    )
    group_loss = jnp.sum(divergence * group_valid) / (2 * near)
    rows_grad = halve(rows_grad.reshape(near, 2, -1, width).transpose(1, 0, 2, 3), "vocab", 1)
    rows_sends = [lax.dynamic_index_in_dim(rows_grad, p ^ k, 0, False) for k in range(near)]
    own_rows_grad = tree_sum(
        [rows_sends[0]] + [swap(send, "fsdp", k) for k, send in enumerate(rows_sends[1:], 1)]
    )
    grad_final = (
        jnp.zeros((own_rows, width), jnp.float32)
        .at[flat_rows]
        .add(own_rows_grad)
    )

    bias_part_grad = sum_far(after(bias_part_grad[0], *rows_sends), near)
    bias_grad = in_order(near_exchange(lambda q: bias_part_grad, near), near).reshape(-1)
    head_grad = lax.dot_general(
        rows,
        after(grad_logits, *rows_sends),
        (((0,), (0,)), ((), ())),
        preferred_element_type=jnp.float32,
    ).reshape(far, near, columns, part)
    if far == 4:
        line = FarLine(after(head_grad, bias_grad), near)
        grad_final = after(grad_final, *line.step())
    else:
        line = None

    def embed_columns(grad_embed):
        embed_t = grad_embed.reshape(own_seqs, seq_len, width).astype(jnp.bfloat16)
        embed_t = embed_t.transpose(0, 2, 1).reshape(own_seqs, size, columns, seq_len)
        return embed_t.transpose(1, 0, 2, 3)

    sums = WeightSums(near, far, width)
    embed_t, vectors_grad = layer_backward(
        grad_final,
        saved,
        own_lengths,
        own_seqs,
        weight_qkv,
        weight_out,
        weight_up,
        weight_down,
        parts,
        sums,
        line,
        embed_columns,
        stack_rows,
        down_rows,
    )

    embed_t = lax.all_to_all(embed_t, "fsdp", 0, 0, tiled=True).reshape(half, columns, seq_len)
    if far == 4:
        down_plane, up_plane = sums.plane_totals(("down", "up"), *sums.sent("attention"))
        sums.in_plane(("attention",), up_plane)
        attention_sends = sums.sent("attention")
        embed_t = after(embed_t, *attention_sends)
        other_t = swap(embed_t, "vocab", 1)
        vectors_grad = vectors_grad + swap(after(vectors_grad, *attention_sends), "vocab", 1)
        head_grad = line.total(*attention_sends)
        blocks = near_exchange(lambda q: lax.dynamic_index_in_dim(head_grad, q, 0, False), near)
        token_grad = spread_add(after(embed_t, head_grad, other_t), local_ids[:half], vocab_dev)
        (attention_plane,) = sums.plane_totals(("attention",), token_grad)
        own = jnp.concatenate(
            [jnp.concatenate([attention_plane, up_plane], 0), down_plane], 1
        )
        far_low = own.astype(jnp.bfloat16)
        arrived = exchange(far_low, far_groups(near))
        token_grad = token_grad + spread_add(
            after(other_t, far_low), local_ids[half:], vocab_dev
        )
        vectors_grad = tree_sum(near_exchange(lambda q: after(vectors_grad, far_low), near))
        vectors_far = [swap(vectors_grad, "fsdp", k * near) for k in range(1, far)]
        vectors_grad = tree_sum([vectors_grad] + after(vectors_far, token_grad))
        z = place // near
        other = lax.broadcasted_iota(jnp.int32, (far, 1, 1), 0) != z
        total = jnp.sum(jnp.where(other, arrived.astype(jnp.float32), own), axis=0)
        stack_total = total[:stack_rows]
        down_total = jnp.concatenate(
            jnp.split(total[stack_rows:], units // width, axis=0), 1
        )
        embed_t = jnp.concatenate([embed_t, other_t], 0)
    else:
        embed_t = jnp.concatenate([embed_t, swap(embed_t, "vocab", 1)], 0)
        token_grad = spread_add(embed_t, local_ids, vocab_dev)
        vectors_grad = sum_all(vectors_grad, near)
        head_grad = far_reduce(head_grad, near)
        blocks = near_exchange(lambda q: lax.dynamic_index_in_dim(head_grad, q, 0, False), near)
        stack_grad = [sums.state[name][0] for name in ("attention", "up")]
        stack_total = lax.psum_scatter(
            jnp.concatenate(stack_grad, 0), BOTH, scatter_dimension=0, tiled=True
        )
        down_total = lax.psum_scatter(
            sums.state["down"][0], BOTH, scatter_dimension=0, tiled=True
        )
    head_grad_t = jnp.concatenate(list(in_order(blocks, near)), 1).astype(jnp.float32)
    table_total = head_grad_t + token_grad
    pos_total = jnp.sum(embed_t.astype(jnp.float32), axis=0)
    pos_total = lax.dynamic_slice_in_dim(pos_total, core * (columns // 2), columns // 2, 0)
    vectors_total = lax.dynamic_slice_in_dim(
        vectors_grad, (2 * place + core) * small_count, small_count
    )

    stack_total = stack_total + jnp.where(stack_mask, 0.0, PRUNE_DECAY) * proj_stack
    down_total = down_total + jnp.where(down_mask, 0.0, PRUNE_DECAY) * ffn_down
    changes = jnp.sum((stack_mask != kept(stack_next)).astype(jnp.float32)) + jnp.sum(
        (down_mask != kept(down_next)).astype(jnp.float32)
    )
    squares = (
        jnp.sum(stack_total * stack_total)
        + jnp.sum(down_total * down_total)
        + jnp.sum(pos_total * pos_total)
        + jnp.sum(vectors_total * vectors_total)
        + jnp.sum(table_total * table_total)
        + jnp.sum(bias_grad * bias_grad) / size
    )
    scalars = jnp.stack([squares, group_loss, changes])
    scalars = sum_all(scalars, near)
    total_squares, loss_sum, change_total = scalars[0], scalars[1], scalars[2]
    grad_norm = jnp.sqrt(total_squares)
    factor = jnp.minimum(1.0, CLIP / (grad_norm + 1e-06))
    table_out = adam(table_t, table_total * factor, table_first.T, table_second.T, RATE_MATRIX)
    pos_out = adam(pos_table.T, pos_total * factor, pos_first.T, pos_second.T, RATE_MATRIX)
    stack_out = adam(proj_stack, stack_total * factor, stack_first, stack_second, RATE_MATRIX)
    down_out = adam(ffn_down, down_total * factor, down_first, down_second, RATE_MATRIX)
    vectors_out = adam(vectors, vectors_total * factor, vectors_first, vectors_second, RATE_VECTOR)
    bias_out = adam(head_bias, bias_grad * factor, bias_first, bias_second_moment, RATE_VECTOR)
    return (
        table_out[0].T,
        table_out[1].T,
        table_out[2].T,
        pos_out[0].T,
        pos_out[1].T,
        pos_out[2].T,
        stack_out[0],
        stack_out[1],
        stack_out[2],
        down_out[0],
        down_out[1],
        down_out[2],
        vectors_out[0],
        vectors_out[1],
        vectors_out[2],
        bias_out[0],
        bias_out[1],
        bias_out[2],
        loss_sum,
        count,
        grad_norm,
        change_total.astype(jnp.int32),
    )


def solution(mesh):
    in_specs = (
        P("fsdp", None),
        P(),
        P(),
        P("fsdp", "vocab"),
        P(("fsdp", "vocab"), None),
        P(("fsdp", "vocab"), None),
        P(("fsdp", "vocab"), None),
        P(("fsdp", "vocab"), None),
        P("vocab", "fsdp"),
        P("vocab", "fsdp"),
        P("vocab", "fsdp"),
        P(None, ("fsdp", "vocab")),
        P(None, ("fsdp", "vocab")),
        P(None, ("fsdp", "vocab")),
        P(("fsdp", "vocab"), None),
        P(("fsdp", "vocab"), None),
        P(("fsdp", "vocab"), None),
        P(("fsdp", "vocab"), None),
        P(("fsdp", "vocab"), None),
        P(("fsdp", "vocab"), None),
        P(("fsdp", "vocab")),
        P(("fsdp", "vocab")),
        P(("fsdp", "vocab")),
        P("vocab"),
        P("vocab"),
        P("vocab"),
    )
    out_specs = (
        P("vocab", "fsdp"),
        P("vocab", "fsdp"),
        P("vocab", "fsdp"),
        P(None, ("fsdp", "vocab")),
        P(None, ("fsdp", "vocab")),
        P(None, ("fsdp", "vocab")),
        P(("fsdp", "vocab"), None),
        P(("fsdp", "vocab"), None),
        P(("fsdp", "vocab"), None),
        P(("fsdp", "vocab"), None),
        P(("fsdp", "vocab"), None),
        P(("fsdp", "vocab"), None),
        P(("fsdp", "vocab")),
        P(("fsdp", "vocab")),
        P(("fsdp", "vocab")),
        P("vocab"),
        P("vocab"),
        P("vocab"),
        P(),
        P(),
        P(),
        P(),
    )
    return jax.shard_map(local, mesh=mesh, in_specs=in_specs, out_specs=out_specs, check_vma=False)
```

time: 1060 us -> 659 us (0.62)
  waiting for transfers between devices: 422 us -> 125 us
  Pallas kernels: 62.7 us -> 137 us
  matrix products: 122 us -> 59.5 us
  starting transfers between devices: 185 us -> 130 us
  local copies, waits for them, and re-layouts: 105 us -> 71.6 us
  other arithmetic: 129 us -> 99.2 us
    ppermute x12 -> x13, waiting for transfers between devices: 213 us -> 27.1 us  [the longest x3 17.8 us: step(): lax.ppermute(sends[1], 'fsdp', [(i, i - near) for i in range(size - k * n...]
    pallas_call x0 -> x6, Pallas kernels: none -> 74 us  [the longest x2 17.6 us: place_blocks(): pl.pallas_call(functools.partial(place_kernel, spans, pieces[0].shape[0])...]
    ppermute x25 -> x45, starting transfers between devices: 112 us -> 42.6 us  [swap(): return lax.ppermute(x, axis, [(i, i ^ bit) for i in range(size)])]
    dot_general x21 -> x13, matrix products: 115 us -> 52 us  [the longest x4 14.2 us: project(): jnp.einsum('mh,ph->mp', input_batch, weight_matrix, preferred_element_typ...]
    ppermute x25 -> x45, waiting for transfers between devices: 97.7 us -> 46.3 us  [swap(): return lax.ppermute(x, axis, [(i, i ^ bit) for i in range(size)])]
    ppermute x9 -> x18, waiting for transfers between devices: 63 us -> 15.5 us  [near_exchange(): lax.ppermute(take(p ^ k), 'fsdp', [(i, i ^ k) for i in range(size)])]
    all_to_all x1, waiting for transfers between devices: 47.3 us -> 0.01 us  [local(): lax.all_to_all(jnp.broadcast_to(token_ids[None], (size, pair_seqs, seq_le...]
    all_to_all x1 -> x5, waiting for transfers between devices: 0.01 us -> 36.3 us  [exchange(): return lax.all_to_all(x, 'fsdp', 0, 0, tiled=True, axis_index_groups=groups)]
  transfers between devices with their start and end apart: 52 -> 84, of which waited for: 30 -> 24; matrix products, arithmetic and copies ran while one was open for 24% -> 29% of each run, Pallas kernels for 6% -> 17%
where the time goes in v2:
time: 659 us; the launch traced here: 649 us
  Pallas kernels  137 us (21%)
  starting transfers between devices  130 us (20%)
  waiting for transfers between devices  125 us (19%)
  other arithmetic  99.2 us (15%)
  local copies, waits for them, and re-layouts  71.6 us (11%)
  matrix products  59.5 us (9%)
  between operations  26.7 us (4%)
    ppermute x45, waiting for transfers between devices, swap(): return lax.ppermute(x, axis, [(i, i ^ bit) for i in range(size)])  46.3 us
    ppermute x45, starting transfers between devices, swap(): return lax.ppermute(x, axis, [(i, i ^ bit) for i in range(size)])  42.6 us
    all_to_all x5, waiting for transfers between devices, exchange(): return lax.all_to_all(x, 'fsdp', 0, 0, tiled=True, axis_index_groups=groups)  36.3 us
    pallas_call x2, Pallas kernels, spread_add(): pl.pallas_call(functools.partial(spread_kernel, low_count), grid=(blocks,...  32.2 us
    pallas_call x1, Pallas kernels, lookup(): pl.pallas_call(functools.partial(lookup_kernel, low_count), grid=(blocks,...  30.7 us
    all_to_all x5, starting transfers between devices, exchange(): return lax.all_to_all(x, 'fsdp', 0, 0, tiled=True, axis_index_groups=groups)  30.3 us
    ppermute x18, starting transfers between devices, near_exchange(): lax.ppermute(take(p ^ k), 'fsdp', [(i, i ^ k) for i in range(size)])  21.2 us
    ppermute x3, waiting for transfers between devices, step(): lax.ppermute(sends[1], 'fsdp', [(i, i - near) for i in range(size - k * n...  17.8 us
  transfers between devices with their start and end apart: 84, of which 24 were waited for; matrix products, arithmetic and copies ran while one was open for 29% of the time, Pallas kernels for 17%

profile of v2, /device:TPU:0, one launch (start us, length us, event | category | flops | bytes accessed | tf_op | source)
XLA Modules:
  0.0 649.0 jit_solution(15987730160028448001)
XLA Ops:
  8.5 8.3 %all-to-all-start = ((s32[16,2,512]{2,1,0:T(2,128)}), s32[16,2,512]{2,1,0:T(2,128)S(1)}, u32[]{:S(2)}, u32[]{:S(2)}) async-start(s32[16,2,512]{2,1,0:T(2,128)} %broadcast_in_dim.68), calls=%async_computation | async-start | bytes 131072 | tf_op jit(solution)/shard_map/all_to_all | solution.py:880
  36.4 30.7 %lookup.1 = bf16[32,48,512]{2,1,0:T(8,128)(2,1)S(1)} custom-call(s32[32,1,512]{2,1,0:T(1,128)S(1)} %add_subtract_fusion.ids_ref, f32[48,15360]{1,0:T(8,128)S(1)} %bitcast.376), custom_call_target="tpu_custom_call" | custom-call | flops 24159191040 | bytes 4521984 | tf_op jit(solution)/shard_map/lookup/pallas_call | solution.py:293
  77.5 6.2 all-to-all-start.2
  86.5 5.4 collective-permute-done.8.refs_6_
  96.1 17.5 %collective-permute-done.4.refs_1_ = bf16[2,240,768]{2,1,0:T(8,128)(2,1)} collective-permute-done((bf16[2,240,768]{2,1,0:T(8,128)(2,1)S(1)}, bf16[2,240,768]{2,1,0:T(8,128)(2,1)}, u32[]{:S(2)}, u32[]{:S(2)}) %collective-permute-start.4) | collective-permute-done | bytes 737312 | tf_op jit(solution)/shard_map/ppermute | solution.py:48
  118.3 12.0 %collective-permute-done.9.refs_7_ = bf16[2,240,768]{2,1,0:T(8,128)(2,1)} collective-permute-done((bf16[2,240,768]{2,1,0:T(8,128)(2,1)S(1)}, bf16[2,240,768]{2,1,0:T(8,128)(2,1)}, u32[]{:S(2)}, u32[]{:S(2)}) %collective-permute-start.9) | collective-permute-done | bytes 737312 | tf_op jit(solution)/shard_map/ppermute | solution.py:48
  134.1 5.0 all-to-all-start.3
  141.7 5.1 constant_dynamic-slice_fusion.1
  155.1 8.7 %place.2 = (bf16[12,192,768]{2,1,0:T(8,128)(2,1)}, bf16[4,192,768]{2,1,0:T(8,128)(2,1)S(1)}, bf16[16,192,768]{2,1,0:T(8,128)(2,1)}, bf16[32,48,768]{2,1,0:T(8,128)(2,1)}) custom-call(s32[32]{0:T(128)S(1)} %stack.325.order_ref, bf16[2,240,768]{2,1,0:T(8,128)(2,1)S(1)} %pad_maximum_fusion.6.refs_0_, bf16[2,240,768]{2,1,0:T(8,128)(2,1)} %collective-permute-done.4.refs_1_, ...), custom_call_target="tpu_custom_call" | custom-call | tf_op jit(solution)/shard_map/place/pallas_call | solution.py:248
  171.7 7.4 %all-to-all-start.4 = ((bf16[4,4,24,3072]{3,2,1,0:T(8,128)(2,1)}), bf16[4,4,24,3072]{3,2,1,0:T(8,128)(2,1)}, u32[]{:S(2)}, u32[]{:S(2)}) async-start(bf16[4,4,24,3072]{3,2,1,0:T(8,128)(2,1)} %broadcast_in_dim.132), calls=%async_computation.4 | async-start | bytes 4718592 | tf_op jit(solution)/shard_map/all_to_all | solution.py:118
  183.9 11.8 %attend.1 = bf16[512,768]{1,0:T(8,128)(2,1)S(1)} custom-call(s32[1]{0:T(128)} %dynamic_slice.146.lengths_ref, bf16[512,2304]{1,0:T(8,128)(2,1)S(1)} %fusion.8.query_ref.key_ref.value_ref, bf16[512,2304]{1,0:T(8,128)(2,1)S(1)} %fusion.8.query_ref.key_ref.value_ref, bf16[512,2304]{1,0:T(8,128)(2,1)S(1)} %fusion.8.query_ref.key_ref.value_ref), custom_call_target="tpu_custom_call" | custom-call | flops 805306368 | bytes 3145728 | tf_op jit(solution)/shard_map/attend/pallas_call | solution.py:437
  195.7 35.3 %all-to-all-done.4 = bf16[4,4,24,3072]{3,2,1,0:T(8,128)(2,1)} async-done(((bf16[4,4,24,3072]{3,2,1,0:T(8,128)(2,1)}), bf16[4,4,24,3072]{3,2,1,0:T(8,128)(2,1)}, u32[]{:S(2)}, u32[]{:S(2)}) %all-to-all-start.4) | async-done | bytes 2359328 | tf_op jit(solution)/shard_map/all_to_all | solution.py:118
  234.8 6.5 %multiply_convert_fusion = (bf16[512,3072]{1,0:T(8,128)(2,1)S(1)}, f32[512,3072]{1,0:T(8,128)}) fusion(f32[3072]{0:T(1024)S(1)} %slice.200, bf16[512,768]{1,0:T(8,128)(2,1)S(1)} %fusion.22, bf16[3072,768]{1,0:T(8,128)(2,1)} %bitcast.423), kind=kOutput, calls=%fused_computation.11 | convolution fusion | flops 2425356288 | bytes 14954496 | tf_op jit(solution)/shard_map/mh,ph->mp/dot_general | solution.py:394
  244.6 8.9 %place.3 = bf16[32,24,3072]{2,1,0:T(8,128)(2,1)S(1)} custom-call(s32[32]{0:T(128)S(1)} %stack.364.order_ref, bf16[16,24,3072]{2,1,0:T(8,128)(2,1)} %bitcast.88.refs_0_, bf16[16,24,3072]{2,1,0:T(8,128)(2,1)S(1)} %bitcast.386), custom_call_target="tpu_custom_call" | custom-call | tf_op jit(solution)/shard_map/place/pallas_call | solution.py:248
  270.7 5.8 collective-permute-done.21
  276.7 12.7 %head.1 = (f32[640,3840]{1,0:T(8,128)}, f32[4,8,160]{2,1,0:T(8,128)S(1)}) custom-call(bf16[640,768]{1,0:T(8,128)(2,1)S(1)} %bitcast.381, bf16[768,3840]{1,0:T(8,128)(2,1)} %all-gather.2.cloned.1.call-done.table_ref, f32[1,3840]{1,0:T(1,128)S(1)} %broadcast_in_dim.134.bias_ref, bf16[640,3840]{1,0:T(8,128)(2,1)} %constant_dynamic-update-slice_fusion.1.teach_ref), custom_call_target="tpu_custom_call" | custom-call | flops 3774873600 | bytes 20643840 | tf_op jit(solution)/shard_map/head/pallas_call | solution.py:542
  302.4 15.1 %head_back.1 = (bf16[640,3840]{1,0:T(8,128)(2,1)}, f32[640,768]{1,0:T(8,128)S(1)}, f32[1,3840]{1,0:T(1,128)S(1)}, f32[4,1,160]{2,1,0:T(1,128)S(1)}) custom-call(f32[640,3840]{1,0:T(8,128)} %get-tuple-element.95.logits_ref, bf16[640,3840]{1,0:T(8,128)(2,1)} %constant_dynamic-update-slice_fusion.1.teach_ref, ...), custom_call_target="tpu_custom_call" | custom-call | flops 3774873600 | bytes 25559040 | tf_op jit(solution)/shard_map/head_back/pallas_call | solution.py:611
  343.5 11.8 %fusion.6 = f32[4,4,48,3840]{3,2,1,0:T(8,128)} fusion(bf16[4,4,48,640]{3,2,1,0:T(8,128)(2,1)} %bitcast.418, bf16[640,3840]{1,0:T(8,128)(2,1)} %get-tuple-element.99), kind=kOutput, calls=%fused_computation.13 | convolution fusion | flops 3774873600 | bytes 17694720 | tf_op jit(solution)/shard_map/dot_general | solution.py:1056
  381.7 6.6 %fusion.5 = bf16[512,3072]{1,0:T(8,128)(2,1)S(1)} fusion(f32[512,3072]{1,0:T(8,128)} %get-tuple-element.280, bf16[512,768]{1,0:T(8,128)(2,1)S(1)} %get-tuple-element.104, bf16[768,3072]{1,0:T(8,128)(2,1)S(1)} %bitcast.380, f32[3072]{0:T(1024)S(1)} %copy-done.60), kind=kOutput, calls=%fused_computation.9 | convolution fusion | flops 2433220608 | bytes 14954496 | tf_op jit(solution)/shard_map/az,zh->ah/dot_general | solution.py:398
  403.0 5.9 fusion.11
  427.7 16.9 %attend_back.1 = bf16[512,2304]{1,0:T(8,128)(2,1)S(1)} custom-call(s32[1]{0:T(128)} %dynamic_slice.146.lengths_ref, bf16[512,2304]{1,0:T(8,128)(2,1)S(1)} %fusion.8.query_ref.key_ref.value_ref, bf16[512,2304]{1,0:T(8,128)(2,1)S(1)} %fusion.8.query_ref.key_ref.value_ref, bf16[512,2304]{1,0:T(8,128)(2,1)S(1)} %fusion.8.query_ref.key_ref.value_ref, ...), custom_call_target="tpu_custom_call" | custom-call | flops 2013265920 | bytes 5505024 | tf_op jit(solution)/shard_map/attend_back/pallas_call | solution.py:500
  454.5 5.8 fusion.10
  460.3 5.1 fusion.25
  465.4 7.9 %pad_maximum_fusion = f32[3072,768]{1,0:T(8,128)} fusion(f32[768,768]{1,0:T(8,128)} %fusion.149, f32[2304,768]{1,0:T(8,128)} %fusion.25), kind=kLoop, calls=%fused_computation.3 | loop fusion | flops 2359296 | bytes 18874368 | tf_op jit(solution)/shard_map/concatenate | solution.py:758
  479.3 5.7 collective-permute-start.49
  497.4 17.8 %collective-permute-done.50 = bf16[4,48,3840]{2,1,0:T(8,128)(2,1)} collective-permute-done((bf16[4,48,3840]{2,1,0:T(8,128)(2,1)}, bf16[4,48,3840]{2,1,0:T(8,128)(2,1)}, u32[]{:S(2)}, u32[]{:S(2)}) %collective-permute-start.50) | collective-permute-done | bytes 1474592 | tf_op jit(solution)/shard_map/ppermute | solution.py:155
  525.9 16.1 %spread_add.2 = f32[48,15360]{1,0:T(8,128)S(1)} custom-call(s32[16,1,512]{2,1,0:T(1,128)S(1)} %get-tuple-element.247.ids_ref, bf16[16,48,512]{2,1,0:T(8,128)(2,1)S(1)} %bitcast.384), custom_call_target="tpu_custom_call" | custom-call | flops 12079595520 | bytes 3735552 | tf_op jit(solution)/shard_map/spread_add/pallas_call | solution.py:348
  547.4 7.1 %all-to-all-start.6 = ((bf16[4,288,768]{2,1,0:T(8,128)(2,1)}), bf16[4,288,768]{2,1,0:T(8,128)(2,1)}, u32[]{:S(2)}, u32[]{:S(2)}) async-start(bf16[4,288,768]{2,1,0:T(8,128)(2,1)} %fusion.15), calls=%async_computation.6 | async-start | bytes 3538944 | tf_op jit(solution)/shard_map/all_to_all | solution.py:118
  564.0 16.1 %spread_add.3 = f32[48,15360]{1,0:T(8,128)S(1)} custom-call(s32[16,1,512]{2,1,0:T(1,128)S(1)} %get-tuple-element.246.ids_ref, bf16[16,48,512]{2,1,0:T(8,128)(2,1)S(1)} %collective-permute-done.58.grad_ref), custom_call_target="tpu_custom_call" | custom-call | flops 12079595520 | bytes 3735552 | tf_op jit(solution)/shard_map/spread_add/pallas_call | solution.py:348
  583.2 5.5 collective-permute-start.68
  590.9 8.0 %collective-permute-done.67 = f32[10752]{0:T(1024)S(1)} collective-permute-done((f32[10752]{0:T(1024)S(1)}, f32[10752]{0:T(1024)S(1)}, u32[]{:S(2)}, u32[]{:S(2)}) %collective-permute-start.67) | collective-permute-done | bytes 43040 | tf_op jit(solution)/shard_map/ppermute | solution.py:48
  632.8 6.9 %subtract_bitcast_fusion = (f32[15360,48]{0,1:T(8,128)}, f32[15360,48]{0,1:T(8,128)}, f32[15360,48]{0,1:T(8,128)}) fusion(f32[48,15360]{1,0:T(8,128)S(1)} %copy-done.29, f32[]{:T(128)S(6)} %min.32, f32[15360,48]{0,1:T(8,128)S(1)} %copy-done.37, f32[15360,48]{0,1:T(8,128)} %param.36, f32[15360,48]{0,1:T(8,128)S(1)} %copy-done.1), kind=kLoop, calls=%fused_computation.43 | loop fusion | flops 11796480 | bytes 20643844 | tf_op jit(solution)/shard_map/transpose | solution.py:1170
  (561 shorter events, 276.7 us)
Async XLA Ops:
  27.2 41.0 %collective-permute-start.3 = (bf16[240,768]{1,0:T(8,128)(2,1)S(1)}, bf16[240,768]{1,0:T(8,128)(2,1)}, u32[]{:S(2)}, u32[]{:S(2)}) collective-permute-start(bf16[240,768]{1,0:T(8,128)(2,1)S(1)} %fusion.61), channel_id=1, source_target_pairs={{0,24},{2,26},{4,28},{6,30},{8,16},{10,18},{12,20},{14,22},{16,8},... | collective-permute-start | bytes 1105928 | tf_op jit(solution)/shard_map/ppermute | solution.py:48
  31.0 37.3 %collective-permute-start.2 = (bf16[240,768]{1,0:T(8,128)(2,1)S(1)}, bf16[240,768]{1,0:T(8,128)(2,1)}, u32[]{:S(2)}, u32[]{:S(2)}) collective-permute-start(bf16[240,768]{1,0:T(8,128)(2,1)S(1)} %fusion.61), channel_id=1, source_target_pairs={{0,16},{2,18},{4,20},{6,22},{8,24},{10,26},{12,28},{14,30},{16,0},... | collective-permute-start | bytes 1105928 | tf_op jit(solution)/shard_map/ppermute | solution.py:48
  31.0 37.3 %collective-permute-start.1 = (bf16[240,768]{1,0:T(8,128)(2,1)S(1)}, bf16[240,768]{1,0:T(8,128)(2,1)}, u32[]{:S(2)}, u32[]{:S(2)}) collective-permute-start(bf16[240,768]{1,0:T(8,128)(2,1)S(1)} %fusion.61), channel_id=1, source_target_pairs={{0,8},{2,10},{4,12},{6,14},{8,0},{10,2},{12,4},{14,6},{16,24},{18,... | collective-permute-start | bytes 1105928 | tf_op jit(solution)/shard_map/ppermute | solution.py:48
  31.8 45.7 %all-to-all-start.1 = ((bf16[4,48,3840]{2,1,0:T(8,128)(2,1)}), bf16[4,48,3840]{2,1,0:T(8,128)(2,1)}, u32[]{:S(2)}, u32[]{:S(2)}) async-start(bf16[4,48,3840]{2,1,0:T(8,128)(2,1)} %bitcast.397), calls=%async_computation.1 | async-start | bytes 2949120 | tf_op jit(solution)/shard_map/all_to_all | solution.py:118
  74.5 39.1 %collective-permute-start.4 = (bf16[2,240,768]{2,1,0:T(8,128)(2,1)S(1)}, bf16[2,240,768]{2,1,0:T(8,128)(2,1)}, u32[]{:S(2)}, u32[]{:S(2)}) collective-permute-start(bf16[2,240,768]{2,1,0:T(8,128)(2,1)S(1)} %pad_maximum_fusion.6.refs_0_), channel_id=1, source_target_pairs={{0,2},{2,0},{4,6},{6,4},{8,10},{10,8},{12,14},{14,12},{16,18},{18,... | collective-permute-start | bytes 2211848 | tf_op jit(solution)/shard_map/ppermute | solution.py:48
  77.5 55.7 %all-to-all-start.2 = ((bf16[16,1,48,512]{3,2,1,0:T(8,128)(2,1)}), bf16[16,1,48,512]{3,2,1,0:T(8,128)(2,1)}, u32[]{:S(2)}, u32[]{:S(2)}) async-start(bf16[16,1,48,512]{3,2,1,0:T(8,128)(2,1)} %bitcast.404), calls=%async_computation.2 | async-start | bytes 1572864 | tf_op jit(solution)/shard_map/all_to_all | solution.py:118
  83.7 193.1 %all-gather.2.cloned.1.call-start = ((), (), s32[]{:S(2)}) async-start(), calls=%async_computation.7 | async-start | bytes 7372800 | tf_op jit(solution)/shard_map/all_gather | solution.py:131
  84.5 32.4 %collective-permute-start.5 = (bf16[2,240,768]{2,1,0:T(8,128)(2,1)S(1)}, bf16[2,240,768]{2,1,0:T(8,128)(2,1)}, u32[]{:S(2)}, u32[]{:S(2)}) collective-permute-start(bf16[2,240,768]{2,1,0:T(8,128)(2,1)S(1)} %pad_maximum_fusion.6.refs_0_), channel_id=1, source_target_pairs={{0,4},{2,6},{4,0},{6,2},{8,12},{10,14},{12,8},{14,10},{16,20},{18,... | collective-permute-start | bytes 2211848 | tf_op jit(solution)/shard_map/ppermute | solution.py:48
  92.1 38.2 %collective-permute-start.9 = (bf16[2,240,768]{2,1,0:T(8,128)(2,1)S(1)}, bf16[2,240,768]{2,1,0:T(8,128)(2,1)}, u32[]{:S(2)}, u32[]{:S(2)}) collective-permute-start(bf16[2,240,768]{2,1,0:T(8,128)(2,1)S(1)} %collective-permute-done.8.refs_6_), channel_id=1, source_target_pairs={{0,2},{2,0},{4,6},{6,4},{8,10},{10,8},{12,14},{14,12},{16,18},{18,... | collective-permute-start | bytes 2211848 | tf_op jit(solution)/shard_map/ppermute | solution.py:48
  116.9 35.4 %collective-permute-start.11 = (bf16[2,240,768]{2,1,0:T(8,128)(2,1)}, bf16[2,240,768]{2,1,0:T(8,128)(2,1)}, u32[]{:S(2)}, u32[]{:S(2)}) collective-permute-start(bf16[2,240,768]{2,1,0:T(8,128)(2,1)} %collective-permute-done.4.refs_1_), channel_id=1, source_target_pairs={{0,1},{1,0},{2,3},{3,2},{4,5},{5,4},{6,7},{7,6},{8,9},{9,8},{10,11... | collective-permute-start | bytes 2211848 | tf_op jit(solution)/shard_map/ppermute | solution.py:48
  116.9 32.5 %collective-permute-start.15 = (bf16[2,240,768]{2,1,0:T(8,128)(2,1)}, bf16[2,240,768]{2,1,0:T(8,128)(2,1)}, u32[]{:S(2)}, u32[]{:S(2)}) collective-permute-start(bf16[2,240,768]{2,1,0:T(8,128)(2,1)} %collective-permute-done.7.refs_5_), channel_id=1, source_target_pairs={{0,1},{1,0},{2,3},{3,2},{4,5},{5,4},{6,7},{7,6},{8,9},{9,8},{10,11... | collective-permute-start | bytes 2211848 | tf_op jit(solution)/shard_map/ppermute | solution.py:48
  118.3 32.6 %collective-permute-start.12 = (bf16[2,240,768]{2,1,0:T(8,128)(2,1)}, bf16[2,240,768]{2,1,0:T(8,128)(2,1)}, u32[]{:S(2)}, u32[]{:S(2)}) collective-permute-start(bf16[2,240,768]{2,1,0:T(8,128)(2,1)} %collective-permute-done.5.refs_2_), channel_id=1, source_target_pairs={{0,1},{1,0},{2,3},{3,2},{4,5},{5,4},{6,7},{7,6},{8,9},{9,8},{10,11... | collective-permute-start | bytes 2211848 | tf_op jit(solution)/shard_map/ppermute | solution.py:48
  134.1 34.8 %all-to-all-start.3 = ((bf16[4,24,3072]{2,1,0:T(8,128)(2,1)}), bf16[4,24,3072]{2,1,0:T(8,128)(2,1)}, u32[]{:S(2)}, u32[]{:S(2)}) async-start(bf16[4,24,3072]{2,1,0:T(8,128)(2,1)} %broadcast_in_dim.131), calls=%async_computation.3 | async-start | bytes 1179648 | tf_op jit(solution)/shard_map/all_to_all | solution.py:118
  149.4 116.0 %collective-permute-start.25 = (bf16[160,3840]{1,0:T(8,128)(2,1)}, bf16[160,3840]{1,0:T(8,128)(2,1)}, u32[]{:S(2)}, u32[]{:S(2)}) collective-permute-start(bf16[160,3840]{1,0:T(8,128)(2,1)} %get-tuple-element.191), channel_id=1, source_target_pairs={{0,6},{2,4},{4,2},{6,0},{8,14},{10,12},{12,10},{14,8},{16,22},{18,... | collective-permute-start | bytes 3686408 | tf_op jit(solution)/shard_map/ppermute | solution.py:103
  150.9 108.3 %collective-permute-start.24 = (bf16[160,3840]{1,0:T(8,128)(2,1)}, bf16[160,3840]{1,0:T(8,128)(2,1)}, u32[]{:S(2)}, u32[]{:S(2)}) collective-permute-start(bf16[160,3840]{1,0:T(8,128)(2,1)} %get-tuple-element.192), channel_id=1, source_target_pairs={{0,4},{2,6},{4,0},{6,2},{8,12},{10,14},{12,8},{14,10},{16,20},{18,... | collective-permute-start | bytes 3686408 | tf_op jit(solution)/shard_map/ppermute | solution.py:103
  152.3 88.9 %collective-permute-start.23 = (bf16[160,3840]{1,0:T(8,128)(2,1)}, bf16[160,3840]{1,0:T(8,128)(2,1)}, u32[]{:S(2)}, u32[]{:S(2)}) collective-permute-start(bf16[160,3840]{1,0:T(8,128)(2,1)} %get-tuple-element.193), channel_id=1, source_target_pairs={{0,2},{2,0},{4,6},{6,4},{8,10},{10,8},{12,14},{14,12},{16,18},{18,... | collective-permute-start | bytes 3686408 | tf_op jit(solution)/shard_map/ppermute | solution.py:103
  171.7 59.2 %all-to-all-start.4 = ((bf16[4,4,24,3072]{3,2,1,0:T(8,128)(2,1)}), bf16[4,4,24,3072]{3,2,1,0:T(8,128)(2,1)}, u32[]{:S(2)}, u32[]{:S(2)}) async-start(bf16[4,4,24,3072]{3,2,1,0:T(8,128)(2,1)} %broadcast_in_dim.132), calls=%async_computation.4 | async-start | bytes 4718592 | tf_op jit(solution)/shard_map/all_to_all | solution.py:118
  362.5 40.4 %collective-permute-start.41 = (bf16[4,48,3840]{2,1,0:T(8,128)(2,1)}, bf16[4,48,3840]{2,1,0:T(8,128)(2,1)}, u32[]{:S(2)}, u32[]{:S(2)}) collective-permute-start(bf16[4,48,3840]{2,1,0:T(8,128)(2,1)} %get-tuple-element.182), channel_id=1, source_target_pairs={{24,16},{26,18},{28,20},{30,22},{25,17},{27,19},{29,21},{31,23}} | collective-permute-start | bytes 4423688 | tf_op jit(solution)/shard_map/ppermute | solution.py:155
  364.3 38.6 %collective-permute-start.40 = (bf16[4,48,3840]{2,1,0:T(8,128)(2,1)}, bf16[4,48,3840]{2,1,0:T(8,128)(2,1)}, u32[]{:S(2)}, u32[]{:S(2)}) collective-permute-start(bf16[4,48,3840]{2,1,0:T(8,128)(2,1)} %get-tuple-element.183), channel_id=1, source_target_pairs={{0,8},{2,10},{4,12},{6,14},{1,9},{3,11},{5,13},{7,15}} | collective-permute-start | bytes 4423688 | tf_op jit(solution)/shard_map/ppermute | solution.py:154
  408.9 45.6 %collective-permute-start.46 = (bf16[4,48,3840]{2,1,0:T(8,128)(2,1)}, bf16[4,48,3840]{2,1,0:T(8,128)(2,1)}, u32[]{:S(2)}, u32[]{:S(2)}) collective-permute-start(bf16[4,48,3840]{2,1,0:T(8,128)(2,1)} %get-tuple-element.180), channel_id=1, source_target_pairs={{16,8},{18,10},{20,12},{22,14},{24,16},{26,18},{28,20},{30,22},{17... | collective-permute-start | bytes 4423688 | tf_op jit(solution)/shard_map/ppermute | solution.py:155
  410.7 43.8 %collective-permute-start.45 = (bf16[4,48,3840]{2,1,0:T(8,128)(2,1)}, bf16[4,48,3840]{2,1,0:T(8,128)(2,1)}, u32[]{:S(2)}, u32[]{:S(2)}) collective-permute-start(bf16[4,48,3840]{2,1,0:T(8,128)(2,1)} %get-tuple-element.181), channel_id=1, source_target_pairs={{0,8},{2,10},{4,12},{6,14},{8,16},{10,18},{12,20},{14,22},{1,9},{3... | collective-permute-start | bytes 4423688 | tf_op jit(solution)/shard_map/ppermute | solution.py:154
  421.8 57.5 %collective-permute-start.52 = (bf16[768,768]{1,0:T(8,128)(2,1)}, bf16[768,768]{1,0:T(8,128)(2,1)}, u32[]{:S(2)}, u32[]{:S(2)}) collective-permute-start(bf16[768,768]{1,0:T(8,128)(2,1)} %pad_maximum_fusion.2), channel_id=1, source_target_pairs={{0,2},{2,0},{4,6},{6,4},{8,10},{10,8},{12,14},{14,12},{16,18},{18,... | collective-permute-start | bytes 3538952 | tf_op jit(solution)/shard_map/ppermute | solution.py:48
  423.6 61.4 %collective-permute-start.53 = (bf16[768,768]{1,0:T(8,128)(2,1)}, bf16[768,768]{1,0:T(8,128)(2,1)}, u32[]{:S(2)}, u32[]{:S(2)}) collective-permute-start(bf16[768,768]{1,0:T(8,128)(2,1)} %pad_maximum_fusion.3), channel_id=1, source_target_pairs={{0,4},{2,6},{4,0},{6,2},{8,12},{10,14},{12,8},{14,10},{16,20},{18,... | collective-permute-start | bytes 3538952 | tf_op jit(solution)/shard_map/ppermute | solution.py:48
  425.9 59.2 %collective-permute-start.54 = (bf16[768,768]{1,0:T(8,128)(2,1)}, bf16[768,768]{1,0:T(8,128)(2,1)}, u32[]{:S(2)}, u32[]{:S(2)}) collective-permute-start(bf16[768,768]{1,0:T(8,128)(2,1)} %pad_maximum_fusion.4), channel_id=1, source_target_pairs={{0,6},{2,4},{4,2},{6,0},{8,14},{10,12},{12,10},{14,8},{16,22},{18,... | collective-permute-start | bytes 3538952 | tf_op jit(solution)/shard_map/ppermute | solution.py:48
  449.1 48.3 %all-to-all-start.5 = ((bf16[16,1,48,512]{3,2,1,0:T(8,128)(2,1)}), bf16[16,1,48,512]{3,2,1,0:T(8,128)(2,1)S(1)}, u32[]{:S(2)}, u32[]{:S(2)}) async-start(bf16[16,1,48,512]{3,2,1,0:T(8,128)(2,1)} %bitcast.403), calls=%async_computation.5 | async-start | bytes 1572864 | tf_op jit(solution)/shard_map/all_to_all | solution.py:1091
  477.7 37.4 %collective-permute-start.50 = (bf16[4,48,3840]{2,1,0:T(8,128)(2,1)}, bf16[4,48,3840]{2,1,0:T(8,128)(2,1)}, u32[]{:S(2)}, u32[]{:S(2)}) collective-permute-start(bf16[4,48,3840]{2,1,0:T(8,128)(2,1)} %get-tuple-element.178), channel_id=1, source_target_pairs={{8,0},{10,2},{12,4},{14,6},{16,8},{18,10},{20,12},{22,14},{24,16},... | collective-permute-start | bytes 4423688 | tf_op jit(solution)/shard_map/ppermute | solution.py:155
  479.3 37.1 %collective-permute-start.49 = (bf16[4,48,3840]{2,1,0:T(8,128)(2,1)}, bf16[4,48,3840]{2,1,0:T(8,128)(2,1)}, u32[]{:S(2)}, u32[]{:S(2)}) collective-permute-start(bf16[4,48,3840]{2,1,0:T(8,128)(2,1)} %get-tuple-element.179), channel_id=1, source_target_pairs={{0,8},{2,10},{4,12},{6,14},{8,16},{10,18},{12,20},{14,22},{16,24},... | collective-permute-start | bytes 4423688 | tf_op jit(solution)/shard_map/ppermute | solution.py:154
  495.9 46.1 %collective-permute-start.61 = (bf16[384,768]{1,0:T(8,128)(2,1)}, bf16[384,768]{1,0:T(8,128)(2,1)}, u32[]{:S(2)}, u32[]{:S(2)}) collective-permute-start(bf16[384,768]{1,0:T(8,128)(2,1)} %bitcast.154), channel_id=1, source_target_pairs={{0,6},{2,4},{4,2},{6,0},{8,14},{10,12},{12,10},{14,8},{16,22},{18,... | collective-permute-start | bytes 1769480 | tf_op jit(solution)/shard_map/ppermute | solution.py:48
  497.4 44.6 %collective-permute-start.59 = (bf16[384,768]{1,0:T(8,128)(2,1)}, bf16[384,768]{1,0:T(8,128)(2,1)}, u32[]{:S(2)}, u32[]{:S(2)}) collective-permute-start(bf16[384,768]{1,0:T(8,128)(2,1)} %bitcast.152), channel_id=1, source_target_pairs={{0,2},{2,0},{4,6},{6,4},{8,10},{10,8},{12,14},{14,12},{16,18},{18,... | collective-permute-start | bytes 1769480 | tf_op jit(solution)/shard_map/ppermute | solution.py:48
  524.1 34.3 %collective-permute-start.56 = (f32[48,3840]{1,0:T(8,128)}, f32[48,3840]{1,0:T(8,128)}, u32[]{:S(2)}, u32[]{:S(2)}) collective-permute-start(f32[48,3840]{1,0:T(8,128)} %get-tuple-element.205), channel_id=1, source_target_pairs={{0,4},{2,6},{4,0},{6,2},{8,12},{10,14},{12,8},{14,10},{16,20},{18,... | collective-permute-start | bytes 2211848 | tf_op jit(solution)/shard_map/ppermute | solution.py:103
  525.6 32.8 %collective-permute-start.55 = (f32[48,3840]{1,0:T(8,128)}, f32[48,3840]{1,0:T(8,128)}, u32[]{:S(2)}, u32[]{:S(2)}) collective-permute-start(f32[48,3840]{1,0:T(8,128)} %get-tuple-element.206), channel_id=1, source_target_pairs={{0,6},{2,4},{4,2},{6,0},{8,14},{10,12},{12,10},{14,8},{16,22},{18,... | collective-permute-start | bytes 2211848 | tf_op jit(solution)/shard_map/ppermute | solution.py:103
  547.4 52.2 %all-to-all-start.6 = ((bf16[4,288,768]{2,1,0:T(8,128)(2,1)}), bf16[4,288,768]{2,1,0:T(8,128)(2,1)}, u32[]{:S(2)}, u32[]{:S(2)}) async-start(bf16[4,288,768]{2,1,0:T(8,128)(2,1)} %fusion.15), calls=%async_computation.6 | async-start | bytes 3538944 | tf_op jit(solution)/shard_map/all_to_all | solution.py:118
  (154 other events, 1776.6 us)
Sparse Core Ops, SparseCore 0:
  133.3 117.3 all-gather.1

commit v3 on v2

--- a/solution.py
+++ b/solution.py
@@ -25,6 +25,7 @@
 
 
 HIGH_COUNT = 512
+COST = pl.CostEstimate(flops=1, bytes_accessed=1, transcendentals=0)
 BOTH = ("fsdp", "vocab")
 
 
@@ -56,10 +57,24 @@
     return [1 << k for k in range(size.bit_length() - 1)]
 
 
+def gate_kernel(*refs):
+    pass
+
+
 def after(x, *needed):
     if not needed:
         return x
-    return lax.optimization_barrier((x, needed))[0]
+    parts = x if isinstance(x, list) else [x]
+    anywhere = pl.BlockSpec(memory_space=pl.ANY)
+    outs = pl.pallas_call(
+        gate_kernel,
+        in_specs=[anywhere] * (len(parts) + len(needed)),
+        out_specs=[anywhere] * len(parts),
+        out_shape=[jax.ShapeDtypeStruct(part.shape, part.dtype) for part in parts],
+        input_output_aliases={i: i for i in range(len(parts))},
+        name="gate",
+    )(*parts, *needed)
+    return list(outs) if isinstance(x, list) else outs[0]
 
 
 def tree_sum(parts):
@@ -118,15 +133,6 @@
     return lax.all_to_all(x, "fsdp", 0, 0, tiled=True, axis_index_groups=groups)
 
 
-def in_rows(parts, near):
-    p = lax.axis_index("fsdp") % near
-    rows = parts[0].shape[0]
-    stacked = jnp.zeros((near * rows,) + parts[0].shape[1:], parts[0].dtype)
-    for k, part in enumerate(parts):
-        stacked = lax.dynamic_update_slice_in_dim(stacked, part, (p ^ k) * rows, 0)
-    return stacked
-
-
 def far_gather(x, near):
     return lax.all_gather(x, "fsdp", axis=0, tiled=True, axis_index_groups=far_groups(near))
 
@@ -142,13 +148,16 @@
     def entry(self, j):
         return lax.dynamic_index_in_dim(self.x, jnp.clip(j, 0, self.far - 1), 0, False)
 
+    def arrived(self):
+        return [self.up, self.down]
+
     def step(self, *needed):
         self.k += 1
         k, near, size = self.k, self.near, self.far * self.near
         send_up = self.entry(self.far - k + self.z)
         send_down = self.entry(self.z - self.far + k)
         if k > 1:
-            up, down = after([self.up, self.down], *needed)
+            up, down = after([self.up, self.down], *needed) if needed else (self.up, self.down)
             send_up, send_down = send_up + up, send_down + down
         sends = [send_up.astype(jnp.bfloat16), send_down.astype(jnp.bfloat16)]
         self.up = lax.ppermute(sends[0], "fsdp", [(i, i + near) for i in range(k * near)])
@@ -192,6 +201,60 @@
     grad = grad.reshape(-1, near, 2, rows, grad.shape[-1])
     send = lax.dynamic_index_in_dim(grad, 1 - core, 2, False).astype(jnp.bfloat16)
     return (lax.dynamic_index_in_dim(grad, core, 2, False), [send])
+
+
+def weight_kernel(counts, core_ref, *refs):
+    keep_ref, send_ref = refs[-2:]
+    step, first = pl.program_id(0), 0
+    rows = keep_ref.shape[1]
+    mine = core_ref[0] == 0
+    for i, count in enumerate(counts):
+
+        def put(grad_ref=refs[2 * i], input_ref=refs[2 * i + 1]):
+            product = lax.dot_general(
+                grad_ref[...],
+                input_ref[...],
+                (((0,), (0,)), ((), ())),
+                preferred_element_type=jnp.float32,
+            )
+            one, two = product[:rows], product[rows:]
+            keep_ref[0] = jnp.where(mine, one, two)
+            send_ref[0] = jnp.where(mine, two, one).astype(send_ref.dtype)
+
+        pl.when((step >= first) & (step < first + count))(put)
+        first += count
+
+
+def weight_sums(pairs, rows):
+    width = pairs[0][1].shape[1]
+    counts = [grad.shape[1] // (2 * rows) for grad, _ in pairs]
+    total = sum(counts)
+    specs, operands, first = [], [], 0
+    for (grad, given), count in zip(pairs, counts):
+        specs.append(
+            pl.BlockSpec(
+                (grad.shape[0], 2 * rows),
+                lambda i, _, first=first, count=count: (0, jnp.clip(i - first, 0, count - 1)),
+            )
+        )
+        specs.append(pl.BlockSpec(given.shape, lambda i, _: (0, 0)))
+        operands += [grad, given]
+        first += count
+    return pl.pallas_call(
+        functools.partial(weight_kernel, counts),
+        grid_spec=pltpu.PrefetchScalarGridSpec(
+            num_scalar_prefetch=1,
+            grid=(total,),
+            in_specs=specs,
+            out_specs=[pl.BlockSpec((1, rows, width), lambda i, _: (i, 0, 0))] * 2,
+        ),
+        out_shape=[
+            jax.ShapeDtypeStruct((total, rows, width), jnp.float32),
+            jax.ShapeDtypeStruct((total, rows, width), jnp.bfloat16),
+        ],
+        compiler_params=pltpu.CompilerParams(vmem_limit_bytes=40 * 1024 * 1024),
+        name="weight_sums",
+    )(lax.axis_index("vocab").astype(jnp.int32).reshape(1), *operands)
 
 
 def in_order(parts, near):
@@ -206,32 +269,19 @@
 
 
 def place_kernel(spans, blocks, order_ref, *refs):
-    count = len(refs) - len(spans) - 1
-    pieces, outs, sems = refs[:count], refs[count:-1], refs[-1]
+    pieces, outs = refs[: -len(spans)], refs[-len(spans) :]
     for i, piece in enumerate(pieces):
         for kz in range(blocks):
-            n = i * blocks + kz
-            block = order_ref[n]
-            for m, (first, last, start, rows) in enumerate(spans):
-
-                def copy(m=m, kz=kz, n=n, first=first, start=start, rows=rows, piece=piece):
-                    pltpu.make_async_copy(
-                        piece.at[kz, pl.ds(start, rows)], outs[m].at[block - first], sems.at[n, m]
-                    ).start()
-
-                pl.when((block >= first) & (block < last))(copy)
-    for i, piece in enumerate(pieces):
-        for kz in range(blocks):
-            n = i * blocks + kz
-            block = order_ref[n]
-            for m, (first, last, start, rows) in enumerate(spans):
-
-                def wait(m=m, kz=kz, n=n, first=first, start=start, rows=rows, piece=piece):
-                    pltpu.make_async_copy(
-                        piece.at[kz, pl.ds(start, rows)], outs[m].at[block - first], sems.at[n, m]
-                    ).wait()
-
-                pl.when((block >= first) & (block < last))(wait)
+            block = order_ref[i * blocks + kz]
+            for out, (first, last, start, rows) in zip(outs, spans):
+
+                def put(piece=piece, kz=kz, block=block, out=out, first=first, start=start, rows=rows):
+                    out[block - first] = piece[kz, start : start + rows]
+
+                if first == 0 and last == len(pieces) * blocks:
+                    put()
+                else:
+                    pl.when((block >= first) & (block < last))(put)
 
 
 def gather_pieces(line):
@@ -244,15 +294,14 @@
 
 
 def place_blocks(pieces, order, spans):
-    total, width = len(order), pieces[0].shape[-1]
+    width = pieces[0].shape[-1]
     return pl.pallas_call(
         functools.partial(place_kernel, spans, pieces[0].shape[0]),
         grid_spec=pltpu.PrefetchScalarGridSpec(
             num_scalar_prefetch=1,
             grid=(1,),
             in_specs=[pl.BlockSpec(memory_space=pltpu.VMEM)] * len(pieces),
-            out_specs=[pl.BlockSpec(memory_space=pl.ANY)] * len(spans),
-            scratch_shapes=[pltpu.SemaphoreType.DMA((total, len(spans)))],
+            out_specs=[pl.BlockSpec(memory_space=pltpu.VMEM)] * len(spans),
         ),
         out_shape=[
             jax.ShapeDtypeStruct((last - first, rows, width), pieces[0].dtype)
@@ -263,7 +312,8 @@
     )(jnp.stack(order).astype(jnp.int32), *pieces)
 
 
-def lookup_kernel(low_count, ids_ref, table_ref, out_ref, spread):
+def lookup_kernel(low_count, ids_ref, table_ref, *refs):
+    out_ref, spread = refs[-2:]
     width = table_ref.shape[0]
 
     @pl.when(pl.program_id(0) == 0)
@@ -284,7 +334,7 @@
     out_ref[0] = total.astype(out_ref.dtype)
 
 
-def lookup(table_t, ids):
+def lookup(table_t, ids, *needed):
     rows = table_t.shape[0]
     table_t = jnp.pad(table_t, ((0, -rows % 16), (0, 0)))
     width, vocab = table_t.shape
@@ -296,7 +346,8 @@
         in_specs=[
             pl.BlockSpec((1, 1, length), lambda i: (i, 0, 0)),
             pl.BlockSpec((width, vocab), lambda i: (0, 0)),
-        ],
+        ]
+        + [pl.BlockSpec(memory_space=pl.ANY)] * len(needed),
         out_specs=pl.BlockSpec((1, width, length), lambda i: (i, 0, 0)),
         out_shape=jax.ShapeDtypeStruct((blocks, width, length), jnp.bfloat16),
         scratch_shapes=[pltpu.VMEM((low_count * width, HIGH_COUNT), jnp.bfloat16)],
@@ -307,11 +358,12 @@
             transcendentals=0,
         ),
         name="lookup",
-    )(ids, table_t)
+    )(ids, table_t, *needed)
     return found[:, :rows]
 
 
-def spread_kernel(low_count, ids_ref, grad_ref, out_ref, lhs, total):
+def spread_kernel(low_count, ids_ref, grad_ref, *refs):
+    out_ref, lhs, total = refs[-3:]
     width = grad_ref.shape[1]
     step = pl.program_id(0)
 
@@ -339,7 +391,7 @@
             out_ref[:, span] = total[low * width : (low + 1) * width, :]
 
 
-def spread_add(grads, ids, vocab):
+def spread_add(grads, ids, vocab, *needed):
     rows = grads.shape[1]
     grads = jnp.pad(grads, ((0, 0), (0, -rows % 16), (0, 0)))
     width = grads.shape[1]
@@ -351,7 +403,8 @@
         in_specs=[
             pl.BlockSpec((1, 1, length), lambda i: (i, 0, 0)),
             pl.BlockSpec((1, width, length), lambda i: (i, 0, 0)),
-        ],
+        ]
+        + [pl.BlockSpec(memory_space=pl.ANY)] * len(needed),
         out_specs=pl.BlockSpec((width, vocab), lambda i: (0, 0)),
         out_shape=jax.ShapeDtypeStruct((width, vocab), jnp.float32),
         scratch_shapes=[
@@ -359,13 +412,9 @@
             pltpu.VMEM((low_count * width, HIGH_COUNT), jnp.float32),
         ],
         compiler_params=pltpu.CompilerParams(vmem_limit_bytes=40 * 1024 * 1024),
-        cost_estimate=pl.CostEstimate(
-            flops=2 * blocks * length * width * vocab,
-            bytes_accessed=4 * width * vocab + 2 * blocks * width * length,
-            transcendentals=0,
-        ),
+        cost_estimate=COST,
         name="spread_add",
-    )(ids, grads)
+    )(ids, grads, *needed)
     return summed[:rows]
 
 
@@ -415,7 +464,8 @@
     return powers * (1.0 / jnp.sum(powers, axis=-1, keepdims=True))
 
 
-def attend_kernel(lengths_ref, query_ref, key_ref, value_ref, out_ref):
+def attend_kernel(lengths_ref, query_ref, key_ref, value_ref, *refs):
+    out_ref = refs[-1]
     length = lengths_ref[pl.program_id(0)]
     live = lax.broadcasted_iota(jnp.int32, (1, key_ref.shape[0]), 1) < length
     for start in range(0, query_ref.shape[1], HEAD_DIM):
@@ -425,7 +475,7 @@
         out_ref[:, span] = context.astype(out_ref.dtype)
 
 
-def attend(qkv, lengths, seqs):
+def attend(qkv, lengths, seqs, *needed):
     rows, total = qkv.shape
     seq_len, width = rows // seqs, total // 3
     lanes = 2 * HEAD_DIM
@@ -439,21 +489,19 @@
         grid_spec=pltpu.PrefetchScalarGridSpec(
             num_scalar_prefetch=1,
             grid=(seqs, blocks),
-            in_specs=[part(0), part(1), part(2)],
+            in_specs=[part(0), part(1), part(2)]
+            + [pl.BlockSpec(memory_space=pl.ANY)] * len(needed),
             out_specs=pl.BlockSpec((seq_len, lanes), lambda s, j, _: (s, j)),
         ),
         out_shape=jax.ShapeDtypeStruct((rows, width), jnp.bfloat16),
         compiler_params=pltpu.CompilerParams(vmem_limit_bytes=40 * 1024 * 1024),
-        cost_estimate=pl.CostEstimate(
-            flops=4 * rows * seq_len * width,
-            bytes_accessed=2 * rows * (total + width),
-            transcendentals=rows * seq_len * width // HEAD_DIM,
-        ),
+        cost_estimate=COST,
         name="attend",
-    )(lengths, qkv, qkv, qkv)
-
-
-def attend_back_kernel(lengths_ref, query_ref, key_ref, value_ref, grad_ref, out_ref):
+    )(lengths, qkv, qkv, qkv, *needed)
+
+
+def attend_back_kernel(lengths_ref, query_ref, key_ref, value_ref, grad_ref, *refs):
+    out_ref = refs[-1]
     length = lengths_ref[pl.program_id(0)]
     step = pl.program_id(1)
     width = out_ref.shape[1] // 3
@@ -488,7 +536,7 @@
         out_ref[:, pl.ds(start, lanes)] = jnp.concatenate(pieces, 1).astype(out_ref.dtype)
 
 
-def attend_back(qkv, grad_context, lengths, seqs):
+def attend_back(qkv, grad_context, lengths, seqs, *needed):
     rows, total = qkv.shape
     seq_len, width = rows // seqs, total // 3
     lanes = 2 * HEAD_DIM
@@ -502,26 +550,35 @@
         grid_spec=pltpu.PrefetchScalarGridSpec(
             num_scalar_prefetch=1,
             grid=(seqs, blocks),
-            in_specs=[part(0), part(1), part(2), part(0)],
+            in_specs=[part(0), part(1), part(2), part(0)]
+            + [pl.BlockSpec(memory_space=pl.ANY)] * len(needed),
             out_specs=pl.BlockSpec((seq_len, total), lambda s, j, _: (s, 0)),
         ),
         out_shape=jax.ShapeDtypeStruct((rows, total), jnp.bfloat16),
         compiler_params=pltpu.CompilerParams(vmem_limit_bytes=40 * 1024 * 1024),
-        cost_estimate=pl.CostEstimate(
-            flops=10 * rows * seq_len * width,
-            bytes_accessed=2 * rows * (2 * total + width),
-            transcendentals=rows * seq_len * width // HEAD_DIM,
-        ),
+        cost_estimate=COST,
         name="attend_back",
-    )(lengths, qkv, qkv, qkv, grad_context)
-
-
-def head_kernel(rows_ref, table_ref, bias_ref, teach_ref, logits_ref, stats_ref):
+    )(lengths, qkv, qkv, qkv, grad_context, *needed)
+
+
+def teacher_rows(place_ref, parts, held):
+    which = place_ref[0] ^ pl.program_id(0)
+    for k, part_ref in enumerate(parts):
+
+        def hold(part_ref=part_ref):
+            held[...] = part_ref[...]
+
+        pl.when(which == k)(hold)
+    return held[...].astype(jnp.float32)
+
+
+def head_kernel(place_ref, rows_ref, table_ref, bias_ref, *refs):
+    parts, (logits_ref, stats_ref, held) = refs[:-3], refs[-3:]
     logits = (
         jnp.dot(rows_ref[...], table_ref[...], preferred_element_type=jnp.float32) + bias_ref[...]
     )
     logits_ref[...] = logits
-    teach = teach_ref[...].astype(jnp.float32)
+    teach = teacher_rows(place_ref, parts, held)
     student_top = jnp.max(logits, axis=-1, keepdims=True)
     student_total = jnp.sum(jnp.exp(logits - student_top), axis=-1, keepdims=True)
     teacher_top = jnp.max(teach, axis=-1, keepdims=True)
@@ -535,40 +592,41 @@
     stats_ref[0] = packed.T[:8]
 
 
-def head(rows, table_part, bias_part, teach, near):
+def head(place, rows, table_part, bias_part, teach_parts, near):
     count, width = rows.shape
     vocab = table_part.shape[1]
     block = count // near
+    whole = pl.BlockSpec((block, vocab), lambda i, _: (0, 0))
     return pl.pallas_call(
         head_kernel,
-        grid=(near,),
-        in_specs=[
-            pl.BlockSpec((block, width), lambda i: (i, 0)),
-            pl.BlockSpec((width, vocab), lambda i: (0, 0)),
-            pl.BlockSpec((1, vocab), lambda i: (0, 0)),
-            pl.BlockSpec((block, vocab), lambda i: (i, 0)),
-        ],
-        out_specs=[
-            pl.BlockSpec((block, vocab), lambda i: (i, 0)),
-            pl.BlockSpec((1, 8, block), lambda i: (i, 0, 0)),
-        ],
+        grid_spec=pltpu.PrefetchScalarGridSpec(
+            num_scalar_prefetch=1,
+            grid=(near,),
+            in_specs=[
+                pl.BlockSpec((block, width), lambda i, _: (i, 0)),
+                pl.BlockSpec((width, vocab), lambda i, _: (0, 0)),
+                pl.BlockSpec((1, vocab), lambda i, _: (0, 0)),
+            ]
+            + [whole] * near,
+            out_specs=[
+                pl.BlockSpec((block, vocab), lambda i, _: (i, 0)),
+                pl.BlockSpec((1, 8, block), lambda i, _: (i, 0, 0)),
+            ],
+            scratch_shapes=[pltpu.VMEM((block, vocab), jnp.bfloat16)],
+        ),
         out_shape=[
             jax.ShapeDtypeStruct((count, vocab), jnp.float32),
             jax.ShapeDtypeStruct((near, 8, block), jnp.float32),
         ],
-        compiler_params=pltpu.CompilerParams(vmem_limit_bytes=48 * 1024 * 1024),
-        cost_estimate=pl.CostEstimate(
-            flops=2 * count * width * vocab,
-            bytes_accessed=count * vocab * 6 + 2 * width * vocab,
-            transcendentals=2 * count * vocab,
-        ),
+        compiler_params=pltpu.CompilerParams(vmem_limit_bytes=56 * 1024 * 1024),
+        cost_estimate=COST,
         name="head",
-    )(rows, table_part, bias_part, teach)
-
-
-def head_back_kernel(
-    logits_ref, teach_ref, stats_ref, scale_ref, table_ref, grad_ref, rows_ref, bias_ref, loss_ref
-):
+    )(place, rows, table_part, bias_part, *teach_parts)
+
+
+def head_back_kernel(place_ref, logits_ref, stats_ref, scale_ref, table_ref, *refs):
+    parts, (grad_ref, rows_ref, bias_ref, loss_ref, held) = refs[:-5], refs[-5:]
+    teach = teacher_rows(place_ref, parts, held)
     step = pl.program_id(0)
     stats = stats_ref[:, 0]
     tops, totals, teacher_tops, teacher_totals, crosses = (stats[:, i] for i in range(5))
@@ -587,7 +645,7 @@
     grad = (
         (
             jnp.exp(logits_ref[...] - packed[:, 0:1])
-            - jnp.exp(teach_ref[...].astype(jnp.float32) - packed[:, 1:2])
+            - jnp.exp(teach - packed[:, 1:2])
         )
         * packed[:, 2:3]
     ).astype(jnp.bfloat16)
@@ -603,45 +661,54 @@
     bias_ref[...] += jnp.sum(grad.astype(jnp.float32), axis=0, keepdims=True)
 
 
-def head_back(logits, teach, stats, scale, table_part, near):
+def head_back(place, logits, stats, scale, table_part, teach_parts, near):
     count, vocab = logits.shape
     width = table_part.shape[0]
     block = count // near
     members = stats.shape[0]
+    whole = pl.BlockSpec((block, vocab), lambda i, _: (0, 0))
     return pl.pallas_call(
         head_back_kernel,
-        grid=(near,),
-        in_specs=[
-            pl.BlockSpec((block, vocab), lambda i: (i, 0)),
-            pl.BlockSpec((block, vocab), lambda i: (i, 0)),
-            pl.BlockSpec((members, 1, 8, block), lambda i: (0, i, 0, 0)),
-            pl.BlockSpec((1, 1, block), lambda i: (i, 0, 0)),
-            pl.BlockSpec((width, vocab), lambda i: (0, 0)),
-        ],
-        out_specs=[
-            pl.BlockSpec((block, vocab), lambda i: (i, 0)),
-            pl.BlockSpec((block, width), lambda i: (i, 0)),
-            pl.BlockSpec((1, vocab), lambda i: (0, 0)),
-            pl.BlockSpec((1, 1, block), lambda i: (i, 0, 0)),
-        ],
+        grid_spec=pltpu.PrefetchScalarGridSpec(
+            num_scalar_prefetch=1,
+            grid=(near,),
+            in_specs=[
+                pl.BlockSpec((block, vocab), lambda i, _: (i, 0)),
+                pl.BlockSpec((members, 1, 8, block), lambda i, _: (0, i, 0, 0)),
+                pl.BlockSpec((1, 1, block), lambda i, _: (i, 0, 0)),
+                pl.BlockSpec((width, vocab), lambda i, _: (0, 0)),
+            ]
+            + [whole] * near,
+            out_specs=[
+                pl.BlockSpec((block, vocab), lambda i, _: (i, 0)),
+                pl.BlockSpec((block, width), lambda i, _: (i, 0)),
+                pl.BlockSpec((1, vocab), lambda i, _: (0, 0)),
+                pl.BlockSpec((1, 1, block), lambda i, _: (i, 0, 0)),
+            ],
+            scratch_shapes=[pltpu.VMEM((block, vocab), jnp.bfloat16)],
+        ),
         out_shape=[
             jax.ShapeDtypeStruct((count, vocab), jnp.bfloat16),
             jax.ShapeDtypeStruct((count, width), jnp.float32),
             jax.ShapeDtypeStruct((1, vocab), jnp.float32),
             jax.ShapeDtypeStruct((near, 1, block), jnp.float32),
         ],
-        compiler_params=pltpu.CompilerParams(vmem_limit_bytes=48 * 1024 * 1024),
-        cost_estimate=pl.CostEstimate(
-            flops=2 * count * width * vocab,
-            bytes_accessed=count * vocab * 8 + 2 * width * vocab,
-            transcendentals=2 * count * vocab,
-        ),
+        compiler_params=pltpu.CompilerParams(vmem_limit_bytes=56 * 1024 * 1024),
+        cost_estimate=COST,
         name="head_back",
-    )(logits, teach, stats, scale, table_part)
+    )(place, logits, stats, scale, table_part, *teach_parts)
 
 
 def layer_forward(
-    embedded, lengths, seqs, weight_qkv, weight_out, weight_up, weight_down_after, parts
+    embedded,
+    lengths,
+    seqs,
+    weight_qkv,
+    weight_out,
+    weight_up,
+    weight_down_after,
+    parts,
+    before_attention,
 ):
     (
         gain_embed,
@@ -660,14 +727,14 @@
     normed_low = normed.astype(jnp.bfloat16)
     qkv_bias = jnp.concatenate([bias_query, jnp.zeros_like(bias_query), bias_value])
     qkv_low = (project(normed_low, weight_qkv) + qkv_bias).astype(jnp.bfloat16)
-    context_low = attend(qkv_low, lengths, seqs)
+    context_low = attend(qkv_low, lengths, seqs, *before_attention)
     first_sum = normed + project(context_low, weight_out) + bias_out
     first_out = layer_norm(first_sum, gain_attn, shift_attn)
     first_low = first_out.astype(jnp.bfloat16)
     pre_act = project(first_low, weight_up) + bias_hidden
     share = 0.5 + 0.5 * lax.erf(pre_act * math.sqrt(0.5))
     act_low = (pre_act * share).astype(jnp.bfloat16)
-    weight_down = weight_down_after(first_low)
+    weight_down = weight_down_after()
     slope = share + pre_act * jnp.exp(-0.5 * pre_act * pre_act) * (1.0 / math.sqrt(2.0 * math.pi))
     second_sum = first_out + project(act_low, weight_down) + bias_down
     final = layer_norm(second_sum, gain_ffn, shift_ffn)
@@ -730,32 +797,37 @@
         second_sum, gain_ffn, shift_ffn, grad_final
     )
     grad_down_low = grad_second.astype(jnp.bfloat16)
-    sums.begin("down", weight_grad(grad_down_low, act_low), down_rows)
+    sums.begin("down", [(grad_down_low, act_low)], down_rows)
     grad_pre_low = (
-        project_back(after(grad_down_low, *sums.sent("down")), weight_down) * slope
+        project_back(grad_down_low, weight_down) * slope
     ).astype(jnp.bfloat16)
     grad_pre_low = lax.optimization_barrier(grad_pre_low)
-    sums.begin("up", weight_grad(grad_pre_low, first_low), stack_rows)
-    grad_first = grad_second + project_back(after(grad_pre_low, *sums.sent("up")), weight_up)
+    sums.begin("up", [(grad_pre_low, first_low)], stack_rows)
+    grad_first = grad_second + project_back(grad_pre_low, weight_up)
     grad_first_sum, grad_gain_attn, grad_shift_attn = norm_back(
         first_sum, gain_attn, shift_attn, grad_first
     )
     grad_out_low = grad_first_sum.astype(jnp.bfloat16)
     grad_context_low = project_back(grad_out_low, weight_out).astype(jnp.bfloat16)
-    out_grad = weight_grad(grad_out_low, context_low)
-    sums.in_plane(("down", "up"), grad_context_low)
+    sums.in_plane(("down", "up"))
     line_sends = line.step(grad_context_low) if line else []
     grad_qkv_low = attend_back(
-        qkv_low, after(grad_context_low, *sums.sent("up"), *line_sends), lengths, seqs
+        qkv_low, grad_context_low, lengths, seqs, *sums.sent("up"), *line_sends
     )
     grad_normed = grad_first_sum + project_back(grad_qkv_low, weight_qkv)
     grad_embed, grad_gain_embed, grad_shift_embed = norm_back(
         embedded, gain_embed, shift_embed, grad_normed
     )
     embed_t = embed_columns(grad_embed)
-    line_sends = line.step(embed_t) if line else []
-    qkv_grad = weight_grad(after(grad_qkv_low, embed_t, *line_sends), normed_low)
-    sums.begin("attention", jnp.concatenate([qkv_grad, out_grad], 0), stack_rows)
+    sums.begin(
+        "attention",
+        [(grad_qkv_low, normed_low), (grad_out_low, context_low)],
+        stack_rows,
+    )
+    sums.hold("attention", *(line.arrived() if line else []))
+    sums.arrive(("down", "up"))
+    if line:
+        line.step(*sums.sent("attention"))
     vectors_grad = jnp.concatenate(
         [
             grad_gain_embed,
@@ -779,8 +851,17 @@
         self.near, self.staged, self.width = near, far == 4, width
         self.state = {}
 
-    def begin(self, name, grad, rows):
-        self.state[name] = begin_pair_sum(grad, rows, self.near) if self.staged else (grad, [])
+    def begin(self, name, pairs, rows):
+        if not self.staged:
+            grads = [weight_grad(grad, given) for grad, given in pairs]
+            self.state[name] = (jnp.concatenate(grads, 0), [])
+        elif pairs[0][0].shape[1] % (2 * rows) or 2 * rows % 128:
+            grads = [weight_grad(grad, given) for grad, given in pairs]
+            self.state[name] = begin_pair_sum(jnp.concatenate(grads, 0), rows, self.near)
+        else:
+            keep, send = weight_sums(pairs, rows)
+            shape = (-1, self.near) + keep.shape[1:]
+            self.state[name] = (keep.reshape(shape), [send.reshape(shape)])
 
     def sent(self, name):
         return self.state[name][1] if self.staged else []
@@ -791,35 +872,39 @@
         ]
         return parts[0] if len(parts) == 1 else jnp.concatenate(parts, -2)
 
-    def in_plane(self, names, *needed):
+    def in_plane(self, names):
         if not self.staged:
             return
         p = lax.axis_index("fsdp") % self.near
-        owns, sends = [], [[] for _ in range(1, self.near)]
+        sends = [[] for _ in range(self.near)]
         for name in names:
             keep, pair_sends = self.state[name]
-            arrived = after(swap(pair_sends[0], "vocab", 1), *needed)
-            keep = keep + arrived.astype(jnp.float32)
-            owns.append(self.narrow(lax.dynamic_index_in_dim(keep, p, 1, False)))
-            for k in range(1, self.near):
-                send = lax.dynamic_index_in_dim(keep, p ^ k, 1, False).astype(jnp.bfloat16)
-                sends[k - 1].append(self.narrow(send).reshape(-1, self.width))
-        sends = [parts[0] if len(parts) == 1 else jnp.concatenate(parts, 0) for parts in sends]
-        for name, own in zip(names, owns):
+            arrived = swap(pair_sends[0], "vocab", 1)
+            for k in range(self.near):
+                part = lax.dynamic_index_in_dim(keep, p ^ k, 1, False)
+                part = part + lax.dynamic_index_in_dim(arrived, p ^ k, 1, False).astype(jnp.float32)
+                part = part.astype(jnp.bfloat16) if k else part
+                sends[k].append(self.narrow(part).reshape(-1, self.width))
+        own, *sends = [
+            parts[0] if len(parts) == 1 else jnp.concatenate(parts, 0) for parts in sends
+        ]
+        for name in names:
             self.state[name] = (own, sends)
 
-    def plane_totals(self, names, *needed):
+    def hold(self, name, *needed):
+        if self.staged:
+            keep, sends = self.state[name]
+            self.state[name] = (keep, after(sends, *needed))
+
+    def arrive(self, names):
+        if not self.staged:
+            return []
         sends = self.state[names[0]][1]
-        arrived = after([swap(send, "fsdp", k) for k, send in enumerate(sends, 1)], *needed)
-        totals, start = [], 0
-        for name in names:
-            own = self.state[name][0]
-            count = own.shape[0] * own.shape[1]
-            totals.append(
-                added(own, [part[start : start + count].reshape(own.shape) for part in arrived])
-            )
-            start += count
-        return totals
+        self.arrived = [swap(send, "fsdp", k) for k, send in enumerate(sends, 1)]
+        return self.arrived
+
+    def plane_total(self, name, arrived):
+        return added(self.state[name][0], arrived)
 
 
 def adam(weight_matrix, grad, first, second, rate):
@@ -915,25 +1000,29 @@
     table_low = table_t.astype(jnp.bfloat16)
     half = size * own_seqs
     table_blocks = table_low.reshape(columns, near, part).transpose(1, 0, 2)
-    def teacher_parts(*needed):
-        given = after(teacher, *needed)
-        return near_exchange(lambda q: lax.dynamic_slice_in_dim(given, q * part, part, 1), near)
-
+    teacher_blocks = [
+        lax.dynamic_slice_in_dim(teacher, (p ^ k) * part, part, 1) for k in range(near)
+    ]
+    teach_parts = teacher_blocks[:1] + [
+        swap(block, "fsdp", k) for k, block in enumerate(teacher_blocks[1:], 1)
+    ]
     if far == 4:
         own_stack = after(own_stack, all_ids)
         stack_line = [swap(own_stack, "fsdp", k * near) for k in range(1, far)]
-        near_table = exchange(after(table_blocks, all_ids), near_groups(near))
-        found = lookup(table_t, after(local_ids, own_stack))
-        near_table = after(near_table, found).reshape(near * columns, part)
-        own_found = found[:half] + swap(found[half:], "vocab", 1)
-        stack_line = jnp.stack([own_stack] + after(stack_line, found))
+        near_table = exchange(table_blocks, near_groups(near)).reshape(near * columns, part)
+        other_found = lookup(table_t, local_ids[half:], own_stack)
+        swapped = swap(other_found, "vocab", 1)
+        own_found = lookup(table_t, local_ids[:half], other_found, near_table)
+        stack_line = jnp.stack([own_stack] + after(stack_line, own_found))
+        own_found = own_found + swapped
         stack_pieces = gather_pieces(stack_line)
-        own_found = after(own_found, stack_line, near_table)
         tokens_t = exchange(own_found.reshape(size, own_seqs, columns, seq_len), None)
-        own_down = after(own_down, own_found)
         down_line = exchange(
             after(jnp.broadcast_to(own_down[None], (far,) + own_down.shape), tokens_t),
             far_groups(near),
+        )
+        own_blocks = exchange(
+            jnp.broadcast_to(down_line[None], (near,) + down_line.shape), near_groups(near)
         )
         stack_others = [[swap(piece, "vocab", 1) for piece in half] for half in stack_pieces]
         own_blocks = exchange(
@@ -945,7 +1034,7 @@
             near_groups(near),
         )
         other_blocks = swap(own_blocks, "vocab", 1)
-        teach_parts = teacher_parts(stack_pieces[0][3], stack_pieces[1][3])
+        before_attention = [own_blocks]
         qkv_blocks = 3 * width // stack_rows
         attention_blocks = 4 * width // stack_rows
         weight_qkv, weight_out, weight_up, small = place_blocks(
@@ -968,8 +1057,8 @@
         weight_out = weight_out.reshape(-1, width)
         weight_up = weight_up.reshape(-1, width)
 
-        def weight_down_after(*needed):
-            arrived = after([own_blocks, other_blocks], *needed)
+        def weight_down_after():
+            arrived = [own_blocks, other_blocks]
             (weight_down,) = place_blocks(
                 [blocks.reshape((size,) + own_down.shape) for blocks in arrived],
                 [
@@ -983,7 +1072,7 @@
             return weight_down.reshape(-1, units)
 
     else:
-        teach_parts = teacher_parts()
+        before_attention = []
         stack_all = lax.all_gather(own_stack, BOTH, axis=0)
         dense_stack = stack_all[:, :stack_rows].reshape(-1, width)
         small = stack_all[:, stack_rows:]
@@ -992,7 +1081,7 @@
         weight_up = dense_stack[4 * width :]
         weight_down = lax.all_gather(own_down, BOTH, axis=0, tiled=True)
 
-        def weight_down_after(*needed):
+        def weight_down_after():
             return weight_down
 
         near_table = exchange(table_blocks, near_groups(near)).reshape(near * columns, part)
@@ -1013,9 +1102,16 @@
     seq_start = place * pair_seqs + core * own_seqs
     own_lengths = lax.dynamic_slice_in_dim(lengths, seq_start, own_seqs)
     final, saved, weight_down = layer_forward(
-        embedded, own_lengths, own_seqs, weight_qkv, weight_out, weight_up, weight_down_after, parts
-    )
-    teach = in_rows(teach_parts, near)
+        embedded,
+        own_lengths,
+        own_seqs,
+        weight_qkv,
+        weight_out,
+        weight_up,
+        weight_down_after,
+        parts,
+        before_attention,
+    )
     own_pos = lax.dynamic_slice_in_dim(masked_pos, seq_start, own_seqs, 0)
     flat_rows = (jnp.arange(own_seqs, dtype=jnp.int32)[:, None] * seq_len + own_pos).reshape(-1)
     picked = jnp.take(final.reshape(own_rows, width), flat_rows, axis=0).astype(jnp.bfloat16)
@@ -1023,21 +1119,19 @@
     rows = in_order(near_exchange(lambda q: rows, near), near).reshape(-1, width)
 
     bias_part = lax.dynamic_slice_in_dim(head_bias, p * part, part)
-    output_logits, stats = head(rows, table_part, bias_part[None], teach, near)
-    stats = jnp.stack(
-        [stats]
-        + [
-            lax.ppermute(stats, BOTH, [(i, i ^ k) for i in range(2 * size)])
-            for k in range(1, 2 * near)
-        ]
-    )
+    own_place = p.astype(jnp.int32).reshape(1)
+    output_logits, stats = head(
+        own_place, rows, table_part, bias_part[None], teach_parts, near
+    )
+    stats = jnp.stack([stats, swap(stats, "vocab", 1)])
+    stats = jnp.concatenate(near_exchange(lambda q: stats, near), 0)
     group_start = (place - p) * pair_seqs
     group_pos = lax.dynamic_slice_in_dim(masked_pos, group_start, near * pair_seqs, 0)
     group_lengths = lax.dynamic_slice_in_dim(lengths, group_start, near * pair_seqs)
     group_valid = (group_pos < group_lengths[:, None]).astype(jnp.float32).reshape(near, 1, -1)
     count = jnp.sum((masked_pos < lengths[:, None]).astype(jnp.float32))
     grad_logits, rows_grad, bias_part_grad, divergence = head_back(
-        output_logits, teach, stats, group_valid / count, table_part, near
+        own_place, output_logits, stats, group_valid / count, table_part, teach_parts, near
     )
     group_loss = jnp.sum(divergence * group_valid) / (2 * near)
     rows_grad = halve(rows_grad.reshape(near, 2, -1, width).transpose(1, 0, 2, 3), "vocab", 1)
@@ -1051,17 +1145,19 @@
         .add(own_rows_grad)
     )
 
-    bias_part_grad = sum_far(after(bias_part_grad[0], *rows_sends), near)
-    bias_grad = in_order(near_exchange(lambda q: bias_part_grad, near), near).reshape(-1)
+    bias_full = lax.dynamic_update_slice_in_dim(
+        jnp.zeros((vocab_dev,), jnp.float32), bias_part_grad[0], p * part, 0
+    )
     head_grad = lax.dot_general(
         rows,
-        after(grad_logits, *rows_sends),
+        grad_logits,
         (((0,), (0,)), ((), ())),
         preferred_element_type=jnp.float32,
     ).reshape(far, near, columns, part)
     if far == 4:
-        line = FarLine(after(head_grad, bias_grad), near)
-        grad_final = after(grad_final, *line.step())
+        line = FarLine(head_grad, near)
+        line_sends = line.step()
+        grad_final = after(grad_final, *line_sends)
     else:
         line = None
 
@@ -1090,27 +1186,36 @@
 
     embed_t = lax.all_to_all(embed_t, "fsdp", 0, 0, tiled=True).reshape(half, columns, seq_len)
     if far == 4:
-        down_plane, up_plane = sums.plane_totals(("down", "up"), *sums.sent("attention"))
-        sums.in_plane(("attention",), up_plane)
+        first_plane = sums.plane_total("up", sums.arrived)
+        down_plane = first_plane[: far * (units // width) * down_rows].reshape(far, -1, width)
+        up_plane = first_plane[far * (units // width) * down_rows :].reshape(-1, stack_rows, width)
+        sums.in_plane(("attention",))
         attention_sends = sums.sent("attention")
-        embed_t = after(embed_t, *attention_sends)
         other_t = swap(embed_t, "vocab", 1)
-        vectors_grad = vectors_grad + swap(after(vectors_grad, *attention_sends), "vocab", 1)
-        head_grad = line.total(*attention_sends)
-        blocks = near_exchange(lambda q: lax.dynamic_index_in_dim(head_grad, q, 0, False), near)
-        token_grad = spread_add(after(embed_t, head_grad, other_t), local_ids[:half], vocab_dev)
-        (attention_plane,) = sums.plane_totals(("attention",), token_grad)
+        token_grad = spread_add(embed_t, local_ids[:half], vocab_dev, other_t, *attention_sends)
+        head_grad = line.total(token_grad)
+        blocks_sent = [
+            lax.dynamic_index_in_dim(head_grad, p ^ k, 0, False) for k in range(near)
+        ]
+        blocks = [swap(block, "fsdp", k) for k, block in enumerate(blocks_sent[1:], 1)]
+        attention_plane = sums.plane_total(
+            "attention", after(sums.arrive(("attention",)), token_grad)
+        ).reshape(-1, stack_rows, width)
         own = jnp.concatenate(
             [jnp.concatenate([attention_plane, up_plane], 0), down_plane], 1
         )
         far_low = own.astype(jnp.bfloat16)
         arrived = exchange(far_low, far_groups(near))
-        token_grad = token_grad + spread_add(
-            after(other_t, far_low), local_ids[half:], vocab_dev
-        )
-        vectors_grad = tree_sum(near_exchange(lambda q: after(vectors_grad, far_low), near))
-        vectors_far = [swap(vectors_grad, "fsdp", k * near) for k in range(1, far)]
-        vectors_grad = tree_sum([vectors_grad] + after(vectors_far, token_grad))
+        last_grad = spread_add(
+            other_t, local_ids[half:], vocab_dev, far_low, *blocks_sent
+        )
+        blocks = blocks_sent[:1] + after(blocks, last_grad)
+        token_grad = token_grad + last_grad
+        vectors_grad = after(vectors_grad, far_low)
+        vectors_grad = vectors_grad + swap(vectors_grad, "vocab", 1)
+        small_sums = jnp.concatenate([bias_full, vectors_grad])
+        small_sums = tree_sum(near_exchange(lambda q: small_sums, near))
+        small_sums = sum_far(small_sums, near)
         z = place // near
         other = lax.broadcasted_iota(jnp.int32, (far, 1, 1), 0) != z
         total = jnp.sum(jnp.where(other, arrived.astype(jnp.float32), own), axis=0)
@@ -1122,7 +1227,10 @@
     else:
         embed_t = jnp.concatenate([embed_t, swap(embed_t, "vocab", 1)], 0)
         token_grad = spread_add(embed_t, local_ids, vocab_dev)
-        vectors_grad = sum_all(vectors_grad, near)
+        vectors_grad = vectors_grad + swap(vectors_grad, "vocab", 1)
+        small_sums = jnp.concatenate([bias_full, vectors_grad])
+        small_sums = tree_sum(near_exchange(lambda q: small_sums, near))
+        small_sums = sum_far(small_sums, near)
         head_grad = far_reduce(head_grad, near)
         blocks = near_exchange(lambda q: lax.dynamic_index_in_dim(head_grad, q, 0, False), near)
         stack_grad = [sums.state[name][0] for name in ("attention", "up")]
@@ -1132,6 +1240,7 @@
         down_total = lax.psum_scatter(
             sums.state["down"][0], BOTH, scatter_dimension=0, tiled=True
         )
+    bias_grad, vectors_grad = small_sums[:vocab_dev], small_sums[vocab_dev:]
     head_grad_t = jnp.concatenate(list(in_order(blocks, near)), 1).astype(jnp.float32)
     table_total = head_grad_t + token_grad
     pos_total = jnp.sum(embed_t.astype(jnp.float32), axis=0)

time: 659 us -> 632 us (0.959)
  waiting for transfers between devices: 125 us -> 94.9 us
  Pallas kernels: 137 us -> 147 us
  matrix products: 59.5 us -> 50.1 us
    all_to_all x5, waiting for transfers between devices: 36.3 us -> 2.73 us  [exchange(): return lax.all_to_all(x, 'fsdp', 0, 0, tiled=True, axis_index_groups=groups)]
    ppermute x45 -> x49, waiting for transfers between devices: 46.3 us -> 72 us  [swap(): return lax.ppermute(x, axis, [(i, i ^ bit) for i in range(size)])]
    ppermute x18 -> x12, starting transfers between devices: 21.2 us -> 40.7 us  [near_exchange(): lax.ppermute(take(p ^ k), 'fsdp', [(i, i ^ k) for i in range(size)])]
    ppermute x3, waiting for transfers between devices: 17.8 us -> 0.01 us  [step(): lax.ppermute(sends[1], 'fsdp', [(i, i - near) for i in range(size - k * n...]
    pallas_call x2 -> x16, Pallas kernels: 27.8 us -> 41.4 us  [the longest x1 16.6 us: head_back(): pl.pallas_call(head_back_kernel, grid_spec=pltpu.PrefetchScalarGridSpec(n...]
    unnamed x221 -> x314, local copies, waits for them, and re-layouts: 15.5 us -> 26.9 us
    ppermute x7 -> x0, waiting for transfers between devices: 8.09 us -> none  [local(): lax.ppermute(stats, BOTH, [(i, i ^ k) for i in range(2 * size)])]
    concatenate x1, other arithmetic: 7.95 us -> 0.01 us  [local(): small_sums = jnp.concatenate([bias_full, vectors_grad])]
  transfers between devices with their start and end apart: 84 -> 75, of which waited for: 24 -> 22; matrix products, arithmetic and copies ran while one was open for 29% -> 26% of each run, Pallas kernels for 17% -> 18%
where the time goes in v3:
time: 632 us; the launch traced here: 621 us
  Pallas kernels  147 us (23%)
  starting transfers between devices  136 us (22%)
  other arithmetic  100 us (16%)
  waiting for transfers between devices  94.9 us (15%)
  local copies, waits for them, and re-layouts  65.4 us (10%)
  matrix products  50.1 us (8%)
  between operations  27 us (4%)
    ppermute x49, waiting for transfers between devices, swap(): return lax.ppermute(x, axis, [(i, i ^ bit) for i in range(size)])  72 us
    ppermute x12, starting transfers between devices, near_exchange(): lax.ppermute(take(p ^ k), 'fsdp', [(i, i ^ k) for i in range(size)])  40.7 us
    ppermute x49, starting transfers between devices, swap(): return lax.ppermute(x, axis, [(i, i ^ bit) for i in range(size)])  38.4 us
    pallas_call x2, Pallas kernels, spread_add(): pl.pallas_call(functools.partial(spread_kernel, low_count), grid=(blocks,...  32.2 us
    pallas_call x2, Pallas kernels, lookup(): pl.pallas_call(functools.partial(lookup_kernel, low_count), grid=(blocks,...  31.6 us
    unnamed x314, local copies, waits for them, and re-layouts  26.9 us
    all_to_all x5, starting transfers between devices, exchange(): return lax.all_to_all(x, 'fsdp', 0, 0, tiled=True, axis_index_groups=groups)  25.4 us
    pallas_call x1, Pallas kernels, attend_back(): pl.pallas_call(attend_back_kernel, grid_spec=pltpu.PrefetchScalarGridSpec...  17.3 us
  transfers between devices with their start and end apart: 75, of which 22 were waited for; matrix products, arithmetic and copies ran while one was open for 26% of the time, Pallas kernels for 18%

profile of v3, /device:TPU:0, one launch (start us, length us, event | category | flops | bytes accessed | tf_op | source)
XLA Modules:
  0.0 621.1 jit_solution(4860596076377866201)
XLA Ops:
  8.5 8.3 %all-to-all-start = ((s32[16,2,512]{2,1,0:T(2,128)}), s32[16,2,512]{2,1,0:T(2,128)S(1)}, u32[]{:S(2)}, u32[]{:S(2)}) async-start(s32[16,2,512]{2,1,0:T(2,128)} %broadcast_in_dim.68), calls=%async_computation | async-start | bytes 131072 | tf_op jit(solution)/shard_map/all_to_all | solution.py:965
  38.4 16.1 %lookup.2.refs_0_ = bf16[16,48,512]{2,1,0:T(8,128)(2,1)} custom-call(s32[16,1,512]{2,1,0:T(1,128)S(1)} %get-tuple-element.189.ids_ref, f32[48,15360]{1,0:T(8,128)S(1)} %bitcast.347, bf16[240,768]{1,0:T(8,128)(2,1)S(1)} %copy-done.12), custom_call_target="tpu_custom_call" | custom-call | flops 12079595520 | bytes 3735552 | tf_op jit(solution)/shard_map/lookup/pallas_call | solution.py:343
  54.5 15.5 %lookup.3.refs_3_ = bf16[16,48,512]{2,1,0:T(8,128)(2,1)S(1)} custom-call(s32[16,1,512]{2,1,0:T(1,128)S(1)} %get-tuple-element.190.ids_ref, f32[48,15360]{1,0:T(8,128)S(1)} %bitcast.348, bf16[16,48,512]{2,1,0:T(8,128)(2,1)} %lookup.2.refs_0_, bf16[192,3840]{1,0:T(8,128)(2,1)} %bitcast.6.refs_1_), custom_call_target="tpu_custom_call" | custom-call | flops 12079595520 | bytes 3735552 | tf_op jit(solution)/shard_map/lookup/pallas_call | solution.py:343
  73.0 7.5 %all-to-all-start.2 = ((bf16[16,1,48,512]{3,2,1,0:T(8,128)(2,1)}), bf16[16,1,48,512]{3,2,1,0:T(8,128)(2,1)}, u32[]{:S(2)}, u32[]{:S(2)}) async-start(bf16[16,1,48,512]{3,2,1,0:T(8,128)(2,1)} %add_bitcast_fusion), calls=%async_computation.2 | async-start | bytes 1572864 | tf_op jit(solution)/shard_map/all_to_all | solution.py:133
  89.1 19.0 %collective-permute-done.8.refs_6_ = bf16[2,240,768]{2,1,0:T(8,128)(2,1)S(1)} collective-permute-done((bf16[2,240,768]{2,1,0:T(8,128)(2,1)S(1)}, bf16[2,240,768]{2,1,0:T(8,128)(2,1)S(1)}, u32[]{:S(2)}, u32[]{:S(2)}) %collective-permute-start.8) | collective-permute-done | bytes 737312 | tf_op jit(solution)/shard_map/ppermute | solution.py:49
  111.4 14.6 %collective-permute-done.4.refs_1_ = bf16[2,240,768]{2,1,0:T(8,128)(2,1)} collective-permute-done((bf16[2,240,768]{2,1,0:T(8,128)(2,1)S(1)}, bf16[2,240,768]{2,1,0:T(8,128)(2,1)}, u32[]{:S(2)}, u32[]{:S(2)}) %collective-permute-start.4) | collective-permute-done | bytes 737312 | tf_op jit(solution)/shard_map/ppermute | solution.py:49
  135.2 5.9 collective-permute-done.9.refs_7_.refs_2_
  143.3 5.3 constant_dynamic-slice_fusion.2
  151.5 4.7 all-to-all-start.4
  164.7 9.3 %place.2 = (bf16[12,192,768]{2,1,0:T(8,128)(2,1)}, bf16[4,192,768]{2,1,0:T(8,128)(2,1)S(1)}, bf16[16,192,768]{2,1,0:T(8,128)(2,1)}, bf16[32,48,768]{2,1,0:T(8,128)(2,1)}) custom-call(s32[32]{0:T(128)S(1)} %stack.292.order_ref, bf16[2,240,768]{2,1,0:T(8,128)(2,1)S(1)} %pad_maximum_fusion.6.refs_0_, bf16[2,240,768]{2,1,0:T(8,128)(2,1)} %collective-permute-done.4.refs_1_, ...), custom_call_target="tpu_custom_call" | custom-call | tf_op jit(solution)/shard_map/place/pallas_call | solution.py:298
  185.2 4.7 fusion.8.query_ref.key_ref.value_ref
  189.9 12.0 %attend.1.refs_3_ = bf16[512,768]{1,0:T(8,128)(2,1)S(1)} custom-call(s32[1]{0:T(128)} %dynamic_slice.169.lengths_ref, bf16[512,2304]{1,0:T(8,128)(2,1)S(1)} %fusion.8.query_ref.key_ref.value_ref, bf16[512,2304]{1,0:T(8,128)(2,1)S(1)} %fusion.8.query_ref.key_ref.value_ref, bf16[512,2304]{1,0:T(8,128)(2,1)S(1)} %fusion.8.query_ref.key_ref.value_ref, ...), custom_call_target="tpu_custom_call" | custom-call | flops 1 | bytes 1 | tf_op jit(solution)/shard_map/attend/pallas_call | solution.py:487
  203.7 4.8 multiply_convert_fusion
  222.3 27.7 %collective-permute-start.22 = (bf16[160,768]{1,0:T(8,128)(2,1)S(1)}, bf16[160,768]{1,0:T(8,128)(2,1)}, u32[]{:S(2)}, u32[]{:S(2)}) collective-permute-start(bf16[160,768]{1,0:T(8,128)(2,1)S(1)} %bitcast.390), channel_id=1, source_target_pairs={{0,2},{2,0},{4,6},{6,4},{8,10},{10,8},{12,14},{14,12},{16,18},{18,... | collective-permute-start | bytes 737288 | tf_op jit(solution)/shard_map/ppermute | solution.py:118
  251.5 4.8 collective-permute-done.22
  269.4 15.5 %head.1 = (f32[640,3840]{1,0:T(8,128)}, f32[4,8,160]{2,1,0:T(8,128)}) custom-call(s32[1]{0:T(128)} %bitcast.101.place_ref, bf16[640,768]{1,0:T(8,128)(2,1)} %bitcast.375, bf16[768,3840]{1,0:T(8,128)(2,1)} %all-gather.2.cloned.1.call-done.table_ref, f32[1,3840]{1,0:T(1,128)} %broadcast_in_dim.134.bias_ref, bf16[160,3840]{1,0:T(8,128)(2,1)} %get-tuple-element.144.refs_0_, ...), custom_call_target="tpu_custom_call" | custom-call | flops 1 | bytes 1 | tf_op jit(solution)/shard_map/head/pallas_call | solution.py:600
  295.0 16.6 %head_back.1 = (bf16[640,3840]{1,0:T(8,128)(2,1)}, f32[640,768]{1,0:T(8,128)}, f32[1,3840]{1,0:T(1,128)}, f32[4,1,160]{2,1,0:T(1,128)}) custom-call(s32[1]{0:T(128)} %bitcast.101.place_ref, f32[640,3840]{1,0:T(8,128)} %get-tuple-element.58.logits_ref, f32[8,4,8,160]{3,2,1,0:T(8,128)} %copy-done.67, f32[4,1,160]{2,1,0:T(1,128)} %broadcast_select_fusion.scale_ref, ...), custom_call_target="tpu_custom_call" | custom-call | flops 1 | bytes 1 | tf_op jit(solution)/shard_map/head_back/pallas_call | solution.py:670
  313.1 7.3 %fusion.6 = f32[4,4,48,3840]{3,2,1,0:T(8,128)S(1)} fusion(bf16[4,4,48,640]{3,2,1,0:T(8,128)(2,1)S(1)} %bitcast.389, bf16[640,3840]{1,0:T(8,128)(2,1)} %get-tuple-element.60), kind=kOutput, calls=%fused_computation.12 | convolution fusion | flops 3774873600 | bytes 17694720 | tf_op jit(solution)/shard_map/dot_general | solution.py:1151
  345.3 8.0 %fusion.5.refs_0_ = bf16[512,3072]{1,0:T(8,128)(2,1)S(1)} fusion(f32[512,3072]{1,0:T(8,128)} %get-tuple-element.221, bf16[512,768]{1,0:T(8,128)(2,1)S(1)} %get-tuple-element.106, bf16[768,3072]{1,0:T(8,128)(2,1)} %bitcast.354, f32[3072]{0:T(1024)S(1)} %slice.186), kind=kOutput, calls=%fused_computation.8 | convolution fusion | flops 2433220608 | bytes 14954496 | tf_op jit(solution)/shard_map/az,zh->ah/dot_general | solution.py:447
  362.5 6.5 %fusion.133 = f32[768,3072]{1,0:T(8,128)S(1)} fusion(bf16[512,768]{1,0:T(8,128)(2,1)} %copy-done.50, bf16[512,3072]{1,0:T(8,128)(2,1)} %copy-done.51), kind=kOutput, calls=%fused_computation.366 | convolution fusion | flops 2415919104 | bytes 13369344 | tf_op jit(solution)/shard_map/bu,bw->uw/dot_general | solution.py:451
  388.5 4.8 convert_add_fusion
  401.1 17.3 %attend_back.1.refs_0_ = bf16[512,2304]{1,0:T(8,128)(2,1)S(1)} custom-call(s32[1]{0:T(128)} %dynamic_slice.169.lengths_ref, bf16[512,2304]{1,0:T(8,128)(2,1)S(1)} %fusion.8.query_ref.key_ref.value_ref, bf16[512,2304]{1,0:T(8,128)(2,1)S(1)} %fusion.8.query_ref.key_ref.value_ref, bf16[512,2304]{1,0:T(8,128)(2,1)S(1)} %fusion.8.query_ref.key_ref.value_ref, ...), custom_call_target="tpu_custom_call" | custom-call | flops 1 | bytes 1 | tf_op jit(solution)/shard_map/attend_back/pallas_call | solution.py:548
  424.8 4.7 weight_sums.3
  441.3 5.9 fusion.10
  449.1 6.0 collective-permute-start.40
  455.1 7.0 %all-to-all-done.5 = bf16[16,1,48,512]{3,2,1,0:T(8,128)(2,1)S(1)} async-done(((bf16[16,1,48,512]{3,2,1,0:T(8,128)(2,1)}), bf16[16,1,48,512]{3,2,1,0:T(8,128)(2,1)S(1)}, u32[]{:S(2)}, u32[]{:S(2)}) %all-to-all-start.5) | async-done | bytes 786464 | tf_op jit(solution)/shard_map/all_to_all | solution.py:1187
  464.2 4.8 convert_add_fusion.4
  477.1 16.1 %spread_add.2.refs_2_.refs_3_ = f32[48,15360]{1,0:T(8,128)S(1)} custom-call(s32[16,1,512]{2,1,0:T(1,128)S(1)} %copy-done.25, bf16[16,48,512]{2,1,0:T(8,128)(2,1)S(1)} %bitcast.352, bf16[16,48,512]{2,1,0:T(8,128)(2,1)S(1)} %collective-permute-done.42.refs_0_.grad_ref, bf16[384,768]{1,0:T(8,128)(2,1)S(1)} %bitcast.363, bf16[384,768]{1,0:T(8,128)(2,1)} %bitcast.144.refs_2_, ...), custom_call_target="tpu_custom_call" | custom-call | flops 1 | bytes 1 | tf_op jit(solution)/shard_map/spread_add/pallas_call | solution.py:400
  518.0 16.1 %spread_add.3.refs_3_ = f32[48,15360]{1,0:T(8,128)S(1)} custom-call(s32[16,1,512]{2,1,0:T(1,128)S(1)} %copy-done.23, bf16[16,48,512]{2,1,0:T(8,128)(2,1)S(1)} %collective-permute-done.42.refs_0_.grad_ref, bf16[4,288,768]{2,1,0:T(8,128)(2,1)} %fusion.15.refs_0_.refs_1_, f32[48,3840]{1,0:T(8,128)S(1)} %get-tuple-element.151.refs_1_, ...), custom_call_target="tpu_custom_call" | custom-call | flops 1 | bytes 1 | tf_op jit(solution)/shard_map/spread_add/pallas_call | solution.py:400
  546.2 6.9 %collective-permute-done.44.refs_0_ = f32[48,3840]{1,0:T(8,128)S(1)} collective-permute-done((f32[48,3840]{1,0:T(8,128)S(1)}, f32[48,3840]{1,0:T(8,128)S(1)}, u32[]{:S(2)}, u32[]{:S(2)}) %collective-permute-start.44) | collective-permute-done | bytes 737312 | tf_op jit(solution)/shard_map/ppermute | solution.py:49
  559.0 8.7 %collective-permute-done.58 = f32[26112]{0:T(1024)S(1)} collective-permute-done((f32[26112]{0:T(1024)S(1)}, f32[26112]{0:T(1024)S(1)}, u32[]{:S(2)}, u32[]{:S(2)}) %collective-permute-start.58) | collective-permute-done | bytes 104480 | tf_op jit(solution)/shard_map/ppermute | solution.py:49
  604.9 6.9 %subtract_bitcast_fusion = (f32[15360,48]{0,1:T(8,128)}, f32[15360,48]{0,1:T(8,128)}, f32[15360,48]{0,1:T(8,128)}) fusion(f32[48,15360]{1,0:T(8,128)S(1)} %get-tuple-element.104, f32[]{:T(128)S(6)} %min.32, f32[15360,48]{0,1:T(8,128)S(1)} %copy-done.53, f32[15360,48]{0,1:T(8,128)} %param.36, f32[15360,48]{0,1:T(8,128)S(1)} %copy-done.7), kind=kLoop, calls=%fused_computation.37 | loop fusion | flops 11796480 | bytes 20643844 | tf_op jit(solution)/shard_map/transpose | solution.py:1279
  (634 shorter events, 274.8 us)
Async XLA Ops:
  32.8 47.6 %collective-permute-start.3 = (bf16[240,768]{1,0:T(8,128)(2,1)}, bf16[240,768]{1,0:T(8,128)(2,1)S(1)}, u32[]{:S(2)}, u32[]{:S(2)}) collective-permute-start(bf16[240,768]{1,0:T(8,128)(2,1)} %gate.12.refs_0_), channel_id=1, source_target_pairs={{0,24},{2,26},{4,28},{6,30},{8,16},{10,18},{12,20},{14,22},{16,8},... | collective-permute-start | bytes 1105928 | tf_op jit(solution)/shard_map/ppermute | solution.py:49
  36.6 43.9 %collective-permute-start.2 = (bf16[240,768]{1,0:T(8,128)(2,1)}, bf16[240,768]{1,0:T(8,128)(2,1)}, u32[]{:S(2)}, u32[]{:S(2)}) collective-permute-start(bf16[240,768]{1,0:T(8,128)(2,1)} %gate.12.refs_0_), channel_id=1, source_target_pairs={{0,16},{2,18},{4,20},{6,22},{8,24},{10,26},{12,28},{14,30},{16,0},... | collective-permute-start | bytes 1105928 | tf_op jit(solution)/shard_map/ppermute | solution.py:49
  36.6 43.9 %collective-permute-start.1 = (bf16[240,768]{1,0:T(8,128)(2,1)}, bf16[240,768]{1,0:T(8,128)(2,1)}, u32[]{:S(2)}, u32[]{:S(2)}) collective-permute-start(bf16[240,768]{1,0:T(8,128)(2,1)} %gate.12.refs_0_), channel_id=1, source_target_pairs={{0,8},{2,10},{4,12},{6,14},{8,0},{10,2},{12,4},{14,6},{16,24},{18,... | collective-permute-start | bytes 1105928 | tf_op jit(solution)/shard_map/ppermute | solution.py:49
  73.0 54.7 %all-to-all-start.2 = ((bf16[16,1,48,512]{3,2,1,0:T(8,128)(2,1)}), bf16[16,1,48,512]{3,2,1,0:T(8,128)(2,1)}, u32[]{:S(2)}, u32[]{:S(2)}) async-start(bf16[16,1,48,512]{3,2,1,0:T(8,128)(2,1)} %add_bitcast_fusion), calls=%async_computation.2 | async-start | bytes 1572864 | tf_op jit(solution)/shard_map/all_to_all | solution.py:133
  87.0 39.0 %collective-permute-start.4 = (bf16[2,240,768]{2,1,0:T(8,128)(2,1)S(1)}, bf16[2,240,768]{2,1,0:T(8,128)(2,1)}, u32[]{:S(2)}, u32[]{:S(2)}) collective-permute-start(bf16[2,240,768]{2,1,0:T(8,128)(2,1)S(1)} %pad_maximum_fusion.6.refs_0_), channel_id=1, source_target_pairs={{0,2},{2,0},{4,6},{6,4},{8,10},{10,8},{12,14},{14,12},{16,18},{18,... | collective-permute-start | bytes 2211848 | tf_op jit(solution)/shard_map/ppermute | solution.py:49
  88.6 45.9 %collective-permute-start.10 = (bf16[2,240,768]{2,1,0:T(8,128)(2,1)S(1)}, bf16[2,240,768]{2,1,0:T(8,128)(2,1)}, u32[]{:S(2)}, u32[]{:S(2)}) collective-permute-start(bf16[2,240,768]{2,1,0:T(8,128)(2,1)S(1)} %pad_maximum_fusion.6.refs_0_), channel_id=1, source_target_pairs={{0,1},{1,0},{2,3},{3,2},{4,5},{5,4},{6,7},{7,6},{8,9},{9,8},{10,11... | collective-permute-start | bytes 2211848 | tf_op jit(solution)/shard_map/ppermute | solution.py:49
  88.7 45.9 %collective-permute-start.5 = (bf16[2,240,768]{2,1,0:T(8,128)(2,1)S(1)}, bf16[2,240,768]{2,1,0:T(8,128)(2,1)}, u32[]{:S(2)}, u32[]{:S(2)}) collective-permute-start(bf16[2,240,768]{2,1,0:T(8,128)(2,1)S(1)} %pad_maximum_fusion.6.refs_0_), channel_id=1, source_target_pairs={{0,4},{2,6},{4,0},{6,2},{8,12},{10,14},{12,8},{14,10},{16,20},{18,... | collective-permute-start | bytes 2211848 | tf_op jit(solution)/shard_map/ppermute | solution.py:49
  110.1 30.9 %collective-permute-start.9 = (bf16[2,240,768]{2,1,0:T(8,128)(2,1)S(1)}, bf16[2,240,768]{2,1,0:T(8,128)(2,1)}, u32[]{:S(2)}, u32[]{:S(2)}) collective-permute-start(bf16[2,240,768]{2,1,0:T(8,128)(2,1)S(1)} %collective-permute-done.8.refs_6_), channel_id=1, source_target_pairs={{0,2},{2,0},{4,6},{6,4},{8,10},{10,8},{12,14},{14,12},{16,18},{18,... | collective-permute-start | bytes 2211848 | tf_op jit(solution)/shard_map/ppermute | solution.py:49
  133.0 136.3 %all-gather.2.cloned.1.call-start = ((), (), s32[]{:S(2)}) async-start(), calls=%async_computation.7 | async-start | bytes 7372800 | tf_op jit(solution)/shard_map/all_gather | solution.py:137
  134.5 29.0 %collective-permute-start.11 = (bf16[2,240,768]{2,1,0:T(8,128)(2,1)}, bf16[2,240,768]{2,1,0:T(8,128)(2,1)}, u32[]{:S(2)}, u32[]{:S(2)}) collective-permute-start(bf16[2,240,768]{2,1,0:T(8,128)(2,1)} %collective-permute-done.4.refs_1_), channel_id=1, source_target_pairs={{0,1},{1,0},{2,3},{3,2},{4,5},{5,4},{6,7},{7,6},{8,9},{9,8},{10,11... | collective-permute-start | bytes 2211848 | tf_op jit(solution)/shard_map/ppermute | solution.py:49
  135.1 27.9 %collective-permute-start.12 = (bf16[2,240,768]{2,1,0:T(8,128)(2,1)}, bf16[2,240,768]{2,1,0:T(8,128)(2,1)}, u32[]{:S(2)}, u32[]{:S(2)}) collective-permute-start(bf16[2,240,768]{2,1,0:T(8,128)(2,1)} %collective-permute-done.5.refs_2_), channel_id=1, source_target_pairs={{0,1},{1,0},{2,3},{3,2},{4,5},{5,4},{6,7},{7,6},{8,9},{9,8},{10,11... | collective-permute-start | bytes 2211848 | tf_op jit(solution)/shard_map/ppermute | solution.py:49
  151.5 33.8 %all-to-all-start.4 = ((bf16[4,4,24,3072]{3,2,1,0:T(8,128)(2,1)}), bf16[4,4,24,3072]{3,2,1,0:T(8,128)(2,1)}, u32[]{:S(2)}, u32[]{:S(2)}) async-start(bf16[4,4,24,3072]{3,2,1,0:T(8,128)(2,1)} %gate.15), calls=%async_computation.4 | async-start | bytes 4718592 | tf_op jit(solution)/shard_map/all_to_all | solution.py:133
  160.1 109.2 %collective-permute-start.25 = (bf16[160,3840]{1,0:T(8,128)(2,1)}, bf16[160,3840]{1,0:T(8,128)(2,1)}, u32[]{:S(2)}, u32[]{:S(2)}) collective-permute-start(bf16[160,3840]{1,0:T(8,128)(2,1)} %get-tuple-element.142), channel_id=1, source_target_pairs={{0,6},{2,4},{4,2},{6,0},{8,14},{10,12},{12,10},{14,8},{16,22},{18,... | collective-permute-start | bytes 3686408 | tf_op jit(solution)/shard_map/ppermute | solution.py:49
  163.0 106.4 %collective-permute-start.23 = (bf16[160,3840]{1,0:T(8,128)(2,1)}, bf16[160,3840]{1,0:T(8,128)(2,1)}, u32[]{:S(2)}, u32[]{:S(2)}) collective-permute-start(bf16[160,3840]{1,0:T(8,128)(2,1)} %get-tuple-element.143), channel_id=1, source_target_pairs={{0,2},{2,0},{4,6},{6,4},{8,10},{10,8},{12,14},{14,12},{16,18},{18,... | collective-permute-start | bytes 3686408 | tf_op jit(solution)/shard_map/ppermute | solution.py:49
  163.5 105.8 %collective-permute-start.24 = (bf16[160,3840]{1,0:T(8,128)(2,1)}, bf16[160,3840]{1,0:T(8,128)(2,1)}, u32[]{:S(2)}, u32[]{:S(2)}) collective-permute-start(bf16[160,3840]{1,0:T(8,128)(2,1)} %get-tuple-element.145), channel_id=1, source_target_pairs={{0,4},{2,6},{4,0},{6,2},{8,12},{10,14},{12,8},{14,10},{16,20},{18,... | collective-permute-start | bytes 3686408 | tf_op jit(solution)/shard_map/ppermute | solution.py:49
  222.3 34.0 %collective-permute-start.22 = (bf16[160,768]{1,0:T(8,128)(2,1)S(1)}, bf16[160,768]{1,0:T(8,128)(2,1)}, u32[]{:S(2)}, u32[]{:S(2)}) collective-permute-start(bf16[160,768]{1,0:T(8,128)(2,1)S(1)} %bitcast.390), channel_id=1, source_target_pairs={{0,2},{2,0},{4,6},{6,4},{8,10},{10,8},{12,14},{14,12},{16,18},{18,... | collective-permute-start | bytes 737288 | tf_op jit(solution)/shard_map/ppermute | solution.py:118
  328.5 50.6 %collective-permute-start.31 = (bf16[4,48,3840]{2,1,0:T(8,128)(2,1)}, bf16[4,48,3840]{2,1,0:T(8,128)(2,1)}, u32[]{:S(2)}, u32[]{:S(2)}) collective-permute-start(bf16[4,48,3840]{2,1,0:T(8,128)(2,1)} %get-tuple-element.129.refs_2_), channel_id=1, source_target_pairs={{24,16},{26,18},{28,20},{30,22},{25,17},{27,19},{29,21},{31,23}} | collective-permute-start | bytes 4423688 | tf_op jit(solution)/shard_map/ppermute | solution.py:164
  330.3 48.8 %collective-permute-start.30 = (bf16[4,48,3840]{2,1,0:T(8,128)(2,1)}, bf16[4,48,3840]{2,1,0:T(8,128)(2,1)}, u32[]{:S(2)}, u32[]{:S(2)}) collective-permute-start(bf16[4,48,3840]{2,1,0:T(8,128)(2,1)} %get-tuple-element.130.refs_1_), channel_id=1, source_target_pairs={{0,8},{2,10},{4,12},{6,14},{1,9},{3,11},{5,13},{7,15}} | collective-permute-start | bytes 4423688 | tf_op jit(solution)/shard_map/ppermute | solution.py:163
  383.3 49.8 %collective-permute-start.37 = (bf16[4,48,3840]{2,1,0:T(8,128)(2,1)S(1)}, bf16[4,48,3840]{2,1,0:T(8,128)(2,1)S(1)}, u32[]{:S(2)}, u32[]{:S(2)}) collective-permute-start(bf16[4,48,3840]{2,1,0:T(8,128)(2,1)S(1)} %get-tuple-element.127.refs_4_), channel_id=1, source_target_pairs={{16,8},{18,10},{20,12},{22,14},{24,16},{26,18},{28,20},{30,22},{17... | collective-permute-start | bytes 4423688 | tf_op jit(solution)/shard_map/ppermute | solution.py:164
  384.0 49.1 %collective-permute-start.36 = (bf16[4,48,3840]{2,1,0:T(8,128)(2,1)S(1)}, bf16[4,48,3840]{2,1,0:T(8,128)(2,1)S(1)}, u32[]{:S(2)}, u32[]{:S(2)}) collective-permute-start(bf16[4,48,3840]{2,1,0:T(8,128)(2,1)S(1)} %get-tuple-element.128.refs_3_), channel_id=1, source_target_pairs={{0,8},{2,10},{4,12},{6,14},{8,16},{10,18},{12,20},{14,22},{1,9},{3... | collective-permute-start | bytes 4423688 | tf_op jit(solution)/shard_map/ppermute | solution.py:163
  398.0 51.1 %collective-permute-start.50 = (bf16[768,768]{1,0:T(8,128)(2,1)}, bf16[768,768]{1,0:T(8,128)(2,1)}, u32[]{:S(2)}, u32[]{:S(2)}) collective-permute-start(bf16[768,768]{1,0:T(8,128)(2,1)} %pad_maximum_fusion.1.refs_0_), channel_id=1, source_target_pairs={{0,2},{2,0},{4,6},{6,4},{8,10},{10,8},{12,14},{14,12},{16,18},{18,... | collective-permute-start | bytes 3538952 | tf_op jit(solution)/shard_map/ppermute | solution.py:49
  400.4 68.7 %collective-permute-start.51 = (bf16[768,768]{1,0:T(8,128)(2,1)}, bf16[768,768]{1,0:T(8,128)(2,1)}, u32[]{:S(2)}, u32[]{:S(2)}) collective-permute-start(bf16[768,768]{1,0:T(8,128)(2,1)} %pad_maximum_fusion.2.refs_1_), channel_id=1, source_target_pairs={{0,4},{2,6},{4,0},{6,2},{8,12},{10,14},{12,8},{14,10},{16,20},{18,... | collective-permute-start | bytes 3538952 | tf_op jit(solution)/shard_map/ppermute | solution.py:49
  418.5 52.0 %collective-permute-start.52 = (bf16[768,768]{1,0:T(8,128)(2,1)S(1)}, bf16[768,768]{1,0:T(8,128)(2,1)}, u32[]{:S(2)}, u32[]{:S(2)}) collective-permute-start(bf16[768,768]{1,0:T(8,128)(2,1)S(1)} %pad_maximum_fusion.3.refs_2_), channel_id=1, source_target_pairs={{0,6},{2,4},{4,2},{6,0},{8,14},{10,12},{12,10},{14,8},{16,22},{18,... | collective-permute-start | bytes 3538952 | tf_op jit(solution)/shard_map/ppermute | solution.py:49
  447.2 47.6 %collective-permute-start.41 = (bf16[4,48,3840]{2,1,0:T(8,128)(2,1)}, bf16[4,48,3840]{2,1,0:T(8,128)(2,1)}, u32[]{:S(2)}, u32[]{:S(2)}) collective-permute-start(bf16[4,48,3840]{2,1,0:T(8,128)(2,1)} %get-tuple-element.121), channel_id=1, source_target_pairs={{8,0},{10,2},{12,4},{14,6},{16,8},{18,10},{20,12},{22,14},{24,16},... | collective-permute-start | bytes 4423688 | tf_op jit(solution)/shard_map/ppermute | solution.py:164
  449.1 45.7 %collective-permute-start.40 = (bf16[4,48,3840]{2,1,0:T(8,128)(2,1)}, bf16[4,48,3840]{2,1,0:T(8,128)(2,1)}, u32[]{:S(2)}, u32[]{:S(2)}) collective-permute-start(bf16[4,48,3840]{2,1,0:T(8,128)(2,1)} %get-tuple-element.122), channel_id=1, source_target_pairs={{0,8},{2,10},{4,12},{6,14},{8,16},{10,18},{12,20},{14,22},{16,24},... | collective-permute-start | bytes 4423688 | tf_op jit(solution)/shard_map/ppermute | solution.py:163
  470.5 28.1 %collective-permute-start.48 = (bf16[384,768]{1,0:T(8,128)(2,1)}, bf16[384,768]{1,0:T(8,128)(2,1)}, u32[]{:S(2)}, u32[]{:S(2)}) collective-permute-start(bf16[384,768]{1,0:T(8,128)(2,1)} %bitcast.144.refs_2_), channel_id=1, source_target_pairs={{0,4},{2,6},{4,0},{6,2},{8,12},{10,14},{12,8},{14,10},{16,20},{18,... | collective-permute-start | bytes 1769480 | tf_op jit(solution)/shard_map/ppermute | solution.py:49
  506.4 29.3 %collective-permute-start.55 = (f32[26112]{0:T(1024)S(1)}, f32[26112]{0:T(1024)S(1)}, u32[]{:S(2)}, u32[]{:S(2)}) collective-permute-start(f32[26112]{0:T(1024)S(1)} %pad_maximum_fusion.12), channel_id=1, source_target_pairs={{0,4},{2,6},{4,0},{6,2},{8,12},{10,14},{12,8},{14,10},{16,20},{18,... | collective-permute-start | bytes 313352 | tf_op jit(solution)/shard_map/ppermute | solution.py:118
  507.3 29.5 %collective-permute-start.56 = (f32[26112]{0:T(1024)S(1)}, f32[26112]{0:T(1024)S(1)}, u32[]{:S(2)}, u32[]{:S(2)}) collective-permute-start(f32[26112]{0:T(1024)S(1)} %pad_maximum_fusion.12), channel_id=1, source_target_pairs={{0,6},{2,4},{4,2},{6,0},{8,14},{10,12},{12,10},{14,8},{16,22},{18,... | collective-permute-start | bytes 313352 | tf_op jit(solution)/shard_map/ppermute | solution.py:118
  508.9 27.8 %collective-permute-start.54 = (f32[26112]{0:T(1024)S(1)}, f32[26112]{0:T(1024)}, u32[]{:S(2)}, u32[]{:S(2)}) collective-permute-start(f32[26112]{0:T(1024)S(1)} %pad_maximum_fusion.12), channel_id=1, source_target_pairs={{0,2},{2,0},{4,6},{6,4},{8,10},{10,8},{12,14},{14,12},{16,18},{18,... | collective-permute-start | bytes 313352 | tf_op jit(solution)/shard_map/ppermute | solution.py:118
  511.1 30.4 %collective-permute-start.46 = (f32[48,3840]{1,0:T(8,128)}, f32[48,3840]{1,0:T(8,128)}, u32[]{:S(2)}, u32[]{:S(2)}) collective-permute-start(f32[48,3840]{1,0:T(8,128)} %get-tuple-element.150.refs_4_), channel_id=1, source_target_pairs={{0,6},{2,4},{4,2},{6,0},{8,14},{10,12},{12,10},{14,8},{16,22},{18,... | collective-permute-start | bytes 2211848 | tf_op jit(solution)/shard_map/ppermute | solution.py:49
  512.6 33.6 %collective-permute-start.45 = (f32[48,3840]{1,0:T(8,128)S(1)}, f32[48,3840]{1,0:T(8,128)}, u32[]{:S(2)}, u32[]{:S(2)}) collective-permute-start(f32[48,3840]{1,0:T(8,128)S(1)} %get-tuple-element.152.refs_3_), channel_id=1, source_target_pairs={{0,4},{2,6},{4,0},{6,2},{8,12},{10,14},{12,8},{14,10},{16,20},{18,... | collective-permute-start | bytes 2211848 | tf_op jit(solution)/shard_map/ppermute | solution.py:49
  513.6 56.8 %all-to-all-start.6 = ((bf16[4,288,768]{2,1,0:T(8,128)(2,1)}), bf16[4,288,768]{2,1,0:T(8,128)(2,1)}, u32[]{:S(2)}, u32[]{:S(2)}) async-start(bf16[4,288,768]{2,1,0:T(8,128)(2,1)} %fusion.15.refs_0_.refs_1_), calls=%async_computation.6 | async-start | bytes 3538944 | tf_op jit(solution)/shard_map/all_to_all | solution.py:133
  (193 other events, 1853.9 us)
Sparse Core Ops, SparseCore 0:
  135.4 110.3 all-gather.1

commit v4 on v3

--- a/solution.py
+++ b/solution.py
@@ -455,30 +455,45 @@
     return jnp.sum(gradient.astype(jnp.float32), axis=0)
 
 
-def scores_of(query, key_rows, live):
-    raw = lax.dot_general(
-        query * SCORE_SCALE, key_rows, (((1,), (1,)), ((), ())), preferred_element_type=jnp.float32
-    )
+STRIP = 128
+HEADS_STEP = 6
+HELD = 3
+
+
+def across(one, two):
+    return lax.dot_general(one, two, (((1,), (1,)), ((), ())), preferred_element_type=jnp.float32)
+
+
+def down(one, two):
+    return lax.dot_general(one, two, (((0,), (0,)), ((), ())), preferred_element_type=jnp.float32)
+
+
+def soften(raw, live):
     scores = jnp.where(live, raw, -1e30)
-    powers = jnp.exp(scores - jnp.max(scores, axis=-1, keepdims=True))
-    return powers * (1.0 / jnp.sum(powers, axis=-1, keepdims=True))
+    powers = jnp.exp(scores - jnp.max(scores, axis=0, keepdims=True))
+    return powers * (1.0 / jnp.sum(powers, axis=0, keepdims=True))
 
 
 def attend_kernel(lengths_ref, query_ref, key_ref, value_ref, *refs):
-    out_ref = refs[-1]
+    out_ref, scores, probs = refs[-3:]
     length = lengths_ref[pl.program_id(0)]
-    live = lax.broadcasted_iota(jnp.int32, (1, key_ref.shape[0]), 1) < length
-    for start in range(0, query_ref.shape[1], HEAD_DIM):
-        span = slice(start, start + HEAD_DIM)
-        prob = scores_of(query_ref[:, span], key_ref[:, span], live).astype(jnp.bfloat16)
-        context = jnp.dot(prob, value_ref[:, span], preferred_element_type=jnp.float32)
-        out_ref[:, span] = context.astype(out_ref.dtype)
+    rows = query_ref.shape[0]
+    live = lax.broadcasted_iota(jnp.int32, (rows, 1), 0) < length
+    contexts = []
+    for head in range(query_ref.shape[1] // HEAD_DIM):
+        span = slice(head * HEAD_DIM, (head + 1) * HEAD_DIM)
+        scores[head % HELD] = across(key_ref[:, span], query_ref[:, span] * SCORE_SCALE)
+        for start in range(0, rows, STRIP):
+            part = slice(start, start + STRIP)
+            probs[head % HELD, :, part] = soften(scores[head % HELD, :, part], live).astype(jnp.bfloat16)
+        contexts.append(down(value_ref[:, span], probs[head % HELD]))
+    out_ref[...] = jnp.concatenate(contexts, 0).T.astype(out_ref.dtype)
 
 
 def attend(qkv, lengths, seqs, *needed):
     rows, total = qkv.shape
     seq_len, width = rows // seqs, total // 3
-    lanes = 2 * HEAD_DIM
+    lanes = HEADS_STEP * HEAD_DIM
     blocks = width // lanes
 
     def part(which):
@@ -492,6 +507,10 @@
             in_specs=[part(0), part(1), part(2)]
             + [pl.BlockSpec(memory_space=pl.ANY)] * len(needed),
             out_specs=pl.BlockSpec((seq_len, lanes), lambda s, j, _: (s, j)),
+            scratch_shapes=[
+                pltpu.VMEM((HELD, seq_len, seq_len), jnp.float32),
+                pltpu.VMEM((HELD, seq_len, seq_len), jnp.bfloat16),
+            ],
         ),
         out_shape=jax.ShapeDtypeStruct((rows, width), jnp.bfloat16),
         compiler_params=pltpu.CompilerParams(vmem_limit_bytes=40 * 1024 * 1024),
@@ -501,45 +520,40 @@
 
 
 def attend_back_kernel(lengths_ref, query_ref, key_ref, value_ref, grad_ref, *refs):
-    out_ref = refs[-1]
+    out_ref, scores, grad_probs, probs, grads = refs[-5:]
     length = lengths_ref[pl.program_id(0)]
     step = pl.program_id(1)
     width = out_ref.shape[1] // 3
-    live = lax.broadcasted_iota(jnp.int32, (1, key_ref.shape[0]), 1) < length
+    rows, lanes = query_ref.shape
+    live = lax.broadcasted_iota(jnp.int32, (rows, 1), 0) < length
     parts = [[], [], []]
-    for start in range(0, query_ref.shape[1], HEAD_DIM):
-        span = slice(start, start + HEAD_DIM)
-        query, key_rows, value_rows = query_ref[:, span], key_ref[:, span], value_ref[:, span]
-        grad_out = grad_ref[:, span]
-        prob = scores_of(query, key_rows, live)
-        grad_prob = lax.dot_general(
-            grad_out, value_rows, (((1,), (1,)), ((), ())), preferred_element_type=jnp.float32
+    for head in range(lanes // HEAD_DIM):
+        span = slice(head * HEAD_DIM, (head + 1) * HEAD_DIM)
+        query, key_rows, grad_out = query_ref[:, span], key_ref[:, span], grad_ref[:, span]
+        scores[head % HELD] = across(key_rows, query * SCORE_SCALE)
+        grad_probs[head % HELD] = across(value_ref[:, span], grad_out)
+        for start in range(0, rows, STRIP):
+            part = slice(start, start + STRIP)
+            prob = soften(scores[head % HELD, :, part], live)
+            grad_prob = grad_probs[head % HELD, :, part]
+            mean = jnp.sum(prob * grad_prob, axis=0, keepdims=True)
+            probs[head % HELD, :, part] = prob.astype(jnp.bfloat16)
+            grads[head % HELD, :, part] = (prob * (grad_prob - mean)).astype(jnp.bfloat16)
+        parts[0].append(down(key_rows, grads[head % HELD]) * SCORE_SCALE)
+        parts[1].append(
+            jnp.dot(grads[head % HELD], query, preferred_element_type=jnp.float32) * SCORE_SCALE
         )
-        grad_value = lax.dot_general(
-            prob.astype(jnp.bfloat16),
-            grad_out,
-            (((0,), (0,)), ((), ())),
-            preferred_element_type=jnp.float32,
-        )
-        mean = jnp.sum(prob * grad_prob, axis=-1, keepdims=True)
-        grad_score = (prob * (grad_prob - mean)).astype(jnp.bfloat16)
-        grad_query = jnp.dot(grad_score, key_rows, preferred_element_type=jnp.float32)
-        grad_key = lax.dot_general(
-            grad_score, query, (((0,), (0,)), ((), ())), preferred_element_type=jnp.float32
-        )
-        parts[0].append(grad_query * SCORE_SCALE)
-        parts[1].append(grad_key * SCORE_SCALE)
-        parts[2].append(grad_value)
-    lanes = query_ref.shape[1]
-    for which, pieces in enumerate(parts):
+        parts[2].append(jnp.dot(probs[head % HELD], grad_out, preferred_element_type=jnp.float32))
+    merged = [jnp.concatenate(parts[0], 0).T] + [jnp.concatenate(part, 1) for part in parts[1:]]
+    for which, gradient in enumerate(merged):
         start = pl.multiple_of(which * width + step * lanes, lanes)
-        out_ref[:, pl.ds(start, lanes)] = jnp.concatenate(pieces, 1).astype(out_ref.dtype)
+        out_ref[:, pl.ds(start, lanes)] = gradient.astype(out_ref.dtype)
 
 
 def attend_back(qkv, grad_context, lengths, seqs, *needed):
     rows, total = qkv.shape
     seq_len, width = rows // seqs, total // 3
-    lanes = 2 * HEAD_DIM
+    lanes = HEADS_STEP * HEAD_DIM
     blocks = width // lanes
 
     def part(which):
@@ -553,6 +567,10 @@
             in_specs=[part(0), part(1), part(2), part(0)]
             + [pl.BlockSpec(memory_space=pl.ANY)] * len(needed),
             out_specs=pl.BlockSpec((seq_len, total), lambda s, j, _: (s, 0)),
+            scratch_shapes=[
+                pltpu.VMEM((HELD, seq_len, seq_len), kind)
+                for kind in (jnp.float32, jnp.float32, jnp.bfloat16, jnp.bfloat16)
+            ],
         ),
         out_shape=jax.ShapeDtypeStruct((rows, total), jnp.bfloat16),
         compiler_params=pltpu.CompilerParams(vmem_limit_bytes=40 * 1024 * 1024),
@@ -569,27 +587,33 @@
             held[...] = part_ref[...]
 
         pl.when(which == k)(hold)
-    return held[...].astype(jnp.float32)
+
+
+HEAD_STRIP = 16
 
 
 def head_kernel(place_ref, rows_ref, table_ref, bias_ref, *refs):
-    parts, (logits_ref, stats_ref, held) = refs[:-3], refs[-3:]
-    logits = (
+    parts, (logits_ref, stats_ref, held, packed) = refs[:-4], refs[-4:]
+    teacher_rows(place_ref, parts, held)
+    logits_ref[...] = (
         jnp.dot(rows_ref[...], table_ref[...], preferred_element_type=jnp.float32) + bias_ref[...]
     )
-    logits_ref[...] = logits
-    teach = teacher_rows(place_ref, parts, held)
-    student_top = jnp.max(logits, axis=-1, keepdims=True)
-    student_total = jnp.sum(jnp.exp(logits - student_top), axis=-1, keepdims=True)
-    teacher_top = jnp.max(teach, axis=-1, keepdims=True)
-    weighted = jnp.exp(teach - teacher_top)
-    teacher_total = jnp.sum(weighted, axis=-1, keepdims=True)
-    cross = jnp.sum(weighted * (teach - logits), axis=-1, keepdims=True)
-    lane = lax.broadcasted_iota(jnp.int32, (logits.shape[0], 128), 1)
-    packed = jnp.zeros((logits.shape[0], 128), jnp.float32)
-    for i, stat in enumerate((student_top, student_total, teacher_top, teacher_total, cross)):
-        packed = jnp.where(lane == i, stat, packed)
-    stats_ref[0] = packed.T[:8]
+    lane = lax.broadcasted_iota(jnp.int32, (HEAD_STRIP, 128), 1)
+    for row in range(0, held.shape[0], HEAD_STRIP):
+        part = slice(row, row + HEAD_STRIP)
+        logits = logits_ref[part, :]
+        student_top = jnp.max(logits, axis=-1, keepdims=True)
+        student_total = jnp.sum(jnp.exp(logits - student_top), axis=-1, keepdims=True)
+        teach = held[part, :].astype(jnp.float32)
+        teacher_top = jnp.max(teach, axis=-1, keepdims=True)
+        weighted = jnp.exp(teach - teacher_top)
+        teacher_total = jnp.sum(weighted, axis=-1, keepdims=True)
+        cross = jnp.sum(weighted * (teach - logits), axis=-1, keepdims=True)
+        stats = jnp.zeros((HEAD_STRIP, 128), jnp.float32)
+        for i, stat in enumerate((student_top, student_total, teacher_top, teacher_total, cross)):
+            stats = jnp.where(lane == i, stat, stats)
+        packed[part, :] = stats
+    stats_ref[0] = packed[...].T[:8]
 
 
 def head(place, rows, table_part, bias_part, teach_parts, near):
@@ -612,7 +636,10 @@
                 pl.BlockSpec((block, vocab), lambda i, _: (i, 0)),
                 pl.BlockSpec((1, 8, block), lambda i, _: (i, 0, 0)),
             ],
-            scratch_shapes=[pltpu.VMEM((block, vocab), jnp.bfloat16)],
+            scratch_shapes=[
+                pltpu.VMEM((block, vocab), jnp.bfloat16),
+                pltpu.VMEM((block, 128), jnp.float32),
+            ],
         ),
         out_shape=[
             jax.ShapeDtypeStruct((count, vocab), jnp.float32),
@@ -626,7 +653,7 @@
 
 def head_back_kernel(place_ref, logits_ref, stats_ref, scale_ref, table_ref, *refs):
     parts, (grad_ref, rows_ref, bias_ref, loss_ref, held) = refs[:-5], refs[-5:]
-    teach = teacher_rows(place_ref, parts, held)
+    teacher_rows(place_ref, parts, held)
     step = pl.program_id(0)
     stats = stats_ref[:, 0]
     tops, totals, teacher_tops, teacher_totals, crosses = (stats[:, i] for i in range(5))
@@ -642,23 +669,21 @@
     packed = jnp.concatenate(
         [student_lse, teacher_lse, scale_ref[0], jnp.zeros((5, top.shape[1]), jnp.float32)], 0
     ).T
-    grad = (
-        (
-            jnp.exp(logits_ref[...] - packed[:, 0:1])
-            - jnp.exp(teach - packed[:, 1:2])
-        )
-        * packed[:, 2:3]
-    ).astype(jnp.bfloat16)
-    grad_ref[...] = grad
-    rows_ref[...] = lax.dot_general(
-        grad, table_ref[...], (((1,), (1,)), ((), ())), preferred_element_type=jnp.float32
-    )
 
     @pl.when(step == 0)
     def _():
         bias_ref[...] = jnp.zeros_like(bias_ref)
 
-    bias_ref[...] += jnp.sum(grad.astype(jnp.float32), axis=0, keepdims=True)
+    for row in range(0, held.shape[0], HEAD_STRIP):
+        part = slice(row, row + HEAD_STRIP)
+        student = jnp.exp(logits_ref[part, :] - packed[part, 0:1])
+        teach = jnp.exp(held[part, :].astype(jnp.float32) - packed[part, 1:2])
+        grad = ((student - teach) * packed[part, 2:3]).astype(jnp.bfloat16)
+        grad_ref[part, :] = grad
+        bias_ref[...] += jnp.sum(grad.astype(jnp.float32), axis=0, keepdims=True)
+    rows_ref[...] = lax.dot_general(
+        grad_ref[...], table_ref[...], (((1,), (1,)), ((), ())), preferred_element_type=jnp.float32
+    )
 
 
 def head_back(place, logits, stats, scale, table_part, teach_parts, near):

time: 632 us -> 626 us (level)
  no operation moved by 1% of the time
where the time goes in v4:
time: 626 us; the launch traced here: 616 us
  Pallas kernels  141 us (23%)
  starting transfers between devices  136 us (22%)
  other arithmetic  100 us (16%)
  waiting for transfers between devices  95.4 us (15%)
  local copies, waits for them, and re-layouts  65.4 us (10%)
  matrix products  50.1 us (8%)
  between operations  27.2 us (4%)
    ppermute x49, waiting for transfers between devices, swap(): return lax.ppermute(x, axis, [(i, i ^ bit) for i in range(size)])  72 us
    ppermute x12, starting transfers between devices, near_exchange(): lax.ppermute(take(p ^ k), 'fsdp', [(i, i ^ k) for i in range(size)])  40.6 us
    ppermute x49, starting transfers between devices, swap(): return lax.ppermute(x, axis, [(i, i ^ bit) for i in range(size)])  38.5 us
    pallas_call x2, Pallas kernels, spread_add(): pl.pallas_call(functools.partial(spread_kernel, low_count), grid=(blocks,...  32.2 us
    pallas_call x2, Pallas kernels, lookup(): pl.pallas_call(functools.partial(lookup_kernel, low_count), grid=(blocks,...  31.6 us
    unnamed x314, local copies, waits for them, and re-layouts  26.8 us
    all_to_all x5, starting transfers between devices, exchange(): return lax.all_to_all(x, 'fsdp', 0, 0, tiled=True, axis_index_groups=groups)  25.7 us
    dot_general x4, matrix products, project_back(): jnp.einsum('az,zh->ah', gradient, weight_matrix, preferred_element_type=j...  17.2 us
  transfers between devices with their start and end apart: 75, of which 22 were waited for; matrix products, arithmetic and copies ran while one was open for 26% of the time, Pallas kernels for 18%

profile of v4, /device:TPU:0, one launch (start us, length us, event | category | flops | bytes accessed | tf_op | source)
XLA Modules:
  0.0 615.7 jit_solution(12537725940783040592)
XLA Ops:
  8.5 8.3 %all-to-all-start = ((s32[16,2,512]{2,1,0:T(2,128)}), s32[16,2,512]{2,1,0:T(2,128)S(1)}, u32[]{:S(2)}, u32[]{:S(2)}) async-start(s32[16,2,512]{2,1,0:T(2,128)} %broadcast_in_dim.68), calls=%async_computation | async-start | bytes 131072 | tf_op jit(solution)/shard_map/all_to_all | solution.py:990
  38.4 16.1 %lookup.2.refs_0_ = bf16[16,48,512]{2,1,0:T(8,128)(2,1)} custom-call(s32[16,1,512]{2,1,0:T(1,128)S(1)} %get-tuple-element.189.ids_ref, f32[48,15360]{1,0:T(8,128)S(1)} %bitcast.347, bf16[240,768]{1,0:T(8,128)(2,1)S(1)} %copy-done.12), custom_call_target="tpu_custom_call" | custom-call | flops 12079595520 | bytes 3735552 | tf_op jit(solution)/shard_map/lookup/pallas_call | solution.py:343
  54.5 15.5 %lookup.3.refs_3_ = bf16[16,48,512]{2,1,0:T(8,128)(2,1)S(1)} custom-call(s32[16,1,512]{2,1,0:T(1,128)S(1)} %get-tuple-element.190.ids_ref, f32[48,15360]{1,0:T(8,128)S(1)} %bitcast.348, bf16[16,48,512]{2,1,0:T(8,128)(2,1)} %lookup.2.refs_0_, bf16[192,3840]{1,0:T(8,128)(2,1)} %bitcast.6.refs_1_), custom_call_target="tpu_custom_call" | custom-call | flops 12079595520 | bytes 3735552 | tf_op jit(solution)/shard_map/lookup/pallas_call | solution.py:343
  73.0 7.5 %all-to-all-start.2 = ((bf16[16,1,48,512]{3,2,1,0:T(8,128)(2,1)}), bf16[16,1,48,512]{3,2,1,0:T(8,128)(2,1)}, u32[]{:S(2)}, u32[]{:S(2)}) async-start(bf16[16,1,48,512]{3,2,1,0:T(8,128)(2,1)} %add_bitcast_fusion), calls=%async_computation.2 | async-start | bytes 1572864 | tf_op jit(solution)/shard_map/all_to_all | solution.py:133
  89.1 19.0 %collective-permute-done.8.refs_6_ = bf16[2,240,768]{2,1,0:T(8,128)(2,1)S(1)} collective-permute-done((bf16[2,240,768]{2,1,0:T(8,128)(2,1)S(1)}, bf16[2,240,768]{2,1,0:T(8,128)(2,1)S(1)}, u32[]{:S(2)}, u32[]{:S(2)}) %collective-permute-start.8) | collective-permute-done | bytes 737312 | tf_op jit(solution)/shard_map/ppermute | solution.py:49
  111.4 14.6 %collective-permute-done.4.refs_1_ = bf16[2,240,768]{2,1,0:T(8,128)(2,1)} collective-permute-done((bf16[2,240,768]{2,1,0:T(8,128)(2,1)S(1)}, bf16[2,240,768]{2,1,0:T(8,128)(2,1)}, u32[]{:S(2)}, u32[]{:S(2)}) %collective-permute-start.4) | collective-permute-done | bytes 737312 | tf_op jit(solution)/shard_map/ppermute | solution.py:49
  135.2 5.9 collective-permute-done.9.refs_7_.refs_2_
  143.3 5.3 constant_dynamic-slice_fusion.2
  151.5 4.7 all-to-all-start.4
  164.7 9.5 %place.2 = (bf16[12,192,768]{2,1,0:T(8,128)(2,1)}, bf16[4,192,768]{2,1,0:T(8,128)(2,1)S(1)}, bf16[16,192,768]{2,1,0:T(8,128)(2,1)}, bf16[32,48,768]{2,1,0:T(8,128)(2,1)}) custom-call(s32[32]{0:T(128)S(1)} %stack.292.order_ref, bf16[2,240,768]{2,1,0:T(8,128)(2,1)S(1)} %pad_maximum_fusion.6.refs_0_, bf16[2,240,768]{2,1,0:T(8,128)(2,1)} %collective-permute-done.4.refs_1_, ...), custom_call_target="tpu_custom_call" | custom-call | tf_op jit(solution)/shard_map/place/pallas_call | solution.py:298
  189.9 9.4 %attend.1.refs_3_ = bf16[512,768]{1,0:T(8,128)(2,1)S(1)} custom-call(s32[1]{0:T(128)} %dynamic_slice.169.lengths_ref, bf16[512,2304]{1,0:T(8,128)(2,1)S(1)} %fusion.8.query_ref.key_ref.value_ref, bf16[512,2304]{1,0:T(8,128)(2,1)S(1)} %fusion.8.query_ref.key_ref.value_ref, bf16[512,2304]{1,0:T(8,128)(2,1)S(1)} %fusion.8.query_ref.key_ref.value_ref, ...), custom_call_target="tpu_custom_call" | custom-call | flops 1 | bytes 1 | tf_op jit(solution)/shard_map/attend/pallas_call | solution.py:502
  201.0 4.8 multiply_convert_fusion
  219.8 27.7 %collective-permute-start.22 = (bf16[160,768]{1,0:T(8,128)(2,1)S(1)}, bf16[160,768]{1,0:T(8,128)(2,1)}, u32[]{:S(2)}, u32[]{:S(2)}) collective-permute-start(bf16[160,768]{1,0:T(8,128)(2,1)S(1)} %bitcast.390), channel_id=1, source_target_pairs={{0,2},{2,0},{4,6},{6,4},{8,10},{10,8},{12,14},{14,12},{16,18},{18,... | collective-permute-start | bytes 737288 | tf_op jit(solution)/shard_map/ppermute | solution.py:118
  248.9 4.8 collective-permute-done.22
  266.8 13.9 %head.1 = (f32[640,3840]{1,0:T(8,128)}, f32[4,8,160]{2,1,0:T(8,128)}) custom-call(s32[1]{0:T(128)} %bitcast.101.place_ref, bf16[640,768]{1,0:T(8,128)(2,1)} %bitcast.375, bf16[768,3840]{1,0:T(8,128)(2,1)} %all-gather.2.cloned.1.call-done.table_ref, f32[1,3840]{1,0:T(1,128)} %broadcast_in_dim.134.bias_ref, bf16[160,3840]{1,0:T(8,128)(2,1)} %get-tuple-element.144.refs_0_, ...), custom_call_target="tpu_custom_call" | custom-call | flops 1 | bytes 1 | tf_op jit(solution)/shard_map/head/pallas_call | solution.py:624
  290.8 15.2 %head_back.1 = (bf16[640,3840]{1,0:T(8,128)(2,1)}, f32[640,768]{1,0:T(8,128)}, f32[1,3840]{1,0:T(1,128)}, f32[4,1,160]{2,1,0:T(1,128)}) custom-call(s32[1]{0:T(128)} %bitcast.101.place_ref, f32[640,3840]{1,0:T(8,128)} %get-tuple-element.58.logits_ref, f32[8,4,8,160]{3,2,1,0:T(8,128)} %copy-done.67, f32[4,1,160]{2,1,0:T(1,128)} %broadcast_select_fusion.scale_ref, ...), custom_call_target="tpu_custom_call" | custom-call | flops 1 | bytes 1 | tf_op jit(solution)/shard_map/head_back/pallas_call | solution.py:695
  307.4 7.3 %fusion.6 = f32[4,4,48,3840]{3,2,1,0:T(8,128)S(1)} fusion(bf16[4,4,48,640]{3,2,1,0:T(8,128)(2,1)S(1)} %bitcast.389, bf16[640,3840]{1,0:T(8,128)(2,1)} %get-tuple-element.60), kind=kOutput, calls=%fused_computation.12 | convolution fusion | flops 3774873600 | bytes 17694720 | tf_op jit(solution)/shard_map/dot_general | solution.py:1176
  339.6 8.0 %fusion.5.refs_0_ = bf16[512,3072]{1,0:T(8,128)(2,1)S(1)} fusion(f32[512,3072]{1,0:T(8,128)} %get-tuple-element.221, bf16[512,768]{1,0:T(8,128)(2,1)S(1)} %get-tuple-element.106, bf16[768,3072]{1,0:T(8,128)(2,1)} %bitcast.354, f32[3072]{0:T(1024)S(1)} %slice.186), kind=kOutput, calls=%fused_computation.8 | convolution fusion | flops 2433220608 | bytes 14954496 | tf_op jit(solution)/shard_map/az,zh->ah/dot_general | solution.py:447
  356.8 6.5 %fusion.133 = f32[768,3072]{1,0:T(8,128)S(1)} fusion(bf16[512,768]{1,0:T(8,128)(2,1)} %copy-done.50, bf16[512,3072]{1,0:T(8,128)(2,1)} %copy-done.51), kind=kOutput, calls=%fused_computation.366 | convolution fusion | flops 2415919104 | bytes 13369344 | tf_op jit(solution)/shard_map/bu,bw->uw/dot_general | solution.py:451
  382.7 4.8 convert_add_fusion
  395.3 16.6 %attend_back.1.refs_0_ = bf16[512,2304]{1,0:T(8,128)(2,1)S(1)} custom-call(s32[1]{0:T(128)} %dynamic_slice.169.lengths_ref, bf16[512,2304]{1,0:T(8,128)(2,1)S(1)} %fusion.8.query_ref.key_ref.value_ref, bf16[512,2304]{1,0:T(8,128)(2,1)S(1)} %fusion.8.query_ref.key_ref.value_ref, bf16[512,2304]{1,0:T(8,128)(2,1)S(1)} %fusion.8.query_ref.key_ref.value_ref, ...), custom_call_target="tpu_custom_call" | custom-call | flops 1 | bytes 1 | tf_op jit(solution)/shard_map/attend_back/pallas_call | solution.py:562
  418.2 4.7 weight_sums.3
  430.1 4.7 all-to-all-start.5
  434.9 5.9 fusion.10
  442.7 5.8 collective-permute-start.40
  448.5 7.8 %all-to-all-done.5 = bf16[16,1,48,512]{3,2,1,0:T(8,128)(2,1)S(1)} async-done(((bf16[16,1,48,512]{3,2,1,0:T(8,128)(2,1)}), bf16[16,1,48,512]{3,2,1,0:T(8,128)(2,1)S(1)}, u32[]{:S(2)}, u32[]{:S(2)}) %all-to-all-start.5) | async-done | bytes 786464 | tf_op jit(solution)/shard_map/all_to_all | solution.py:1212
  458.4 4.8 convert_add_fusion.4
  471.2 16.1 %spread_add.2.refs_2_.refs_3_ = f32[48,15360]{1,0:T(8,128)S(1)} custom-call(s32[16,1,512]{2,1,0:T(1,128)S(1)} %copy-done.25, bf16[16,48,512]{2,1,0:T(8,128)(2,1)S(1)} %bitcast.352, bf16[16,48,512]{2,1,0:T(8,128)(2,1)S(1)} %collective-permute-done.42.refs_0_.grad_ref, bf16[384,768]{1,0:T(8,128)(2,1)S(1)} %bitcast.363, bf16[384,768]{1,0:T(8,128)(2,1)} %bitcast.144.refs_2_, ...), custom_call_target="tpu_custom_call" | custom-call | flops 1 | bytes 1 | tf_op jit(solution)/shard_map/spread_add/pallas_call | solution.py:400
  512.4 16.1 %spread_add.3.refs_3_ = f32[48,15360]{1,0:T(8,128)S(1)} custom-call(s32[16,1,512]{2,1,0:T(1,128)S(1)} %copy-done.23, bf16[16,48,512]{2,1,0:T(8,128)(2,1)S(1)} %collective-permute-done.42.refs_0_.grad_ref, bf16[4,288,768]{2,1,0:T(8,128)(2,1)} %fusion.15.refs_0_.refs_1_, f32[48,3840]{1,0:T(8,128)S(1)} %get-tuple-element.151.refs_1_, ...), custom_call_target="tpu_custom_call" | custom-call | flops 1 | bytes 1 | tf_op jit(solution)/shard_map/spread_add/pallas_call | solution.py:400
  540.4 7.2 %collective-permute-done.44.refs_0_ = f32[48,3840]{1,0:T(8,128)S(1)} collective-permute-done((f32[48,3840]{1,0:T(8,128)S(1)}, f32[48,3840]{1,0:T(8,128)S(1)}, u32[]{:S(2)}, u32[]{:S(2)}) %collective-permute-start.44) | collective-permute-done | bytes 737312 | tf_op jit(solution)/shard_map/ppermute | solution.py:49
  553.4 8.7 %collective-permute-done.58 = f32[26112]{0:T(1024)S(1)} collective-permute-done((f32[26112]{0:T(1024)S(1)}, f32[26112]{0:T(1024)S(1)}, u32[]{:S(2)}, u32[]{:S(2)}) %collective-permute-start.58) | collective-permute-done | bytes 104480 | tf_op jit(solution)/shard_map/ppermute | solution.py:49
  599.3 6.9 %subtract_bitcast_fusion = (f32[15360,48]{0,1:T(8,128)}, f32[15360,48]{0,1:T(8,128)}, f32[15360,48]{0,1:T(8,128)}) fusion(f32[48,15360]{1,0:T(8,128)S(1)} %get-tuple-element.104, f32[]{:T(128)S(6)} %min.32, f32[15360,48]{0,1:T(8,128)S(1)} %copy-done.53, f32[15360,48]{0,1:T(8,128)} %param.36, f32[15360,48]{0,1:T(8,128)S(1)} %copy-done.7), kind=kLoop, calls=%fused_computation.37 | loop fusion | flops 11796480 | bytes 20643844 | tf_op jit(solution)/shard_map/transpose | solution.py:1304
  (634 shorter events, 274.6 us)
Async XLA Ops:
  32.8 47.6 %collective-permute-start.3 = (bf16[240,768]{1,0:T(8,128)(2,1)}, bf16[240,768]{1,0:T(8,128)(2,1)S(1)}, u32[]{:S(2)}, u32[]{:S(2)}) collective-permute-start(bf16[240,768]{1,0:T(8,128)(2,1)} %gate.12.refs_0_), channel_id=1, source_target_pairs={{0,24},{2,26},{4,28},{6,30},{8,16},{10,18},{12,20},{14,22},{16,8},... | collective-permute-start | bytes 1105928 | tf_op jit(solution)/shard_map/ppermute | solution.py:49
  36.6 43.9 %collective-permute-start.2 = (bf16[240,768]{1,0:T(8,128)(2,1)}, bf16[240,768]{1,0:T(8,128)(2,1)}, u32[]{:S(2)}, u32[]{:S(2)}) collective-permute-start(bf16[240,768]{1,0:T(8,128)(2,1)} %gate.12.refs_0_), channel_id=1, source_target_pairs={{0,16},{2,18},{4,20},{6,22},{8,24},{10,26},{12,28},{14,30},{16,0},... | collective-permute-start | bytes 1105928 | tf_op jit(solution)/shard_map/ppermute | solution.py:49
  36.6 43.9 %collective-permute-start.1 = (bf16[240,768]{1,0:T(8,128)(2,1)}, bf16[240,768]{1,0:T(8,128)(2,1)}, u32[]{:S(2)}, u32[]{:S(2)}) collective-permute-start(bf16[240,768]{1,0:T(8,128)(2,1)} %gate.12.refs_0_), channel_id=1, source_target_pairs={{0,8},{2,10},{4,12},{6,14},{8,0},{10,2},{12,4},{14,6},{16,24},{18,... | collective-permute-start | bytes 1105928 | tf_op jit(solution)/shard_map/ppermute | solution.py:49
  73.0 54.7 %all-to-all-start.2 = ((bf16[16,1,48,512]{3,2,1,0:T(8,128)(2,1)}), bf16[16,1,48,512]{3,2,1,0:T(8,128)(2,1)}, u32[]{:S(2)}, u32[]{:S(2)}) async-start(bf16[16,1,48,512]{3,2,1,0:T(8,128)(2,1)} %add_bitcast_fusion), calls=%async_computation.2 | async-start | bytes 1572864 | tf_op jit(solution)/shard_map/all_to_all | solution.py:133
  87.0 39.0 %collective-permute-start.4 = (bf16[2,240,768]{2,1,0:T(8,128)(2,1)S(1)}, bf16[2,240,768]{2,1,0:T(8,128)(2,1)}, u32[]{:S(2)}, u32[]{:S(2)}) collective-permute-start(bf16[2,240,768]{2,1,0:T(8,128)(2,1)S(1)} %pad_maximum_fusion.6.refs_0_), channel_id=1, source_target_pairs={{0,2},{2,0},{4,6},{6,4},{8,10},{10,8},{12,14},{14,12},{16,18},{18,... | collective-permute-start | bytes 2211848 | tf_op jit(solution)/shard_map/ppermute | solution.py:49
  88.6 45.9 %collective-permute-start.10 = (bf16[2,240,768]{2,1,0:T(8,128)(2,1)S(1)}, bf16[2,240,768]{2,1,0:T(8,128)(2,1)}, u32[]{:S(2)}, u32[]{:S(2)}) collective-permute-start(bf16[2,240,768]{2,1,0:T(8,128)(2,1)S(1)} %pad_maximum_fusion.6.refs_0_), channel_id=1, source_target_pairs={{0,1},{1,0},{2,3},{3,2},{4,5},{5,4},{6,7},{7,6},{8,9},{9,8},{10,11... | collective-permute-start | bytes 2211848 | tf_op jit(solution)/shard_map/ppermute | solution.py:49
  88.7 45.9 %collective-permute-start.5 = (bf16[2,240,768]{2,1,0:T(8,128)(2,1)S(1)}, bf16[2,240,768]{2,1,0:T(8,128)(2,1)}, u32[]{:S(2)}, u32[]{:S(2)}) collective-permute-start(bf16[2,240,768]{2,1,0:T(8,128)(2,1)S(1)} %pad_maximum_fusion.6.refs_0_), channel_id=1, source_target_pairs={{0,4},{2,6},{4,0},{6,2},{8,12},{10,14},{12,8},{14,10},{16,20},{18,... | collective-permute-start | bytes 2211848 | tf_op jit(solution)/shard_map/ppermute | solution.py:49
  110.1 30.9 %collective-permute-start.9 = (bf16[2,240,768]{2,1,0:T(8,128)(2,1)S(1)}, bf16[2,240,768]{2,1,0:T(8,128)(2,1)}, u32[]{:S(2)}, u32[]{:S(2)}) collective-permute-start(bf16[2,240,768]{2,1,0:T(8,128)(2,1)S(1)} %collective-permute-done.8.refs_6_), channel_id=1, source_target_pairs={{0,2},{2,0},{4,6},{6,4},{8,10},{10,8},{12,14},{14,12},{16,18},{18,... | collective-permute-start | bytes 2211848 | tf_op jit(solution)/shard_map/ppermute | solution.py:49
  133.0 133.7 %all-gather.2.cloned.1.call-start = ((), (), s32[]{:S(2)}) async-start(), calls=%async_computation.7 | async-start | bytes 7372800 | tf_op jit(solution)/shard_map/all_gather | solution.py:137
  134.5 29.0 %collective-permute-start.11 = (bf16[2,240,768]{2,1,0:T(8,128)(2,1)}, bf16[2,240,768]{2,1,0:T(8,128)(2,1)}, u32[]{:S(2)}, u32[]{:S(2)}) collective-permute-start(bf16[2,240,768]{2,1,0:T(8,128)(2,1)} %collective-permute-done.4.refs_1_), channel_id=1, source_target_pairs={{0,1},{1,0},{2,3},{3,2},{4,5},{5,4},{6,7},{7,6},{8,9},{9,8},{10,11... | collective-permute-start | bytes 2211848 | tf_op jit(solution)/shard_map/ppermute | solution.py:49
  135.1 27.9 %collective-permute-start.12 = (bf16[2,240,768]{2,1,0:T(8,128)(2,1)}, bf16[2,240,768]{2,1,0:T(8,128)(2,1)}, u32[]{:S(2)}, u32[]{:S(2)}) collective-permute-start(bf16[2,240,768]{2,1,0:T(8,128)(2,1)} %collective-permute-done.5.refs_2_), channel_id=1, source_target_pairs={{0,1},{1,0},{2,3},{3,2},{4,5},{5,4},{6,7},{7,6},{8,9},{9,8},{10,11... | collective-permute-start | bytes 2211848 | tf_op jit(solution)/shard_map/ppermute | solution.py:49
  151.5 33.8 %all-to-all-start.4 = ((bf16[4,4,24,3072]{3,2,1,0:T(8,128)(2,1)}), bf16[4,4,24,3072]{3,2,1,0:T(8,128)(2,1)}, u32[]{:S(2)}, u32[]{:S(2)}) async-start(bf16[4,4,24,3072]{3,2,1,0:T(8,128)(2,1)} %gate.15), calls=%async_computation.4 | async-start | bytes 4718592 | tf_op jit(solution)/shard_map/all_to_all | solution.py:133
  160.1 106.6 %collective-permute-start.25 = (bf16[160,3840]{1,0:T(8,128)(2,1)}, bf16[160,3840]{1,0:T(8,128)(2,1)}, u32[]{:S(2)}, u32[]{:S(2)}) collective-permute-start(bf16[160,3840]{1,0:T(8,128)(2,1)} %get-tuple-element.142), channel_id=1, source_target_pairs={{0,6},{2,4},{4,2},{6,0},{8,14},{10,12},{12,10},{14,8},{16,22},{18,... | collective-permute-start | bytes 3686408 | tf_op jit(solution)/shard_map/ppermute | solution.py:49
  163.0 103.8 %collective-permute-start.23 = (bf16[160,3840]{1,0:T(8,128)(2,1)}, bf16[160,3840]{1,0:T(8,128)(2,1)}, u32[]{:S(2)}, u32[]{:S(2)}) collective-permute-start(bf16[160,3840]{1,0:T(8,128)(2,1)} %get-tuple-element.143), channel_id=1, source_target_pairs={{0,2},{2,0},{4,6},{6,4},{8,10},{10,8},{12,14},{14,12},{16,18},{18,... | collective-permute-start | bytes 3686408 | tf_op jit(solution)/shard_map/ppermute | solution.py:49
  163.5 103.2 %collective-permute-start.24 = (bf16[160,3840]{1,0:T(8,128)(2,1)}, bf16[160,3840]{1,0:T(8,128)(2,1)}, u32[]{:S(2)}, u32[]{:S(2)}) collective-permute-start(bf16[160,3840]{1,0:T(8,128)(2,1)} %get-tuple-element.145), channel_id=1, source_target_pairs={{0,4},{2,6},{4,0},{6,2},{8,12},{10,14},{12,8},{14,10},{16,20},{18,... | collective-permute-start | bytes 3686408 | tf_op jit(solution)/shard_map/ppermute | solution.py:49
  219.8 34.0 %collective-permute-start.22 = (bf16[160,768]{1,0:T(8,128)(2,1)S(1)}, bf16[160,768]{1,0:T(8,128)(2,1)}, u32[]{:S(2)}, u32[]{:S(2)}) collective-permute-start(bf16[160,768]{1,0:T(8,128)(2,1)S(1)} %bitcast.390), channel_id=1, source_target_pairs={{0,2},{2,0},{4,6},{6,4},{8,10},{10,8},{12,14},{14,12},{16,18},{18,... | collective-permute-start | bytes 737288 | tf_op jit(solution)/shard_map/ppermute | solution.py:118
  322.8 50.6 %collective-permute-start.31 = (bf16[4,48,3840]{2,1,0:T(8,128)(2,1)}, bf16[4,48,3840]{2,1,0:T(8,128)(2,1)}, u32[]{:S(2)}, u32[]{:S(2)}) collective-permute-start(bf16[4,48,3840]{2,1,0:T(8,128)(2,1)} %get-tuple-element.129.refs_2_), channel_id=1, source_target_pairs={{24,16},{26,18},{28,20},{30,22},{25,17},{27,19},{29,21},{31,23}} | collective-permute-start | bytes 4423688 | tf_op jit(solution)/shard_map/ppermute | solution.py:164
  324.6 48.8 %collective-permute-start.30 = (bf16[4,48,3840]{2,1,0:T(8,128)(2,1)}, bf16[4,48,3840]{2,1,0:T(8,128)(2,1)}, u32[]{:S(2)}, u32[]{:S(2)}) collective-permute-start(bf16[4,48,3840]{2,1,0:T(8,128)(2,1)} %get-tuple-element.130.refs_1_), channel_id=1, source_target_pairs={{0,8},{2,10},{4,12},{6,14},{1,9},{3,11},{5,13},{7,15}} | collective-permute-start | bytes 4423688 | tf_op jit(solution)/shard_map/ppermute | solution.py:163
  377.6 48.9 %collective-permute-start.37 = (bf16[4,48,3840]{2,1,0:T(8,128)(2,1)S(1)}, bf16[4,48,3840]{2,1,0:T(8,128)(2,1)S(1)}, u32[]{:S(2)}, u32[]{:S(2)}) collective-permute-start(bf16[4,48,3840]{2,1,0:T(8,128)(2,1)S(1)} %get-tuple-element.127.refs_4_), channel_id=1, source_target_pairs={{16,8},{18,10},{20,12},{22,14},{24,16},{26,18},{28,20},{30,22},{17... | collective-permute-start | bytes 4423688 | tf_op jit(solution)/shard_map/ppermute | solution.py:164
  378.4 48.1 %collective-permute-start.36 = (bf16[4,48,3840]{2,1,0:T(8,128)(2,1)S(1)}, bf16[4,48,3840]{2,1,0:T(8,128)(2,1)S(1)}, u32[]{:S(2)}, u32[]{:S(2)}) collective-permute-start(bf16[4,48,3840]{2,1,0:T(8,128)(2,1)S(1)} %get-tuple-element.128.refs_3_), channel_id=1, source_target_pairs={{0,8},{2,10},{4,12},{6,14},{8,16},{10,18},{12,20},{14,22},{1,9},{3... | collective-permute-start | bytes 4423688 | tf_op jit(solution)/shard_map/ppermute | solution.py:163
  392.1 50.6 %collective-permute-start.50 = (bf16[768,768]{1,0:T(8,128)(2,1)}, bf16[768,768]{1,0:T(8,128)(2,1)}, u32[]{:S(2)}, u32[]{:S(2)}) collective-permute-start(bf16[768,768]{1,0:T(8,128)(2,1)} %pad_maximum_fusion.1.refs_0_), channel_id=1, source_target_pairs={{0,2},{2,0},{4,6},{6,4},{8,10},{10,8},{12,14},{14,12},{16,18},{18,... | collective-permute-start | bytes 3538952 | tf_op jit(solution)/shard_map/ppermute | solution.py:49
  394.5 68.7 %collective-permute-start.51 = (bf16[768,768]{1,0:T(8,128)(2,1)}, bf16[768,768]{1,0:T(8,128)(2,1)}, u32[]{:S(2)}, u32[]{:S(2)}) collective-permute-start(bf16[768,768]{1,0:T(8,128)(2,1)} %pad_maximum_fusion.2.refs_1_), channel_id=1, source_target_pairs={{0,4},{2,6},{4,0},{6,2},{8,12},{10,14},{12,8},{14,10},{16,20},{18,... | collective-permute-start | bytes 3538952 | tf_op jit(solution)/shard_map/ppermute | solution.py:49
  411.9 52.7 %collective-permute-start.52 = (bf16[768,768]{1,0:T(8,128)(2,1)S(1)}, bf16[768,768]{1,0:T(8,128)(2,1)}, u32[]{:S(2)}, u32[]{:S(2)}) collective-permute-start(bf16[768,768]{1,0:T(8,128)(2,1)S(1)} %pad_maximum_fusion.3.refs_2_), channel_id=1, source_target_pairs={{0,6},{2,4},{4,2},{6,0},{8,14},{10,12},{12,10},{14,8},{16,22},{18,... | collective-permute-start | bytes 3538952 | tf_op jit(solution)/shard_map/ppermute | solution.py:49
  440.8 48.1 %collective-permute-start.41 = (bf16[4,48,3840]{2,1,0:T(8,128)(2,1)}, bf16[4,48,3840]{2,1,0:T(8,128)(2,1)}, u32[]{:S(2)}, u32[]{:S(2)}) collective-permute-start(bf16[4,48,3840]{2,1,0:T(8,128)(2,1)} %get-tuple-element.121), channel_id=1, source_target_pairs={{8,0},{10,2},{12,4},{14,6},{16,8},{18,10},{20,12},{22,14},{24,16},... | collective-permute-start | bytes 4423688 | tf_op jit(solution)/shard_map/ppermute | solution.py:164
  442.7 46.2 %collective-permute-start.40 = (bf16[4,48,3840]{2,1,0:T(8,128)(2,1)}, bf16[4,48,3840]{2,1,0:T(8,128)(2,1)}, u32[]{:S(2)}, u32[]{:S(2)}) collective-permute-start(bf16[4,48,3840]{2,1,0:T(8,128)(2,1)} %get-tuple-element.122), channel_id=1, source_target_pairs={{0,8},{2,10},{4,12},{6,14},{8,16},{10,18},{12,20},{14,22},{16,24},... | collective-permute-start | bytes 4423688 | tf_op jit(solution)/shard_map/ppermute | solution.py:163
  464.6 28.1 %collective-permute-start.48 = (bf16[384,768]{1,0:T(8,128)(2,1)}, bf16[384,768]{1,0:T(8,128)(2,1)}, u32[]{:S(2)}, u32[]{:S(2)}) collective-permute-start(bf16[384,768]{1,0:T(8,128)(2,1)} %bitcast.144.refs_2_), channel_id=1, source_target_pairs={{0,4},{2,6},{4,0},{6,2},{8,12},{10,14},{12,8},{14,10},{16,20},{18,... | collective-permute-start | bytes 1769480 | tf_op jit(solution)/shard_map/ppermute | solution.py:49
  500.6 29.5 %collective-permute-start.55 = (f32[26112]{0:T(1024)S(1)}, f32[26112]{0:T(1024)S(1)}, u32[]{:S(2)}, u32[]{:S(2)}) collective-permute-start(f32[26112]{0:T(1024)S(1)} %pad_maximum_fusion.12), channel_id=1, source_target_pairs={{0,4},{2,6},{4,0},{6,2},{8,12},{10,14},{12,8},{14,10},{16,20},{18,... | collective-permute-start | bytes 313352 | tf_op jit(solution)/shard_map/ppermute | solution.py:118
  501.4 29.7 %collective-permute-start.56 = (f32[26112]{0:T(1024)S(1)}, f32[26112]{0:T(1024)S(1)}, u32[]{:S(2)}, u32[]{:S(2)}) collective-permute-start(f32[26112]{0:T(1024)S(1)} %pad_maximum_fusion.12), channel_id=1, source_target_pairs={{0,6},{2,4},{4,2},{6,0},{8,14},{10,12},{12,10},{14,8},{16,22},{18,... | collective-permute-start | bytes 313352 | tf_op jit(solution)/shard_map/ppermute | solution.py:118
  503.1 28.1 %collective-permute-start.54 = (f32[26112]{0:T(1024)S(1)}, f32[26112]{0:T(1024)}, u32[]{:S(2)}, u32[]{:S(2)}) collective-permute-start(f32[26112]{0:T(1024)S(1)} %pad_maximum_fusion.12), channel_id=1, source_target_pairs={{0,2},{2,0},{4,6},{6,4},{8,10},{10,8},{12,14},{14,12},{16,18},{18,... | collective-permute-start | bytes 313352 | tf_op jit(solution)/shard_map/ppermute | solution.py:118
  505.3 30.7 %collective-permute-start.46 = (f32[48,3840]{1,0:T(8,128)}, f32[48,3840]{1,0:T(8,128)}, u32[]{:S(2)}, u32[]{:S(2)}) collective-permute-start(f32[48,3840]{1,0:T(8,128)} %get-tuple-element.150.refs_4_), channel_id=1, source_target_pairs={{0,6},{2,4},{4,2},{6,0},{8,14},{10,12},{12,10},{14,8},{16,22},{18,... | collective-permute-start | bytes 2211848 | tf_op jit(solution)/shard_map/ppermute | solution.py:49
  506.8 33.6 %collective-permute-start.45 = (f32[48,3840]{1,0:T(8,128)S(1)}, f32[48,3840]{1,0:T(8,128)}, u32[]{:S(2)}, u32[]{:S(2)}) collective-permute-start(f32[48,3840]{1,0:T(8,128)S(1)} %get-tuple-element.152.refs_3_), channel_id=1, source_target_pairs={{0,4},{2,6},{4,0},{6,2},{8,12},{10,14},{12,8},{14,10},{16,20},{18,... | collective-permute-start | bytes 2211848 | tf_op jit(solution)/shard_map/ppermute | solution.py:49
  507.7 57.0 %all-to-all-start.6 = ((bf16[4,288,768]{2,1,0:T(8,128)(2,1)}), bf16[4,288,768]{2,1,0:T(8,128)(2,1)}, u32[]{:S(2)}, u32[]{:S(2)}) async-start(bf16[4,288,768]{2,1,0:T(8,128)(2,1)} %fusion.15.refs_0_.refs_1_), calls=%async_computation.6 | async-start | bytes 3538944 | tf_op jit(solution)/shard_map/all_to_all | solution.py:133
  (193 other events, 1829.4 us)
Sparse Core Ops, SparseCore 0:
  135.4 110.3 all-gather.1

commit v5 on v4

--- a/solution.py
+++ b/solution.py
@@ -323,15 +323,16 @@
                 :, low * HIGH_COUNT : (low + 1) * HIGH_COUNT
             ].astype(jnp.bfloat16)
 
-    ids = ids_ref[0]
-    low_ids = ids >> 9
-    row = lax.broadcasted_iota(jnp.int32, (HIGH_COUNT, ids.shape[1]), 0)
-    match = (row == (ids & (HIGH_COUNT - 1))).astype(jnp.bfloat16)
-    found = jnp.dot(spread[...], match, preferred_element_type=jnp.float32)
-    total = jnp.zeros((width, ids.shape[1]), jnp.float32)
-    for low in range(low_count):
-        total = jnp.where(low_ids == low, found[low * width : (low + 1) * width, :], total)
-    out_ref[0] = total.astype(out_ref.dtype)
+    for block in range(ids_ref.shape[0]):
+        ids = ids_ref[block]
+        low_ids = ids >> 9
+        row = lax.broadcasted_iota(jnp.int32, (HIGH_COUNT, ids.shape[1]), 0)
+        match = (row == (ids & (HIGH_COUNT - 1))).astype(jnp.bfloat16)
+        found = jnp.dot(spread[...], match, preferred_element_type=jnp.float32)
+        total = jnp.zeros((width, ids.shape[1]), jnp.float32)
+        for low in range(low_count):
+            total = jnp.where(low_ids == low, found[low * width : (low + 1) * width, :], total)
+        out_ref[block] = total.astype(out_ref.dtype)
 
 
 def lookup(table_t, ids, *needed):
@@ -340,15 +341,16 @@
     width, vocab = table_t.shape
     blocks, _, length = ids.shape
     low_count = vocab // HIGH_COUNT
+    group = math.gcd(2, blocks)
     found = pl.pallas_call(
         functools.partial(lookup_kernel, low_count),
-        grid=(blocks,),
+        grid=(blocks // group,),
         in_specs=[
-            pl.BlockSpec((1, 1, length), lambda i: (i, 0, 0)),
+            pl.BlockSpec((group, 1, length), lambda i: (i, 0, 0)),
             pl.BlockSpec((width, vocab), lambda i: (0, 0)),
         ]
         + [pl.BlockSpec(memory_space=pl.ANY)] * len(needed),
-        out_specs=pl.BlockSpec((1, width, length), lambda i: (i, 0, 0)),
+        out_specs=pl.BlockSpec((group, width, length), lambda i: (i, 0, 0)),
         out_shape=jax.ShapeDtypeStruct((blocks, width, length), jnp.bfloat16),
         scratch_shapes=[pltpu.VMEM((low_count * width, HIGH_COUNT), jnp.bfloat16)],
         compiler_params=pltpu.CompilerParams(vmem_limit_bytes=40 * 1024 * 1024),
@@ -371,15 +373,20 @@
     def _():
         total[...] = jnp.zeros_like(total)
 
-    ids = ids_ref[0]
-    low_ids = ids >> 9
-    grad = grad_ref[0].astype(jnp.float32)
-    for low in range(low_count):
-        lhs[low * width : (low + 1) * width, :] = jnp.where(low_ids == low, grad, 0.0).astype(
-            jnp.bfloat16
-        )
-    row = lax.broadcasted_iota(jnp.int32, (HIGH_COUNT, ids.shape[1]), 0)
-    match = (row == (ids & (HIGH_COUNT - 1))).astype(jnp.bfloat16)
+    length = ids_ref.shape[2]
+    matches = []
+    for block in range(ids_ref.shape[0]):
+        ids = ids_ref[block]
+        low_ids = ids >> 9
+        grad = grad_ref[block].astype(jnp.float32)
+        part = slice(block * length, (block + 1) * length)
+        for low in range(low_count):
+            lhs[low * width : (low + 1) * width, part] = jnp.where(low_ids == low, grad, 0.0).astype(
+                jnp.bfloat16
+            )
+        row = lax.broadcasted_iota(jnp.int32, (HIGH_COUNT, length), 0)
+        matches.append((row == (ids & (HIGH_COUNT - 1))).astype(jnp.bfloat16))
+    match = jnp.concatenate(matches, 1)
     total[...] += lax.dot_general(
         lhs[...], match, (((1,), (1,)), ((), ())), preferred_element_type=jnp.float32
     )
@@ -397,18 +404,19 @@
     width = grads.shape[1]
     blocks, _, length = ids.shape
     low_count = vocab // HIGH_COUNT
+    group = math.gcd(2, blocks)
     summed = pl.pallas_call(
         functools.partial(spread_kernel, low_count),
-        grid=(blocks,),
+        grid=(blocks // group,),
         in_specs=[
-            pl.BlockSpec((1, 1, length), lambda i: (i, 0, 0)),
-            pl.BlockSpec((1, width, length), lambda i: (i, 0, 0)),
+            pl.BlockSpec((group, 1, length), lambda i: (i, 0, 0)),
+            pl.BlockSpec((group, width, length), lambda i: (i, 0, 0)),
         ]
         + [pl.BlockSpec(memory_space=pl.ANY)] * len(needed),
         out_specs=pl.BlockSpec((width, vocab), lambda i: (0, 0)),
         out_shape=jax.ShapeDtypeStruct((width, vocab), jnp.float32),
         scratch_shapes=[
-            pltpu.VMEM((low_count * width, length), jnp.bfloat16),
+            pltpu.VMEM((low_count * width, group * length), jnp.bfloat16),
             pltpu.VMEM((low_count * width, HIGH_COUNT), jnp.float32),
         ],
         compiler_params=pltpu.CompilerParams(vmem_limit_bytes=40 * 1024 * 1024),

time: 626 us -> 624 us (level)
  Pallas kernels: 141 us -> 134 us
    pallas_call x4, Pallas kernels: 63.8 us -> 57.3 us  [the longest x2 28.7 us: spread_add(): pl.pallas_call(functools.partial(spread_kernel, low_count), grid=(blocks...]
  transfers between devices with their start and end apart: 75 -> 75, of which waited for: 22 -> 22; matrix products, arithmetic and copies ran while one was open for 26% -> 26% of each run, Pallas kernels for 18% -> 17%
where the time goes in v5:
time: 624 us; the launch traced here: 613 us
  starting transfers between devices  136 us (22%)
  Pallas kernels  134 us (21%)
  other arithmetic  100 us (16%)
  waiting for transfers between devices  98.9 us (16%)
  local copies, waits for them, and re-layouts  65.4 us (10%)
  matrix products  50.1 us (8%)
  between operations  27.2 us (4%)
    ppermute x49, waiting for transfers between devices, swap(): return lax.ppermute(x, axis, [(i, i ^ bit) for i in range(size)])  75.5 us
    ppermute x12, starting transfers between devices, near_exchange(): lax.ppermute(take(p ^ k), 'fsdp', [(i, i ^ k) for i in range(size)])  40.6 us
    ppermute x49, starting transfers between devices, swap(): return lax.ppermute(x, axis, [(i, i ^ bit) for i in range(size)])  38.4 us
    pallas_call x2, Pallas kernels, spread_add(): pl.pallas_call(functools.partial(spread_kernel, low_count), grid=(blocks...  28.7 us
    pallas_call x2, Pallas kernels, lookup(): pl.pallas_call(functools.partial(lookup_kernel, low_count), grid=(blocks...  28.7 us
    unnamed x314, local copies, waits for them, and re-layouts  26.9 us
    all_to_all x5, starting transfers between devices, exchange(): return lax.all_to_all(x, 'fsdp', 0, 0, tiled=True, axis_index_groups=groups)  25.7 us
    dot_general x4, matrix products, project_back(): jnp.einsum('az,zh->ah', gradient, weight_matrix, preferred_element_type=j...  17.2 us
  transfers between devices with their start and end apart: 75, of which 22 were waited for; matrix products, arithmetic and copies ran while one was open for 26% of the time, Pallas kernels for 17%

profile of v5, /device:TPU:0, one launch (start us, length us, event | category | flops | bytes accessed | tf_op | source)
XLA Modules:
  0.0 612.8 jit_solution(4577502193996953748)
XLA Ops:
  8.5 8.3 %all-to-all-start = ((s32[16,2,512]{2,1,0:T(2,128)}), s32[16,2,512]{2,1,0:T(2,128)S(1)}, u32[]{:S(2)}, u32[]{:S(2)}) async-start(s32[16,2,512]{2,1,0:T(2,128)} %broadcast_in_dim.68), calls=%async_computation | async-start | bytes 131072 | tf_op jit(solution)/shard_map/all_to_all | solution.py:998
  38.4 14.6 %lookup.2.refs_0_ = bf16[16,48,512]{2,1,0:T(8,128)(2,1)} custom-call(s32[16,1,512]{2,1,0:T(1,128)S(1)} %get-tuple-element.189.ids_ref, f32[48,15360]{1,0:T(8,128)S(1)} %bitcast.347, bf16[240,768]{1,0:T(8,128)(2,1)S(1)} %copy-done.12), custom_call_target="tpu_custom_call" | custom-call | flops 12079595520 | bytes 3735552 | tf_op jit(solution)/shard_map/lookup/pallas_call | solution.py:345
  53.1 14.0 %lookup.3.refs_3_ = bf16[16,48,512]{2,1,0:T(8,128)(2,1)S(1)} custom-call(s32[16,1,512]{2,1,0:T(1,128)S(1)} %get-tuple-element.190.ids_ref, f32[48,15360]{1,0:T(8,128)S(1)} %bitcast.348, bf16[16,48,512]{2,1,0:T(8,128)(2,1)} %lookup.2.refs_0_, bf16[192,3840]{1,0:T(8,128)(2,1)} %bitcast.6.refs_1_), custom_call_target="tpu_custom_call" | custom-call | flops 12079595520 | bytes 3735552 | tf_op jit(solution)/shard_map/lookup/pallas_call | solution.py:345
  70.1 7.5 %all-to-all-start.2 = ((bf16[16,1,48,512]{3,2,1,0:T(8,128)(2,1)}), bf16[16,1,48,512]{3,2,1,0:T(8,128)(2,1)}, u32[]{:S(2)}, u32[]{:S(2)}) async-start(bf16[16,1,48,512]{3,2,1,0:T(8,128)(2,1)} %add_bitcast_fusion), calls=%async_computation.2 | async-start | bytes 1572864 | tf_op jit(solution)/shard_map/all_to_all | solution.py:133
  86.2 19.0 %collective-permute-done.8.refs_6_ = bf16[2,240,768]{2,1,0:T(8,128)(2,1)S(1)} collective-permute-done((bf16[2,240,768]{2,1,0:T(8,128)(2,1)S(1)}, bf16[2,240,768]{2,1,0:T(8,128)(2,1)S(1)}, u32[]{:S(2)}, u32[]{:S(2)}) %collective-permute-start.8) | collective-permute-done | bytes 737312 | tf_op jit(solution)/shard_map/ppermute | solution.py:49
  108.5 14.6 %collective-permute-done.4.refs_1_ = bf16[2,240,768]{2,1,0:T(8,128)(2,1)} collective-permute-done((bf16[2,240,768]{2,1,0:T(8,128)(2,1)S(1)}, bf16[2,240,768]{2,1,0:T(8,128)(2,1)}, u32[]{:S(2)}, u32[]{:S(2)}) %collective-permute-start.4) | collective-permute-done | bytes 737312 | tf_op jit(solution)/shard_map/ppermute | solution.py:49
  132.3 5.9 collective-permute-done.9.refs_7_.refs_2_
  140.4 5.4 constant_dynamic-slice_fusion.2
  161.8 9.5 %place.2 = (bf16[12,192,768]{2,1,0:T(8,128)(2,1)}, bf16[4,192,768]{2,1,0:T(8,128)(2,1)S(1)}, bf16[16,192,768]{2,1,0:T(8,128)(2,1)}, bf16[32,48,768]{2,1,0:T(8,128)(2,1)}) custom-call(s32[32]{0:T(128)S(1)} %stack.292.order_ref, bf16[2,240,768]{2,1,0:T(8,128)(2,1)S(1)} %pad_maximum_fusion.6.refs_0_, bf16[2,240,768]{2,1,0:T(8,128)(2,1)} %collective-permute-done.4.refs_1_, ...), custom_call_target="tpu_custom_call" | custom-call | tf_op jit(solution)/shard_map/place/pallas_call | solution.py:298
  187.0 9.4 %attend.1.refs_3_ = bf16[512,768]{1,0:T(8,128)(2,1)S(1)} custom-call(s32[1]{0:T(128)} %dynamic_slice.169.lengths_ref, bf16[512,2304]{1,0:T(8,128)(2,1)S(1)} %fusion.8.query_ref.key_ref.value_ref, bf16[512,2304]{1,0:T(8,128)(2,1)S(1)} %fusion.8.query_ref.key_ref.value_ref, bf16[512,2304]{1,0:T(8,128)(2,1)S(1)} %fusion.8.query_ref.key_ref.value_ref, ...), custom_call_target="tpu_custom_call" | custom-call | flops 1 | bytes 1 | tf_op jit(solution)/shard_map/attend/pallas_call | solution.py:510
  198.1 4.8 multiply_convert_fusion
  216.8 27.7 %collective-permute-start.22 = (bf16[160,768]{1,0:T(8,128)(2,1)S(1)}, bf16[160,768]{1,0:T(8,128)(2,1)}, u32[]{:S(2)}, u32[]{:S(2)}) collective-permute-start(bf16[160,768]{1,0:T(8,128)(2,1)S(1)} %bitcast.390), channel_id=1, source_target_pairs={{0,2},{2,0},{4,6},{6,4},{8,10},{10,8},{12,14},{14,12},{16,18},{18,... | collective-permute-start | bytes 737288 | tf_op jit(solution)/shard_map/ppermute | solution.py:118
  246.0 4.8 collective-permute-done.22
  263.8 13.9 %head.1 = (f32[640,3840]{1,0:T(8,128)}, f32[4,8,160]{2,1,0:T(8,128)}) custom-call(s32[1]{0:T(128)} %bitcast.101.place_ref, bf16[640,768]{1,0:T(8,128)(2,1)} %bitcast.375, bf16[768,3840]{1,0:T(8,128)(2,1)} %all-gather.2.cloned.1.call-done.table_ref, f32[1,3840]{1,0:T(1,128)} %broadcast_in_dim.134.bias_ref, bf16[160,3840]{1,0:T(8,128)(2,1)} %get-tuple-element.144.refs_0_, ...), custom_call_target="tpu_custom_call" | custom-call | flops 1 | bytes 1 | tf_op jit(solution)/shard_map/head/pallas_call | solution.py:632
  287.8 15.2 %head_back.1 = (bf16[640,3840]{1,0:T(8,128)(2,1)}, f32[640,768]{1,0:T(8,128)}, f32[1,3840]{1,0:T(1,128)}, f32[4,1,160]{2,1,0:T(1,128)}) custom-call(s32[1]{0:T(128)} %bitcast.101.place_ref, f32[640,3840]{1,0:T(8,128)} %get-tuple-element.58.logits_ref, f32[8,4,8,160]{3,2,1,0:T(8,128)} %copy-done.67, f32[4,1,160]{2,1,0:T(1,128)} %broadcast_select_fusion.scale_ref, ...), custom_call_target="tpu_custom_call" | custom-call | flops 1 | bytes 1 | tf_op jit(solution)/shard_map/head_back/pallas_call | solution.py:703
  304.5 7.3 %fusion.6 = f32[4,4,48,3840]{3,2,1,0:T(8,128)S(1)} fusion(bf16[4,4,48,640]{3,2,1,0:T(8,128)(2,1)S(1)} %bitcast.389, bf16[640,3840]{1,0:T(8,128)(2,1)} %get-tuple-element.60), kind=kOutput, calls=%fused_computation.12 | convolution fusion | flops 3774873600 | bytes 17694720 | tf_op jit(solution)/shard_map/dot_general | solution.py:1184
  336.7 8.0 %fusion.5.refs_0_ = bf16[512,3072]{1,0:T(8,128)(2,1)S(1)} fusion(f32[512,3072]{1,0:T(8,128)} %get-tuple-element.221, bf16[512,768]{1,0:T(8,128)(2,1)S(1)} %get-tuple-element.106, bf16[768,3072]{1,0:T(8,128)(2,1)} %bitcast.354, f32[3072]{0:T(1024)S(1)} %slice.186), kind=kOutput, calls=%fused_computation.8 | convolution fusion | flops 2433220608 | bytes 14954496 | tf_op jit(solution)/shard_map/az,zh->ah/dot_general | solution.py:455
  353.9 6.5 %fusion.133 = f32[768,3072]{1,0:T(8,128)S(1)} fusion(bf16[512,768]{1,0:T(8,128)(2,1)} %copy-done.50, bf16[512,3072]{1,0:T(8,128)(2,1)} %copy-done.51), kind=kOutput, calls=%fused_computation.366 | convolution fusion | flops 2415919104 | bytes 13369344 | tf_op jit(solution)/shard_map/bu,bw->uw/dot_general | solution.py:459
  379.8 4.8 convert_add_fusion
  392.4 16.6 %attend_back.1.refs_0_ = bf16[512,2304]{1,0:T(8,128)(2,1)S(1)} custom-call(s32[1]{0:T(128)} %dynamic_slice.169.lengths_ref, bf16[512,2304]{1,0:T(8,128)(2,1)S(1)} %fusion.8.query_ref.key_ref.value_ref, bf16[512,2304]{1,0:T(8,128)(2,1)S(1)} %fusion.8.query_ref.key_ref.value_ref, bf16[512,2304]{1,0:T(8,128)(2,1)S(1)} %fusion.8.query_ref.key_ref.value_ref, ...), custom_call_target="tpu_custom_call" | custom-call | flops 1 | bytes 1 | tf_op jit(solution)/shard_map/attend_back/pallas_call | solution.py:570
  415.3 4.7 weight_sums.3
  432.0 5.9 fusion.10
  439.8 5.8 collective-permute-start.40
  445.6 7.8 %all-to-all-done.5 = bf16[16,1,48,512]{3,2,1,0:T(8,128)(2,1)S(1)} async-done(((bf16[16,1,48,512]{3,2,1,0:T(8,128)(2,1)}), bf16[16,1,48,512]{3,2,1,0:T(8,128)(2,1)S(1)}, u32[]{:S(2)}, u32[]{:S(2)}) %all-to-all-start.5) | async-done | bytes 786464 | tf_op jit(solution)/shard_map/all_to_all | solution.py:1220
  455.4 4.8 convert_add_fusion.4
  468.3 14.3 %spread_add.2.refs_2_.refs_3_ = f32[48,15360]{1,0:T(8,128)S(1)} custom-call(s32[16,1,512]{2,1,0:T(1,128)S(1)} %copy-done.25, bf16[16,48,512]{2,1,0:T(8,128)(2,1)S(1)} %bitcast.352, bf16[16,48,512]{2,1,0:T(8,128)(2,1)S(1)} %collective-permute-done.42.refs_0_.grad_ref, bf16[384,768]{1,0:T(8,128)(2,1)S(1)} %bitcast.363, bf16[384,768]{1,0:T(8,128)(2,1)} %bitcast.144.refs_2_, ...), custom_call_target="tpu_custom_call" | custom-call | flops 1 | bytes 1 | tf_op jit(solution)/shard_map/spread_add/pallas_call | solution.py:408
  484.3 5.6 collective-permute-done.48.refs_1_
  509.5 14.3 %spread_add.3.refs_3_ = f32[48,15360]{1,0:T(8,128)S(1)} custom-call(s32[16,1,512]{2,1,0:T(1,128)S(1)} %copy-done.23, bf16[16,48,512]{2,1,0:T(8,128)(2,1)S(1)} %collective-permute-done.42.refs_0_.grad_ref, bf16[4,288,768]{2,1,0:T(8,128)(2,1)} %fusion.15.refs_0_.refs_1_, f32[48,3840]{1,0:T(8,128)S(1)} %get-tuple-element.151.refs_1_, ...), custom_call_target="tpu_custom_call" | custom-call | flops 1 | bytes 1 | tf_op jit(solution)/shard_map/spread_add/pallas_call | solution.py:408
  531.9 5.6 collective-permute-done.45.refs_1_
  537.5 5.4 collective-permute-done.44.refs_0_
  548.7 10.5 %collective-permute-done.58 = f32[26112]{0:T(1024)S(1)} collective-permute-done((f32[26112]{0:T(1024)S(1)}, f32[26112]{0:T(1024)S(1)}, u32[]{:S(2)}, u32[]{:S(2)}) %collective-permute-start.58) | collective-permute-done | bytes 104480 | tf_op jit(solution)/shard_map/ppermute | solution.py:49
  596.4 6.9 %subtract_bitcast_fusion = (f32[15360,48]{0,1:T(8,128)}, f32[15360,48]{0,1:T(8,128)}, f32[15360,48]{0,1:T(8,128)}) fusion(f32[48,15360]{1,0:T(8,128)S(1)} %get-tuple-element.104, f32[]{:T(128)S(6)} %min.32, f32[15360,48]{0,1:T(8,128)S(1)} %copy-done.53, f32[15360,48]{0,1:T(8,128)} %param.36, f32[15360,48]{0,1:T(8,128)S(1)} %copy-done.7), kind=kLoop, calls=%fused_computation.37 | loop fusion | flops 11796480 | bytes 20643844 | tf_op jit(solution)/shard_map/transpose | solution.py:1312
  (634 shorter events, 276.4 us)
Async XLA Ops:
  32.8 44.7 %collective-permute-start.3 = (bf16[240,768]{1,0:T(8,128)(2,1)}, bf16[240,768]{1,0:T(8,128)(2,1)S(1)}, u32[]{:S(2)}, u32[]{:S(2)}) collective-permute-start(bf16[240,768]{1,0:T(8,128)(2,1)} %gate.12.refs_0_), channel_id=1, source_target_pairs={{0,24},{2,26},{4,28},{6,30},{8,16},{10,18},{12,20},{14,22},{16,8},... | collective-permute-start | bytes 1105928 | tf_op jit(solution)/shard_map/ppermute | solution.py:49
  36.6 41.0 %collective-permute-start.2 = (bf16[240,768]{1,0:T(8,128)(2,1)}, bf16[240,768]{1,0:T(8,128)(2,1)}, u32[]{:S(2)}, u32[]{:S(2)}) collective-permute-start(bf16[240,768]{1,0:T(8,128)(2,1)} %gate.12.refs_0_), channel_id=1, source_target_pairs={{0,16},{2,18},{4,20},{6,22},{8,24},{10,26},{12,28},{14,30},{16,0},... | collective-permute-start | bytes 1105928 | tf_op jit(solution)/shard_map/ppermute | solution.py:49
  36.6 41.0 %collective-permute-start.1 = (bf16[240,768]{1,0:T(8,128)(2,1)}, bf16[240,768]{1,0:T(8,128)(2,1)}, u32[]{:S(2)}, u32[]{:S(2)}) collective-permute-start(bf16[240,768]{1,0:T(8,128)(2,1)} %gate.12.refs_0_), channel_id=1, source_target_pairs={{0,8},{2,10},{4,12},{6,14},{8,0},{10,2},{12,4},{14,6},{16,24},{18,... | collective-permute-start | bytes 1105928 | tf_op jit(solution)/shard_map/ppermute | solution.py:49
  70.1 54.7 %all-to-all-start.2 = ((bf16[16,1,48,512]{3,2,1,0:T(8,128)(2,1)}), bf16[16,1,48,512]{3,2,1,0:T(8,128)(2,1)}, u32[]{:S(2)}, u32[]{:S(2)}) async-start(bf16[16,1,48,512]{3,2,1,0:T(8,128)(2,1)} %add_bitcast_fusion), calls=%async_computation.2 | async-start | bytes 1572864 | tf_op jit(solution)/shard_map/all_to_all | solution.py:133
  84.1 39.0 %collective-permute-start.4 = (bf16[2,240,768]{2,1,0:T(8,128)(2,1)S(1)}, bf16[2,240,768]{2,1,0:T(8,128)(2,1)}, u32[]{:S(2)}, u32[]{:S(2)}) collective-permute-start(bf16[2,240,768]{2,1,0:T(8,128)(2,1)S(1)} %pad_maximum_fusion.6.refs_0_), channel_id=1, source_target_pairs={{0,2},{2,0},{4,6},{6,4},{8,10},{10,8},{12,14},{14,12},{16,18},{18,... | collective-permute-start | bytes 2211848 | tf_op jit(solution)/shard_map/ppermute | solution.py:49
  85.7 45.9 %collective-permute-start.10 = (bf16[2,240,768]{2,1,0:T(8,128)(2,1)S(1)}, bf16[2,240,768]{2,1,0:T(8,128)(2,1)}, u32[]{:S(2)}, u32[]{:S(2)}) collective-permute-start(bf16[2,240,768]{2,1,0:T(8,128)(2,1)S(1)} %pad_maximum_fusion.6.refs_0_), channel_id=1, source_target_pairs={{0,1},{1,0},{2,3},{3,2},{4,5},{5,4},{6,7},{7,6},{8,9},{9,8},{10,11... | collective-permute-start | bytes 2211848 | tf_op jit(solution)/shard_map/ppermute | solution.py:49
  85.8 45.9 %collective-permute-start.5 = (bf16[2,240,768]{2,1,0:T(8,128)(2,1)S(1)}, bf16[2,240,768]{2,1,0:T(8,128)(2,1)}, u32[]{:S(2)}, u32[]{:S(2)}) collective-permute-start(bf16[2,240,768]{2,1,0:T(8,128)(2,1)S(1)} %pad_maximum_fusion.6.refs_0_), channel_id=1, source_target_pairs={{0,4},{2,6},{4,0},{6,2},{8,12},{10,14},{12,8},{14,10},{16,20},{18,... | collective-permute-start | bytes 2211848 | tf_op jit(solution)/shard_map/ppermute | solution.py:49
  107.2 30.9 %collective-permute-start.9 = (bf16[2,240,768]{2,1,0:T(8,128)(2,1)S(1)}, bf16[2,240,768]{2,1,0:T(8,128)(2,1)}, u32[]{:S(2)}, u32[]{:S(2)}) collective-permute-start(bf16[2,240,768]{2,1,0:T(8,128)(2,1)S(1)} %collective-permute-done.8.refs_6_), channel_id=1, source_target_pairs={{0,2},{2,0},{4,6},{6,4},{8,10},{10,8},{12,14},{14,12},{16,18},{18,... | collective-permute-start | bytes 2211848 | tf_op jit(solution)/shard_map/ppermute | solution.py:49
  130.1 133.7 %all-gather.2.cloned.1.call-start = ((), (), s32[]{:S(2)}) async-start(), calls=%async_computation.7 | async-start | bytes 7372800 | tf_op jit(solution)/shard_map/all_gather | solution.py:137
  131.6 29.0 %collective-permute-start.11 = (bf16[2,240,768]{2,1,0:T(8,128)(2,1)}, bf16[2,240,768]{2,1,0:T(8,128)(2,1)}, u32[]{:S(2)}, u32[]{:S(2)}) collective-permute-start(bf16[2,240,768]{2,1,0:T(8,128)(2,1)} %collective-permute-done.4.refs_1_), channel_id=1, source_target_pairs={{0,1},{1,0},{2,3},{3,2},{4,5},{5,4},{6,7},{7,6},{8,9},{9,8},{10,11... | collective-permute-start | bytes 2211848 | tf_op jit(solution)/shard_map/ppermute | solution.py:49
  132.2 27.9 %collective-permute-start.12 = (bf16[2,240,768]{2,1,0:T(8,128)(2,1)}, bf16[2,240,768]{2,1,0:T(8,128)(2,1)}, u32[]{:S(2)}, u32[]{:S(2)}) collective-permute-start(bf16[2,240,768]{2,1,0:T(8,128)(2,1)} %collective-permute-done.5.refs_2_), channel_id=1, source_target_pairs={{0,1},{1,0},{2,3},{3,2},{4,5},{5,4},{6,7},{7,6},{8,9},{9,8},{10,11... | collective-permute-start | bytes 2211848 | tf_op jit(solution)/shard_map/ppermute | solution.py:49
  148.6 33.8 %all-to-all-start.4 = ((bf16[4,4,24,3072]{3,2,1,0:T(8,128)(2,1)}), bf16[4,4,24,3072]{3,2,1,0:T(8,128)(2,1)}, u32[]{:S(2)}, u32[]{:S(2)}) async-start(bf16[4,4,24,3072]{3,2,1,0:T(8,128)(2,1)} %gate.15), calls=%async_computation.4 | async-start | bytes 4718592 | tf_op jit(solution)/shard_map/all_to_all | solution.py:133
  157.2 106.6 %collective-permute-start.25 = (bf16[160,3840]{1,0:T(8,128)(2,1)}, bf16[160,3840]{1,0:T(8,128)(2,1)}, u32[]{:S(2)}, u32[]{:S(2)}) collective-permute-start(bf16[160,3840]{1,0:T(8,128)(2,1)} %get-tuple-element.142), channel_id=1, source_target_pairs={{0,6},{2,4},{4,2},{6,0},{8,14},{10,12},{12,10},{14,8},{16,22},{18,... | collective-permute-start | bytes 3686408 | tf_op jit(solution)/shard_map/ppermute | solution.py:49
  160.1 103.7 %collective-permute-start.23 = (bf16[160,3840]{1,0:T(8,128)(2,1)}, bf16[160,3840]{1,0:T(8,128)(2,1)}, u32[]{:S(2)}, u32[]{:S(2)}) collective-permute-start(bf16[160,3840]{1,0:T(8,128)(2,1)} %get-tuple-element.143), channel_id=1, source_target_pairs={{0,2},{2,0},{4,6},{6,4},{8,10},{10,8},{12,14},{14,12},{16,18},{18,... | collective-permute-start | bytes 3686408 | tf_op jit(solution)/shard_map/ppermute | solution.py:49
  160.6 103.2 %collective-permute-start.24 = (bf16[160,3840]{1,0:T(8,128)(2,1)}, bf16[160,3840]{1,0:T(8,128)(2,1)}, u32[]{:S(2)}, u32[]{:S(2)}) collective-permute-start(bf16[160,3840]{1,0:T(8,128)(2,1)} %get-tuple-element.145), channel_id=1, source_target_pairs={{0,4},{2,6},{4,0},{6,2},{8,12},{10,14},{12,8},{14,10},{16,20},{18,... | collective-permute-start | bytes 3686408 | tf_op jit(solution)/shard_map/ppermute | solution.py:49
  216.8 34.0 %collective-permute-start.22 = (bf16[160,768]{1,0:T(8,128)(2,1)S(1)}, bf16[160,768]{1,0:T(8,128)(2,1)}, u32[]{:S(2)}, u32[]{:S(2)}) collective-permute-start(bf16[160,768]{1,0:T(8,128)(2,1)S(1)} %bitcast.390), channel_id=1, source_target_pairs={{0,2},{2,0},{4,6},{6,4},{8,10},{10,8},{12,14},{14,12},{16,18},{18,... | collective-permute-start | bytes 737288 | tf_op jit(solution)/shard_map/ppermute | solution.py:118
  319.9 50.6 %collective-permute-start.31 = (bf16[4,48,3840]{2,1,0:T(8,128)(2,1)}, bf16[4,48,3840]{2,1,0:T(8,128)(2,1)}, u32[]{:S(2)}, u32[]{:S(2)}) collective-permute-start(bf16[4,48,3840]{2,1,0:T(8,128)(2,1)} %get-tuple-element.129.refs_2_), channel_id=1, source_target_pairs={{24,16},{26,18},{28,20},{30,22},{25,17},{27,19},{29,21},{31,23}} | collective-permute-start | bytes 4423688 | tf_op jit(solution)/shard_map/ppermute | solution.py:164
  321.7 48.8 %collective-permute-start.30 = (bf16[4,48,3840]{2,1,0:T(8,128)(2,1)}, bf16[4,48,3840]{2,1,0:T(8,128)(2,1)}, u32[]{:S(2)}, u32[]{:S(2)}) collective-permute-start(bf16[4,48,3840]{2,1,0:T(8,128)(2,1)} %get-tuple-element.130.refs_1_), channel_id=1, source_target_pairs={{0,8},{2,10},{4,12},{6,14},{1,9},{3,11},{5,13},{7,15}} | collective-permute-start | bytes 4423688 | tf_op jit(solution)/shard_map/ppermute | solution.py:163
  374.7 48.9 %collective-permute-start.37 = (bf16[4,48,3840]{2,1,0:T(8,128)(2,1)S(1)}, bf16[4,48,3840]{2,1,0:T(8,128)(2,1)S(1)}, u32[]{:S(2)}, u32[]{:S(2)}) collective-permute-start(bf16[4,48,3840]{2,1,0:T(8,128)(2,1)S(1)} %get-tuple-element.127.refs_4_), channel_id=1, source_target_pairs={{16,8},{18,10},{20,12},{22,14},{24,16},{26,18},{28,20},{30,22},{17... | collective-permute-start | bytes 4423688 | tf_op jit(solution)/shard_map/ppermute | solution.py:164
  375.5 48.1 %collective-permute-start.36 = (bf16[4,48,3840]{2,1,0:T(8,128)(2,1)S(1)}, bf16[4,48,3840]{2,1,0:T(8,128)(2,1)S(1)}, u32[]{:S(2)}, u32[]{:S(2)}) collective-permute-start(bf16[4,48,3840]{2,1,0:T(8,128)(2,1)S(1)} %get-tuple-element.128.refs_3_), channel_id=1, source_target_pairs={{0,8},{2,10},{4,12},{6,14},{8,16},{10,18},{12,20},{14,22},{1,9},{3... | collective-permute-start | bytes 4423688 | tf_op jit(solution)/shard_map/ppermute | solution.py:163
  389.2 50.6 %collective-permute-start.50 = (bf16[768,768]{1,0:T(8,128)(2,1)}, bf16[768,768]{1,0:T(8,128)(2,1)}, u32[]{:S(2)}, u32[]{:S(2)}) collective-permute-start(bf16[768,768]{1,0:T(8,128)(2,1)} %pad_maximum_fusion.1.refs_0_), channel_id=1, source_target_pairs={{0,2},{2,0},{4,6},{6,4},{8,10},{10,8},{12,14},{14,12},{16,18},{18,... | collective-permute-start | bytes 3538952 | tf_op jit(solution)/shard_map/ppermute | solution.py:49
  391.6 68.7 %collective-permute-start.51 = (bf16[768,768]{1,0:T(8,128)(2,1)}, bf16[768,768]{1,0:T(8,128)(2,1)}, u32[]{:S(2)}, u32[]{:S(2)}) collective-permute-start(bf16[768,768]{1,0:T(8,128)(2,1)} %pad_maximum_fusion.2.refs_1_), channel_id=1, source_target_pairs={{0,4},{2,6},{4,0},{6,2},{8,12},{10,14},{12,8},{14,10},{16,20},{18,... | collective-permute-start | bytes 3538952 | tf_op jit(solution)/shard_map/ppermute | solution.py:49
  409.0 52.7 %collective-permute-start.52 = (bf16[768,768]{1,0:T(8,128)(2,1)S(1)}, bf16[768,768]{1,0:T(8,128)(2,1)}, u32[]{:S(2)}, u32[]{:S(2)}) collective-permute-start(bf16[768,768]{1,0:T(8,128)(2,1)S(1)} %pad_maximum_fusion.3.refs_2_), channel_id=1, source_target_pairs={{0,6},{2,4},{4,2},{6,0},{8,14},{10,12},{12,10},{14,8},{16,22},{18,... | collective-permute-start | bytes 3538952 | tf_op jit(solution)/shard_map/ppermute | solution.py:49
  437.9 46.4 %collective-permute-start.41 = (bf16[4,48,3840]{2,1,0:T(8,128)(2,1)}, bf16[4,48,3840]{2,1,0:T(8,128)(2,1)}, u32[]{:S(2)}, u32[]{:S(2)}) collective-permute-start(bf16[4,48,3840]{2,1,0:T(8,128)(2,1)} %get-tuple-element.121), channel_id=1, source_target_pairs={{8,0},{10,2},{12,4},{14,6},{16,8},{18,10},{20,12},{22,14},{24,16},... | collective-permute-start | bytes 4423688 | tf_op jit(solution)/shard_map/ppermute | solution.py:164
  439.8 44.5 %collective-permute-start.40 = (bf16[4,48,3840]{2,1,0:T(8,128)(2,1)}, bf16[4,48,3840]{2,1,0:T(8,128)(2,1)}, u32[]{:S(2)}, u32[]{:S(2)}) collective-permute-start(bf16[4,48,3840]{2,1,0:T(8,128)(2,1)} %get-tuple-element.122), channel_id=1, source_target_pairs={{0,8},{2,10},{4,12},{6,14},{8,16},{10,18},{12,20},{14,22},{16,24},... | collective-permute-start | bytes 4423688 | tf_op jit(solution)/shard_map/ppermute | solution.py:163
  461.7 28.1 %collective-permute-start.48 = (bf16[384,768]{1,0:T(8,128)(2,1)}, bf16[384,768]{1,0:T(8,128)(2,1)}, u32[]{:S(2)}, u32[]{:S(2)}) collective-permute-start(bf16[384,768]{1,0:T(8,128)(2,1)} %bitcast.144.refs_2_), channel_id=1, source_target_pairs={{0,4},{2,6},{4,0},{6,2},{8,12},{10,14},{12,8},{14,10},{16,20},{18,... | collective-permute-start | bytes 1769480 | tf_op jit(solution)/shard_map/ppermute | solution.py:49
  498.5 28.0 %collective-permute-start.56 = (f32[26112]{0:T(1024)S(1)}, f32[26112]{0:T(1024)S(1)}, u32[]{:S(2)}, u32[]{:S(2)}) collective-permute-start(f32[26112]{0:T(1024)S(1)} %pad_maximum_fusion.12), channel_id=1, source_target_pairs={{0,6},{2,4},{4,2},{6,0},{8,14},{10,12},{12,10},{14,8},{16,22},{18,... | collective-permute-start | bytes 313352 | tf_op jit(solution)/shard_map/ppermute | solution.py:118
  502.4 28.9 %collective-permute-start.46 = (f32[48,3840]{1,0:T(8,128)}, f32[48,3840]{1,0:T(8,128)}, u32[]{:S(2)}, u32[]{:S(2)}) collective-permute-start(f32[48,3840]{1,0:T(8,128)} %get-tuple-element.150.refs_4_), channel_id=1, source_target_pairs={{0,6},{2,4},{4,2},{6,0},{8,14},{10,12},{12,10},{14,8},{16,22},{18,... | collective-permute-start | bytes 2211848 | tf_op jit(solution)/shard_map/ppermute | solution.py:49
  503.8 33.6 %collective-permute-start.45 = (f32[48,3840]{1,0:T(8,128)S(1)}, f32[48,3840]{1,0:T(8,128)}, u32[]{:S(2)}, u32[]{:S(2)}) collective-permute-start(f32[48,3840]{1,0:T(8,128)S(1)} %get-tuple-element.152.refs_3_), channel_id=1, source_target_pairs={{0,4},{2,6},{4,0},{6,2},{8,12},{10,14},{12,8},{14,10},{16,20},{18,... | collective-permute-start | bytes 2211848 | tf_op jit(solution)/shard_map/ppermute | solution.py:49
  504.8 57.0 %all-to-all-start.6 = ((bf16[4,288,768]{2,1,0:T(8,128)(2,1)}), bf16[4,288,768]{2,1,0:T(8,128)(2,1)}, u32[]{:S(2)}, u32[]{:S(2)}) async-start(bf16[4,288,768]{2,1,0:T(8,128)(2,1)} %fusion.15.refs_0_.refs_1_), calls=%async_computation.6 | async-start | bytes 3538944 | tf_op jit(solution)/shard_map/all_to_all | solution.py:133
  531.3 28.0 %collective-permute-start.58 = (f32[26112]{0:T(1024)S(1)}, f32[26112]{0:T(1024)S(1)}, u32[]{:S(2)}, u32[]{:S(2)}) collective-permute-start(f32[26112]{0:T(1024)S(1)} %add_add_fusion.8), channel_id=1, source_target_pairs={{0,16},{2,18},{4,20},{6,22},{8,24},{10,26},{12,28},{14,30},{16,0},... | collective-permute-start | bytes 313352 | tf_op jit(solution)/shard_map/ppermute | solution.py:49
  531.3 28.0 %collective-permute-start.57 = (f32[26112]{0:T(1024)S(1)}, f32[26112]{0:T(1024)S(1)}, u32[]{:S(2)}, u32[]{:S(2)}) collective-permute-start(f32[26112]{0:T(1024)S(1)} %add_add_fusion.8), channel_id=1, source_target_pairs={{0,8},{2,10},{4,12},{6,14},{8,0},{10,2},{12,4},{14,6},{16,24},{18,... | collective-permute-start | bytes 313352 | tf_op jit(solution)/shard_map/ppermute | solution.py:49
  (193 other events, 1823.6 us)
Sparse Core Ops, SparseCore 0:
  132.5 110.3 all-gather.1
